TPU v7x, 32 devices: a whole 2x2x4 slice. The times are simulated.
32 devices in a mesh: section: 2 (over y), pb: 8 (over z, core), fsdp: 2 (over x).
Axes of the slice: x: 2, y: 2, z: 4, core: 2. Of those that a mesh axis runs over, the one named last changes fastest.
Arguments:
- decoder_states: bfloat16 [8, 32, 4096], P('pb', None, 'fsdp'), may hold values from -90 to 90
- norm_gain: bfloat16 [4096], P('fsdp'), may hold values from 0.099609375 to 1.8984375
- query_weight: bfloat16 [4096, 2048], P('fsdp', 'section'), may hold values from -0.046875 to 0.046875
- key_weight: bfloat16 [4096, 2048], P(('pb', 'fsdp'), 'section'), may hold values from -0.09375 to 0.09375
- value_weight: bfloat16 [4096, 2048], P(('pb', 'fsdp'), 'section'), may hold values from -0.09375 to 0.09375
- out_weight: bfloat16 [2048, 4096], P('section', 'fsdp'), may hold values from -0.5 to 0.5
- passage_states: bfloat16 [8, 2048, 4096], P('fsdp', 'pb'), may hold values from -400 to 400
- block_mask: int32 [8, 16], replicated, may hold values from 0 to 1, as said below
Outputs:
- cross_out: bfloat16 [8, 32, 4096], P('pb', None, 'fsdp')
Inputs may be any that keep to these rules, and one draw needn't show every extreme that they name: `block_mask`: every question has at least one live block.
All inputs are finite; a program needn't handle non-finite values.
Results may differ from a plain program's by a relative error of at most 0.01.
The roundings to bfloat16 on the way count: a program that leaves them out, or rounds other values in their place, can miss the bound.
Values may be sent and summed in bfloat16 or wider, within the bound.
No kernel may reach another device: no remote copies, remote signals or barrier semaphores. Data moves between devices by JAX's collectives and lax.ppermute only.
A program may use at most 128 MiB of HBM per device.

v0:
```python
import jax
import jax.numpy as jnp
from jax import lax
from jax.sharding import PartitionSpec as P

HD = 64
BLOCK = 128
PASSAGE = 256


NEGATIVE = -1e30


def joined(value, axis, combine):
    everything = jax.tree.map(lambda part: lax.all_gather(part, axis), value)
    leading = jax.tree.map(lambda part: part[0], everything)

    def turn(k, so_far):
        return combine(so_far, jax.tree.map(lambda part: part[k], everything))

    return lax.fori_loop(1, lax.axis_size(axis), turn, leading)


def pack_order(alive_flags):
    amount = alive_flags.shape[0]
    ahead_count = jnp.cumsum(alive_flags) - alive_flags
    behind = jnp.cumsum(1 - alive_flags) - (1 - alive_flags)
    filled = jnp.sum(alive_flags)
    slot_index = jnp.where(alive_flags > 0, ahead_count, filled + behind)
    places = jnp.arange(amount, dtype=jnp.int32)
    order_index = jnp.sum(
        jnp.where(slot_index[None, :] == places[:, None], places[None, :], 0), axis=1
    )
    return (slot_index, order_index, filled)


def project(pieces, alive_flags, stacked):
    amount, piece_rows, model_width = pieces.shape
    slot_index, order_index, filled = pack_order(alive_flags)
    packed = pieces[order_index]
    per_group = min(amount, max(1, 256 // piece_rows))
    columns = stacked.shape[1]

    def compute(row_block):
        return jnp.dot(row_block, stacked, preferred_element_type=jnp.float32).astype(jnp.bfloat16)

    def skipped(row_block):
        return jnp.zeros((row_block.shape[0], columns), jnp.bfloat16)

    def advance(group_index, buffer):
        first_piece = group_index * per_group
        row_block = lax.dynamic_slice_in_dim(packed, first_piece, per_group, 0).reshape(
            per_group * piece_rows, model_width
        )
        result = lax.cond(first_piece < filled, compute, skipped, row_block)
        return lax.dynamic_update_slice_in_dim(
            buffer, result.reshape(per_group, piece_rows, columns), first_piece, 0
        )

    empty_buffer = jnp.zeros((amount, piece_rows, columns), jnp.bfloat16)
    buffer = lax.fori_loop(0, amount // per_group, advance, empty_buffer)
    return (buffer, slot_index, filled)


def attend(query, keyval, live_rows):
    row_total, doubled = keyval.shape
    half_width = doubled // 2
    head_count = half_width // HD
    answer_len = query.shape[0]
    keys_part = keyval[:, :half_width].reshape(row_total, head_count, HD)
    values_part = keyval[:, half_width:].reshape(row_total, head_count, HD)
    queries = query.reshape(answer_len, head_count, HD)
    scores = jnp.einsum("ahd,rhd->ahr", queries, keys_part, preferred_element_type=jnp.float32)
    shown = live_rows[None, None, :]
    scores = jnp.where(shown, scores, NEGATIVE)
    peak = jnp.max(scores, axis=2)
    raw_weights = jnp.where(shown, jnp.exp(scores - peak[:, :, None]), 0.0)
    totals = jnp.sum(raw_weights, axis=2)
    numerator = jnp.einsum(
        "ahr,rhd->ahd",
        raw_weights.astype(jnp.bfloat16),
        values_part,
        preferred_element_type=jnp.float32,
    )
    return (peak, totals, numerator)


def combine_parts(first, second):
    peak_one, totals_one, numer_one = first
    peak_two, totals_two, numer_two = second
    peak = jnp.maximum(peak_one, peak_two)
    factor_one = jnp.exp(peak_one - peak)
    factor_two = jnp.exp(peak_two - peak)
    totals = totals_one * factor_one + totals_two * factor_two
    numerator = numer_one * factor_one[:, :, None] + numer_two * factor_two[:, :, None]
    return (peak, totals, numerator)


def shards(
    decoder_states,
    norm_gain,
    query_weight,
    key_weight,
    value_weight,
    out_weight,
    passage_states,
    block_mask,
):
    pb_count = lax.axis_size("pb")
    fsdp_count = lax.axis_size("fsdp")
    pb_index = lax.axis_index("pb")
    fsdp_index = lax.axis_index("fsdp")
    local_questions, local_rows, model_width = passage_states.shape
    block_total = block_mask.shape[1]
    passages_here = local_rows // PASSAGE
    piece_rows = PASSAGE // fsdp_count
    block_ids = jnp.arange(block_total, dtype=jnp.int32)
    own_mask = lax.dynamic_slice_in_dim(block_mask, pb_index, 1, 0)[0]
    passage_ids = jnp.arange(pb_count * passages_here, dtype=jnp.int32)
    piece_block = (passage_ids * PASSAGE + fsdp_index * piece_rows) // BLOCK
    decoder_live = jnp.sum(
        jnp.where(piece_block[:, None] == block_ids[None, :], own_mask[None, :], 0), axis=1
    )
    stacked_local = jnp.concatenate([key_weight, value_weight], axis=1)
    stacked = lax.all_gather(stacked_local, ("pb", "fsdp"), axis=0, tiled=True)
    own_states = decoder_states[0]
    states_wide = own_states.astype(jnp.float32)
    square_part = jnp.sum(states_wide * states_wide, axis=1)
    scaled = (states_wide * norm_gain.astype(jnp.float32)[None, :]).astype(jnp.bfloat16)
    query_part = jnp.dot(scaled, query_weight, preferred_element_type=jnp.float32)
    square_sum, query_raw = lax.psum((square_part, query_part), "fsdp")
    query = (query_raw * lax.rsqrt(square_sum / model_width + 1e-06)[:, None]).astype(jnp.bfloat16)
    shaped = passage_states.reshape(
        local_questions, passages_here, fsdp_count, piece_rows, model_width
    )
    by_piece = lax.all_to_all(shaped, "fsdp", split_axis=2, concat_axis=0, tiled=True)
    by_question = lax.all_to_all(by_piece, "pb", split_axis=0, concat_axis=1, tiled=True)
    pieces = by_question.reshape(pb_count * passages_here, piece_rows, model_width)
    projected, slot_index, filled = project(pieces, decoder_live, stacked)
    keyval = projected.reshape(pb_count * passages_here * piece_rows, projected.shape[2])
    live_rows = jnp.repeat(passage_ids < filled, piece_rows)
    peak, totals, numerator = attend(query, keyval, live_rows)
    peak, totals, numerator = joined((peak, totals, numerator), "fsdp", combine_parts)
    attention = (
        (numerator / totals[:, :, None])
        .astype(jnp.bfloat16)
        .reshape(query.shape[0], query.shape[1])
    )
    partial_out = jnp.dot(attention, out_weight, preferred_element_type=jnp.float32)
    summed_out = lax.psum(partial_out.astype(jnp.bfloat16), "section")
    return summed_out[None]


def solution(mesh):
    placed = (
        P("pb", None, "fsdp"),
        P("fsdp"),
        P("fsdp", "section"),
        P(("pb", "fsdp"), "section"),
        P(("pb", "fsdp"), "section"),
        P("section", "fsdp"),
        P("fsdp", "pb", None),
        P(),
    )
    return jax.shard_map(
        shards, mesh=mesh, in_specs=placed, out_specs=P("pb", None, "fsdp"), check_vma=False
    )
```

profile of v0, /device:TPU:10, one launch (start us, length us, event | category | flops | bytes accessed | tf_op | source)
XLA Modules:
  0.0 482.5 jit_solution(15917999689604832337)
XLA Ops:
  7.4 0.7 convert_element_type.38
  8.1 3.8 fusion.16
  12.0 1.1 pad_maximum_fusion
  13.1 7.7 %copy.27 = bf16[4,1,2,128,4096]{4,3,0,1,2:T(8,128)(2,1)} copy(bf16[4,1,2,128,4096]{4,3,2,0,1:T(8,128)(2,1)} %bitcast.99) | data formatting | bytes 16777216 | tf_op jit(solution)/shard_map/reshape | solution.py:133
  20.8 152.7 %all_to_all.27 = bf16[4,1,2,128,4096]{4,3,0,1,2:T(8,128)(2,1)} all-to-all(bf16[4,1,2,128,4096]{4,3,0,1,2:T(8,128)(2,1)} %copy.27), channel_id=1, replica_groups=mesh['section'=2,'pb'=8,'fsdp'=2] {'fsdp'}, dimensions={2} | all-to-all | bytes 16777216 | tf_op jit(solution)/shard_map/all_to_all | solution.py:136
  173.5 5.4 %all-to-all-start.1 = ((bf16[8,1,1,128,4096]{4,3,2,1,0:T(8,128)(2,1)}), bf16[8,1,1,128,4096]{4,3,2,1,0:T(8,128)(2,1)}, u32[]{:S(2)}, u32[]{:S(2)}) async-start(bf16[8,1,1,128,4096]{4,3,2,1,0:T(8,128)(2,1)} %bitcast.96), calls=%async_computation.1 | async-start | bytes 16777216 | tf_op jit(solution)/shard_map/all_to_all | solution.py:137
  178.9 0.7 select_reduce_fusion
  179.6 0.2 reduce-window.17
  179.8 0.2 reduce-window.16
  180.0 0.1 fusion.12
  180.2 4.9 %psum.22 = f32[32]{0:T(128)S(1)} all-reduce(f32[32]{0:T(128)S(1)} %fusion.12), channel_id=1, replica_groups=mesh['section'=2,'pb'=8,'fsdp'=2] {'fsdp'}, use_global_device_ids=true, to_apply=%region_11.12 | all-reduce | flops 32 | bytes 256 | tf_op jit(solution)/shard_map/psum | solution.py:131
  185.1 0.6 iota_compare_fusion.2
  185.7 0.6 compare_select_fusion.1
  186.3 0.1 select_reduce_fusion.2
  186.4 0.1 broadcast_bitcast_fusion
  186.5 1.0 multiply_convert_fusion
  187.5 0.1 reshape.205
  187.6 173.5 %all-to-all-done.1 = bf16[8,1,1,128,4096]{4,3,2,1,0:T(8,128)(2,1)} async-done(((bf16[8,1,1,128,4096]{4,3,2,1,0:T(8,128)(2,1)}), bf16[8,1,1,128,4096]{4,3,2,1,0:T(8,128)(2,1)}, u32[]{:S(2)}, u32[]{:S(2)}) %all-to-all-start.1) | async-done | bytes 8388640 | tf_op jit(solution)/shard_map/all_to_all | solution.py:137
  361.1 8.1 %gather_fusion = bf16[8,128,4096]{2,1,0:T(8,128)(2,1)} fusion(bf16[8,128,4096]{2,1,0:T(8,128)(2,1)} %bitcast.8, s32[1024]{0:T(1024)S(1)} %pad_clamp_fusion), kind=kCustom, calls=%fused_computation | custom fusion | bytes 16777248 | tf_op jit(solution)/shard_map/gather | solution.py:40
  369.2 2.5 broadcast_in_dim.71
  371.7 17.2 %while.8 = (s32[]{:T(128)}, bf16[8,128,2048]{2,1,0:T(8,128)(2,1)}, s32[]{:T(128)}, bf16[8,128,4096]{2,1,0:T(8,128)(2,1)}, bf16[4096,2048]{1,0:T(8,128)(2,1)}, /*index=5*/s32[]{:T(128)}, s32[]{:T(128)}, s32[]{:T(128)}, s32[]{:T(128)}) while((s32[]{:T(128)}, bf16[8,128,2048]{2,1,0:T(8,128)(2,1)}, s32[]{:T(128)}, ...), condition=%wide.region_8.9_spmd, body=%wide.region_5.8_spmd.sunk | while | flops 4295491584 | bytes 26215100 | solution.py:61
  372.3 10.1 %conditional.2 = (bf16[2,128,2048]{2,1,0:T(8,128)(2,1)S(1)}) conditional(s32[]{:T(128)} %convert_element_type.57, () %tuple.47, (bf16[8,128,4096]{2,1,0:T(8,128)(2,1)}, s32[]{:T(128)}, bf16[4096,2048]{1,0:T(8,128)(2,1)}) %tuple.48), branch_computations={%region_6.6_spmd, %region_7.7_spmd} | conditional | flops 4295491584 | bytes 24117260 | solution.py:55
  372.3 1.8 constant_dynamic-slice_fusion
  374.1 8.3 %convolution_convert_fusion = bf16[256,2048]{1,0:T(8,128)(2,1)S(1)} fusion(bf16[256,4096]{1,0:T(8,128)(2,1)S(1)} %bitcast.95, bf16[4096,2048]{1,0:T(8,128)(2,1)} %get-tuple-element.141), kind=kOutput, calls=%fused_computation.1 | convolution fusion | flops 4295491584 | bytes 19922944 | tf_op jit(solution)/shard_map/while/body/eval_jaxpr/cond/branch_1_fun/dot_general | solution.py:45
  382.4 1.1 constant_dynamic-update-slice_fusion.2
  384.1 0.1 conditional.2
  384.1 0.1 reshape.185
  384.3 1.0 constant_dynamic-update-slice_fusion.2
  385.9 0.1 conditional.2
  385.9 0.1 reshape.185
  386.0 1.0 constant_dynamic-update-slice_fusion.2
  387.7 0.1 conditional.2
  387.7 0.1 reshape.185
  387.8 1.0 constant_dynamic-update-slice_fusion.2
  388.8 4.0 fusion.33
  392.9 2.6 copy.34
  395.5 2.1 bitcast_reduce_fusion
  397.6 0.6 fusion.3
  398.2 14.0 %all-gather.4 = f32[2,32,16]{1,2,0:T(8,128)S(1)} all-gather(f32[1,32,16]{1,2,0:T(8,128)S(1)} %bitcast.102), channel_id=4, replica_groups=mesh['section'=2,'pb'=8,'fsdp'=2] {'fsdp'}, dimensions={0}, use_global_device_ids=true | all-gather | bytes 6144 | tf_op jit(solution)/shard_map/all_gather | solution.py:15
  412.2 4.4 all-gather.3
  416.5 4.0 copy.33
  420.5 2.4 convolution_bitcast_fusion
  422.8 7.1 %all-gather = f32[64,16,64]{2,0,1:T(8,128)S(1)} all-gather(f32[32,16,64]{2,0,1:T(8,128)S(1)} %convolution_bitcast_fusion), channel_id=2, replica_groups=mesh['section'=2,'pb'=8,'fsdp'=2] {'fsdp'}, dimensions={0}, use_global_device_ids=true | all-gather | bytes 393216 | tf_op jit(solution)/shard_map/all_gather | solution.py:15
  429.9 0.3 fusion.15
  430.3 0.1 reshape.238
  430.4 3.7 fusion
  434.1 39.4 %all-reduce.5.cloned.1.call-done = bf16[1,32,2048]{2,1,0:T(8,128)(2,1)} async-done(((bf16[1,32,2048]{2,1,0:T(8,128)(2,1)}), bf16[1,32,2048]{2,1,0:T(8,128)(2,1)}) %all-reduce.5.cloned.1.call-update) | async-done | bytes 131088 | tf_op jit(solution)/shard_map/psum | solution.py:150
  473.5 1.6 copy.50
  (26 shorter events, 0.2 us)
Async XLA Ops:
  7.4 171.5 %copy-start = (s32[8,16]{1,0:T(8,128)S(1)}, s32[8,16]{1,0:T(8,128)}, u32[]{:S(2)}) copy-start(s32[8,16]{1,0:T(8,128)} %param.19) | copy-start | bytes 1540
  7.4 179.1 %all-reduce.3.cloned.1.call-start = ((), (), s32[]{:S(2)}) async-start(), calls=%async_computation.3 | async-start | bytes 262144 | tf_op jit(solution)/shard_map/psum | solution.py:131
  8.1 3.9 copy-start.3
  8.1 3.9 copy-start.4
  11.9 357.3 %all-gather.7.cloned.1.call-start = ((), (), s32[]{:S(2)}) async-start(), calls=%async_computation.2 | async-start | bytes 17825792 | tf_op jit(solution)/shard_map/all_gather | solution.py:125
  173.5 6.5 %copy-start.2 = (bf16[1,32,2048]{2,1,0:T(8,128)(2,1)S(1)}, bf16[1,32,2048]{2,1,0:T(8,128)(2,1)}, u32[]{:S(2)}) copy-start(bf16[1,32,2048]{2,1,0:T(8,128)(2,1)} %param.12) | copy-start | bytes 393220
  173.5 187.6 %all-to-all-start.1 = ((bf16[8,1,1,128,4096]{4,3,2,1,0:T(8,128)(2,1)}), bf16[8,1,1,128,4096]{4,3,2,1,0:T(8,128)(2,1)}, u32[]{:S(2)}, u32[]{:S(2)}) async-start(bf16[8,1,1,128,4096]{4,3,2,1,0:T(8,128)(2,1)} %bitcast.96), calls=%async_computation.1 | async-start | bytes 16777216 | tf_op jit(solution)/shard_map/all_to_all | solution.py:137
  178.9 294.6 %all-reduce.5.cloned.1.call-start = ((), (), s32[]{:S(2)}) async-start(), calls=%async_computation.4 | async-start | bytes 262144 | tf_op jit(solution)/shard_map/psum | solution.py:150
  430.3 44.8 %copy-start.1 = (s32[8,16]{1,0:T(8,128)S(1)}, s32[8,16]{1,0:T(8,128)}, u32[]{:S(2)}) copy-start(s32[8,16]{1,0:T(8,128)} %param.19) | copy-start | bytes 1540
Sparse Core Ops, SparseCore 0:
  12.0 32.0 all-reduce.2
  434.2 39.2 all-reduce.4
Sparse Core Ops, SparseCore 1:
  14.7 191.9 all-gather.6
where the time goes:
time: 484 us; the launch traced here: 483 us
  waiting for transfers between devices  213 us (44%)
  blocking collectives  183 us (38%)
  local copies, waits for them, and re-layouts  37.2 us (8%)
  matrix products  20.3 us (4%)
  between operations  14.9 us (3%)
  other arithmetic  6.15 us (1%)
  starting transfers between devices  5.42 us (1%)
    all_to_all x1, waiting for transfers between devices, shards(): lax.all_to_all(by_piece, 'pb', split_axis=0, concat_axis=1, tiled=True)  174 us
    all_to_all x1, blocking collectives, shards(): lax.all_to_all(shaped, 'fsdp', split_axis=2, concat_axis=0, tiled=True)  153 us
    psum x1, waiting for transfers between devices, shards(): summed_out = lax.psum(partial_out.astype(jnp.bfloat16), 'section')  39.4 us
    all_gather x3, blocking collectives, joined(): everything = jax.tree.map(lambda part: lax.all_gather(part, axis), value)  25.4 us
  transfers between devices with their start and end apart: 4, of which 2 were waited for; matrix products, arithmetic and copies ran while one was open for 4% of the time, Pallas kernels for 0%

commit v1 on v0

--- a/solution.py
+++ b/solution.py
@@ -1,6 +1,10 @@
+import functools
+
 import jax
 import jax.numpy as jnp
 from jax import lax
+from jax.experimental import pallas as pl
+from jax.experimental.pallas import tpu as pltpu
 from jax.sharding import PartitionSpec as P
 
 HD = 64
@@ -96,7 +100,7 @@
     return (peak, totals, numerator)
 
 
-def shards(
+def plain_shards(
     decoder_states,
     norm_gain,
     query_weight,
@@ -151,6 +155,408 @@
     return summed_out[None]
 
 
+CHIPS = 4
+PIECE = 256
+
+
+def line(step, sources):
+    return [(2 * z + c, 2 * (z + step) + c) for z in sources for c in range(2)]
+
+
+def after(values, done):
+    return lax.optimization_barrier((tuple(values), tuple(done)))[0]
+
+
+def by_chip(z, options):
+    picked = options[0]
+    for place in range(1, CHIPS):
+        if options[place] is not picked:
+            picked = jnp.where(z >= place, options[place], picked)
+    return picked
+
+
+def core_swap(value):
+    return lax.ppermute(value, "pb", [(p, p ^ 1) for p in range(2 * CHIPS)])
+
+
+def gather_pieces(own, partner, z):
+    def left(value, sources):
+        return lax.ppermute(value, "pb", line(-1, sources))
+
+    def right(value, sources):
+        return lax.ppermute(value, "pb", line(1, sources))
+
+    def across(value):
+        return lax.ppermute(value, "fsdp", [(0, 1), (1, 0)])
+
+    l_a1, r_a1, x_b = left(own, (1, 2, 3)), right(own, (0, 1, 2)), across(partner)
+    l_b1, r_b1, x_a = left(partner, (1, 2, 3)), right(partner, (0, 1, 2)), across(own)
+
+    l_a1, r_a1 = after((l_a1, r_a1), (x_b,))
+    a1 = jnp.where(z < 2, l_a1, r_a1)
+    l_a2, r_a2, x_a1 = left(l_a1, (1, 2)), right(r_a1, (1, 2)), across(a1)
+
+    l_b1, r_b1, x_b = after((l_b1, r_b1, x_b), (x_a,))
+    b1 = jnp.where(z < 2, l_b1, r_b1)
+    l_b2 = left(jnp.where(z == 3, x_b, l_b1), (1, 2, 3))
+    r_b2 = right(jnp.where(z == 0, x_b, r_b1), (0, 1, 2))
+    x_b1 = across(b1)
+
+    l_a2, r_a2 = after((l_a2, r_a2), (x_a1,))
+    a2 = by_chip(z, (l_a2, r_a1, l_a1, r_a2))
+    l_a3, r_a3, x_a2 = left(l_a2, (1,)), right(r_a2, (2,)), across(a2)
+
+    l_b2, r_b2 = after((l_b2, r_b2), (x_b1,))
+    l_b3, r_b3 = left(l_b2, (1, 2)), right(r_b2, (1, 2))
+    ends = [(4 * k + 2 * c + x, 4 * k + 2 * c + 1 - x) for k in (0, 3) for c in range(2) for x in range(2)]
+    x_b2 = lax.ppermute(jnp.where(z == 0, l_b2, r_b2), ("pb", "fsdp"), ends)
+
+    l_a3, r_a3 = after((l_a3, r_a3), (x_a2,))
+    a3 = by_chip(z, (l_a3, l_a2, r_a2, r_a3))
+    x_a3 = across(a3)
+
+    l_b3, r_b3 = after((l_b3, r_b3), (x_b2,))
+    l_b4, r_b4 = left(l_b3, (1,)), right(r_b3, (2,))
+
+    here = (0, 1, 2, 3)
+    early = [
+        ((own,) * 4, here, 0, 0),
+        ((partner,) * 4, here, 0, 1),
+        ((x_a,) * 4, here, 1, 0),
+        ((x_b,) * 4, here, 1, 1),
+        ((a1,) * 4, (1, 2, 1, 2), 0, 0),
+        ((b1,) * 4, (1, 2, 1, 2), 0, 1),
+        ((x_a1,) * 4, (1, 2, 1, 2), 1, 0),
+        ((x_b1,) * 4, (1, 2, 1, 2), 1, 1),
+        ((a2,) * 4, (2, 0, 3, 1), 0, 0),
+        ((l_b2, r_b1, l_b1, r_b2), (2, 0, 3, 1), 0, 1),
+    ]
+    later = [
+        ((a3,) * 4, (3, 3, 0, 0), 0, 0),
+        ((l_b3, l_b2, r_b2, r_b3), (3, 3, 0, 0), 0, 1),
+        ((x_a2,) * 4, (2, 0, 3, 1), 1, 0),
+        ((x_b2, r_b2, l_b2, x_b2), (2, 0, 3, 1), 1, 1),
+    ]
+    last = [
+        ((x_a3,) * 4, (3, 3, 0, 0), 1, 0),
+        ((l_b4, l_b3, r_b3, r_b4), (3, 3, 0, 0), 1, 1),
+    ]
+    return early, later, last
+
+
+def feature_blocks(pieces, z, c, f):
+    found = []
+    for _, origins, other_x, other_core in pieces:
+        origin = by_chip(z, [jnp.int32(o) for o in origins])
+        core = 1 - c if other_core else c
+        place = 1 - f if other_x else f
+        found.append(4 * origin + 2 * core + place)
+    return jnp.stack(found)
+
+
+def distinct(pieces):
+    arrays, wanted = [], []
+    for options, _, _, _ in pieces:
+        spots = []
+        for option in options:
+            at = next((k for k, seen in enumerate(arrays) if seen is option), None)
+            if at is None:
+                at = len(arrays)
+                arrays.append(option)
+            spots.append(at)
+        wanted.append(spots)
+    return arrays, wanted
+
+
+def load_weights(wanted, z, sources, weights, sems):
+    for slot, spots in enumerate(wanted):
+        target = weights.at[pl.ds(slot * PIECE, PIECE)]
+        for at in sorted(set(spots)):
+            zs = [k for k, spot in enumerate(spots) if spot == at]
+
+            def begin(at=at, slot=slot, target=target):
+                pltpu.make_async_copy(sources[at], target, sems.at[slot]).start()
+
+            if len(zs) == CHIPS:
+                begin()
+            else:
+                hit = functools.reduce(jnp.logical_or, [z == k for k in zs])
+                pl.when(hit)(begin)
+    for slot, spots in enumerate(wanted):
+        target = weights.at[pl.ds(slot * PIECE, PIECE)]
+        pltpu.make_async_copy(sources[spots[0]], target, sems.at[slot]).wait()
+
+
+def project_kernel(wanted, amount, carried, info, own_rows, other_rows, *refs):
+    refs = list(refs)
+    before = refs.pop(0) if carried else None
+    sources, (total, weights, sems) = refs[:amount], refs[amount:]
+    count = len(wanted)
+
+    @pl.when(pl.program_id(0) == 0)
+    def _():
+        load_weights(wanted, info[0], sources, weights, sems)
+
+    for half, rows in enumerate((own_rows, other_rows)):
+        here = pl.ds(half * rows.shape[1], rows.shape[1])
+        features = jnp.concatenate(
+            [rows[0, :, pl.ds(pl.multiple_of(info[1 + k] * PIECE, PIECE), PIECE)] for k in range(count)],
+            axis=1,
+        )
+        part = jnp.dot(features, weights[...], preferred_element_type=jnp.float32)
+        if carried:
+            part = part + before[0, here, :]
+        total[0, here, :] = part
+
+
+def project_pieces(info, pieces, own_rows, other_rows, before=None):
+    questions, rows, width = own_rows.shape
+    columns = pieces[0][0][0].shape[1]
+    arrays, wanted = distinct(pieces)
+    count = len(pieces)
+    carried = before is not None
+    block = pl.BlockSpec((1, rows, width), lambda i, info: (i, 0, 0))
+    sums = pl.BlockSpec((1, 2 * rows, columns), lambda i, info: (i, 0, 0))
+    anywhere = pl.BlockSpec(memory_space=pl.ANY)
+    flops = 2 * questions * 2 * rows * count * PIECE * columns
+    return pl.pallas_call(
+        functools.partial(project_kernel, wanted, len(arrays), carried),
+        grid_spec=pltpu.PrefetchScalarGridSpec(
+            num_scalar_prefetch=1,
+            grid=(questions,),
+            in_specs=[block, block] + ([sums] if carried else []) + [anywhere] * len(arrays),
+            out_specs=sums,
+            scratch_shapes=[
+                pltpu.VMEM((count * PIECE, columns), jnp.bfloat16),
+                pltpu.SemaphoreType.DMA((count,)),
+            ],
+        ),
+        out_shape=jax.ShapeDtypeStruct((questions, 2 * rows, columns), jnp.float32),
+        input_output_aliases={3: 0} if carried else {},
+        compiler_params=pltpu.CompilerParams(vmem_limit_bytes=48 * 2**20),
+        cost_estimate=pl.CostEstimate(
+            flops=flops, bytes_accessed=questions * rows * (4 * width + 8 * columns), transcendentals=0
+        ),
+        name="project",
+    )(info, own_rows, other_rows, *([before] if carried else []), *arrays)
+
+
+def attend_kernel(wanted, amount, info, *refs):
+    refs = list(refs)
+    count = len(wanted)
+    own_blocks, other_blocks, refs = refs[:count], refs[count : 2 * count], refs[2 * count :]
+    before, queries, live, refs = refs[0], refs[1], refs[2], refs[3:]
+    sources, refs = refs[:amount], refs[amount:]
+    outs, (weights, sems) = refs[:CHIPS], refs[CHIPS:]
+    step = pl.program_id(0)
+
+    @pl.when(step == 0)
+    def _():
+        load_weights(wanted, info[0], sources, weights, sems)
+
+    halves = []
+    for half, blocks in enumerate((own_blocks, other_blocks)):
+        rows = blocks[0].shape[1]
+        features = jnp.concatenate([block[0] for block in blocks], axis=1)
+        part = jnp.dot(features, weights[...], preferred_element_type=jnp.float32)
+        halves.append((part + before[0, pl.ds(half * rows, rows), :]).astype(jnp.bfloat16))
+    keyval = jnp.concatenate(halves, axis=0)
+    width = keyval.shape[1] // 2
+    answers = queries.shape[1]
+    group = 4
+    span = group * HD
+    shown = live[0] > 0
+    lane_head = lax.broadcasted_iota(jnp.int32, (answers, span), 1) // HD
+    tail_lane = lax.broadcasted_iota(jnp.int32, (answers, 128), 1)
+    head_total = width // HD
+    extra = jnp.zeros((answers, 128), jnp.float32)
+    parts = []
+    for g in range(width // span):
+        at = slice(g * span, (g + 1) * span)
+        query = queries[0, :, at]
+        spread = jnp.concatenate(
+            [jnp.where(lane_head == h, query, jnp.zeros_like(query)) for h in range(group)], axis=0
+        )
+        scores = lax.dot_general(
+            spread, keyval[:, at], (((1,), (1,)), ((), ())), preferred_element_type=jnp.float32
+        )
+        scores = jnp.where(shown, scores, NEGATIVE)
+        peak = jnp.max(scores, axis=1, keepdims=True)
+        raw = jnp.where(shown, jnp.exp(scores - peak), 0.0)
+        total = jnp.sum(raw, axis=1, keepdims=True)
+        value_at = slice(width + g * span, width + (g + 1) * span)
+        numer = jnp.dot(raw.astype(jnp.bfloat16), keyval[:, value_at], preferred_element_type=jnp.float32)
+        own = jnp.zeros((answers, span), jnp.float32)
+        for h in range(group):
+            mine = slice(h * answers, (h + 1) * answers)
+            own = jnp.where(lane_head == h, numer[mine], own)
+            extra = jnp.where(tail_lane == g * group + h, peak[mine], extra)
+            extra = jnp.where(tail_lane == head_total + g * group + h, total[mine], extra)
+        parts.append(own)
+    result = jnp.concatenate(parts + [extra], axis=1)
+    for k, out in enumerate(outs):
+
+        @pl.when(step == k)
+        def _(out=out):
+            out[...] = result
+
+
+def attend_last(info, pieces, own_rows, other_rows, before, queries, live):
+    questions, rows, width = own_rows.shape
+    columns = pieces[0][0][0].shape[1]
+    answers = queries.shape[1]
+    arrays, wanted = distinct(pieces)
+    count = len(pieces)
+    wide = columns // 2 + 128
+
+    def question(i, info):
+        return lax.rem(i + info[0], questions)
+
+    blocks = [
+        pl.BlockSpec((1, rows, PIECE), lambda i, info, k=k: (question(i, info), 0, info[1 + k]))
+        for k in range(count)
+    ]
+    whole = lambda *shape: pl.BlockSpec((1,) + shape, lambda i, info: (question(i, info), 0, 0))
+    anywhere = pl.BlockSpec(memory_space=pl.ANY)
+    flops = 4 * questions * rows * count * PIECE * columns + 16 * questions * rows * answers * columns
+    return pl.pallas_call(
+        functools.partial(attend_kernel, wanted, len(arrays)),
+        grid_spec=pltpu.PrefetchScalarGridSpec(
+            num_scalar_prefetch=1,
+            grid=(questions,),
+            in_specs=blocks
+            + blocks
+            + [whole(2 * rows, columns), whole(answers, columns // 2), whole(1, 2 * rows)]
+            + [anywhere] * len(arrays),
+            out_specs=[pl.BlockSpec((answers, wide), lambda i, info: (0, 0))] * CHIPS,
+            scratch_shapes=[
+                pltpu.VMEM((count * PIECE, columns), jnp.bfloat16),
+                pltpu.SemaphoreType.DMA((count,)),
+            ],
+        ),
+        out_shape=[jax.ShapeDtypeStruct((answers, wide), jnp.float32)] * CHIPS,
+        compiler_params=pltpu.CompilerParams(vmem_limit_bytes=48 * 2**20),
+        cost_estimate=pl.CostEstimate(
+            flops=flops,
+            bytes_accessed=questions * rows * (8 * columns + 4 * count * PIECE),
+            transcendentals=questions * rows * answers * columns // HD,
+        ),
+        name="attend",
+    )(info, *([own_rows] * count), *([other_rows] * count), before, queries, live, *arrays)
+
+
+def merge_kernel(*refs):
+    parts, out = refs[:-1], refs[-1]
+    answers, width = out.shape
+    heads = width // HD
+    lane = lax.broadcasted_iota(jnp.int32, (answers, 128), 1)
+    tails = [part[:, pl.ds(width, 128)] for part in parts]
+    peak = functools.reduce(jnp.maximum, tails)
+    factors = [jnp.exp(jnp.where(lane < heads, tail - peak, 0.0)) for tail in tails]
+
+    def column(value, at):
+        return value[:, at : at + 1]
+
+    for tile in range(width // 128):
+        low, high = 2 * tile, 2 * tile + 1
+        numer = jnp.zeros((answers, 128), jnp.float32)
+        total = jnp.zeros((answers, 128), jnp.float32)
+        for part, tail, factor in zip(parts, tails, factors):
+            scale = jnp.where(lane < HD, column(factor, low), column(factor, high))
+            amount = jnp.where(lane < HD, column(tail, heads + low), column(tail, heads + high))
+            numer += part[:, pl.ds(tile * 128, 128)] * scale
+            total += amount * scale
+        out[:, pl.ds(tile * 128, 128)] = (numer / total).astype(out.dtype)
+
+
+def merge(parts):
+    answers, wide = parts[0].shape
+    return pl.pallas_call(
+        merge_kernel,
+        out_shape=jax.ShapeDtypeStruct((answers, wide - 128), jnp.bfloat16),
+        cost_estimate=pl.CostEstimate(flops=8 * answers * wide, bytes_accessed=16 * answers * wide, transcendentals=512 * answers),
+        name="merge",
+    )(*parts)
+
+
+def gathered_shards(
+    decoder_states,
+    norm_gain,
+    query_weight,
+    key_weight,
+    value_weight,
+    out_weight,
+    passage_states,
+    block_mask,
+):
+    pb_index = lax.axis_index("pb")
+    f = lax.axis_index("fsdp")
+    z, c = pb_index // 2, pb_index % 2
+    questions, rows, model_width = passage_states.shape
+    width = key_weight.shape[1] // 2
+
+    def core_columns(core):
+        return jnp.concatenate(
+            [lax.dynamic_slice_in_dim(w, core * width, width, 1) for w in (key_weight, value_weight)], axis=1
+        )
+
+    own = core_columns(c)
+    partner = core_swap(core_columns(1 - c))
+    early, later, last = gather_pieces(own, partner, z)
+    other_rows = core_swap(after((passage_states,), (partner,))[0])
+
+    own_states = decoder_states[0]
+    states_wide = own_states.astype(jnp.float32)
+    square_part = jnp.sum(states_wide * states_wide, axis=1, keepdims=True)
+    scaled = (states_wide * norm_gain.astype(jnp.float32)[None, :]).astype(jnp.bfloat16)
+    query_part = jnp.dot(scaled, query_weight, preferred_element_type=jnp.float32)
+    both = jnp.concatenate([query_part, jnp.broadcast_to(square_part, (square_part.shape[0], 128))], axis=1)
+    both = both + lax.ppermute(both, "fsdp", [(0, 1), (1, 0)])
+    query_raw, square_sum = both[:, :-128], both[:, -128:-127]
+    query = (query_raw * lax.rsqrt(square_sum / model_width + 1e-06)).astype(jnp.bfloat16)
+    every_query = lax.all_gather(query, "pb")
+    queries = lax.dynamic_slice(
+        every_query, (f * questions, 0, c * width), (questions, query.shape[0], width)
+    )
+
+    blocks_here = rows // BLOCK
+    mine = lax.dynamic_slice_in_dim(block_mask, f * questions, questions, 0)
+    live = jnp.concatenate(
+        [lax.dynamic_slice_in_dim(mine, p * blocks_here, blocks_here, 1) for p in (pb_index, pb_index ^ 1)],
+        axis=1,
+    )
+    live = jnp.repeat(live, BLOCK, axis=1)[:, None, :]
+
+    def info(pieces):
+        return jnp.concatenate([z[None], feature_blocks(pieces, z, c, f)]).astype(jnp.int32)
+
+    sums = project_pieces(info(early), early, passage_states, other_rows)
+    sums = project_pieces(info(later), later, passage_states, other_rows, sums)
+    parts = attend_last(info(last), last, passage_states, other_rows, sums, queries, live)
+    arrived = [parts[0]]
+    for step in range(1, CHIPS):
+        turn = [(2 * k + core, 2 * ((k + step) % CHIPS) + core) for k in range(CHIPS) for core in range(2)]
+        arrived.append(lax.ppermute(parts[step], "pb", turn))
+    attention = merge(arrived)
+
+    received = []
+    for flip in range(2):
+        sends = [
+            (2 * (2 * k + core) + x, 2 * (questions * x + k) + (core ^ flip))
+            for k in range(CHIPS)
+            for core in range(2)
+            for x in range(2)
+        ]
+        received.append(lax.ppermute(attention, ("pb", "fsdp"), sends))
+    first = jnp.where(f == 0, received[0], received[1])
+    second = jnp.where(f == 0, received[1], received[0])
+    whole = jnp.concatenate([first, second], axis=1)
+    partial_out = jnp.dot(whole, out_weight, preferred_element_type=jnp.float32).astype(jnp.bfloat16)
+    other_out = lax.ppermute(partial_out, "section", [(0, 1), (1, 0)])
+    summed = (partial_out.astype(jnp.float32) + other_out.astype(jnp.float32)).astype(jnp.bfloat16)
+    return summed[None]
+
+
 def solution(mesh):
     placed = (
         P("pb", None, "fsdp"),
@@ -162,6 +568,12 @@
         P("fsdp", "pb", None),
         P(),
     )
+    sizes = dict(mesh.shape)
+    fits = sizes == {"section": 2, "pb": 2 * CHIPS, "fsdp": 2}
     return jax.shard_map(
-        shards, mesh=mesh, in_specs=placed, out_specs=P("pb", None, "fsdp"), check_vma=False
-    )
+        gathered_shards if fits else plain_shards,
+        mesh=mesh,
+        in_specs=placed,
+        out_specs=P("pb", None, "fsdp"),
+        check_vma=False,
+    )

time: 484 us -> 179 us (0.37)
  waiting for transfers between devices: 213 us -> 46.5 us
  blocking collectives: 183 us -> 21.2 us
  starting transfers between devices: 5.42 us -> 55.6 us
  Pallas kernels: 0 us -> 40.7 us
  local copies, waits for them, and re-layouts: 37.2 us -> 4.16 us
  matrix products: 20.3 us -> 4.73 us
  between operations: 14.9 us -> 0.42 us
    all_to_all x1 -> x0, waiting for transfers between devices: 174 us -> none  [shards(): lax.all_to_all(by_piece, 'pb', split_axis=0, concat_axis=1, tiled=True)]
    all_to_all x1 -> x0, blocking collectives: 153 us -> none  [shards(): lax.all_to_all(shaped, 'fsdp', split_axis=2, concat_axis=0, tiled=True)]
    ppermute x0 -> x30, starting transfers between devices: none -> 55.6 us  [the longest x7 21.8 us: right(): return lax.ppermute(value, 'pb', line(1, sources))]
    ppermute x0 -> x30, waiting for transfers between devices: none -> 46.5 us  [the longest x7 16.8 us: left(): return lax.ppermute(value, 'pb', line(-1, sources))]
    pallas_call x0 -> x4, Pallas kernels: none -> 40.7 us  [the longest x2 30 us: project_pieces(): pl.pallas_call(functools.partial(project_kernel, wanted, len(arrays), car...]
    psum x2 -> x0, waiting for transfers between devices: 39.4 us -> none  [the longest x1 39.4 us: shards(): summed_out = lax.psum(partial_out.astype(jnp.bfloat16), 'section')]
    dot_general x5 -> x2, matrix products: 20.3 us -> 4.73 us  [the longest x1 3.01 us: gathered_shards(): jnp.dot(whole, out_weight, preferred_element_type=jnp.float32)]
    reshape x5 -> x0, local copies, waits for them, and re-layouts: 8.18 us -> none  [the longest x1 7.7 us: shards(): passage_states.reshape(local_questions, passages_here, fsdp_count, piece_...]
  transfers between devices with their start and end apart: 4 -> 30, of which waited for: 2 -> 14; matrix products, arithmetic and copies ran while one was open for 4% -> 3% of each run, Pallas kernels for 0% -> 17%
where the time goes in v1:
time: 179 us; the launch traced here: 177 us
  starting transfers between devices  55.6 us (31%)
  waiting for transfers between devices  46.5 us (26%)
  Pallas kernels  40.7 us (23%)
  blocking collectives  21.2 us (12%)
  matrix products  4.73 us (3%)
  local copies, waits for them, and re-layouts  4.16 us (2%)
  other arithmetic  3.89 us (2%)
    pallas_call x2, Pallas kernels, project_pieces(): pl.pallas_call(functools.partial(project_kernel, wanted, len(arrays), car...  30 us
    ppermute x7, starting transfers between devices, right(): return lax.ppermute(value, 'pb', line(1, sources))  21.8 us
    all_gather x1, blocking collectives, gathered_shards(): every_query = lax.all_gather(query, 'pb')  21.2 us
    ppermute x7, waiting for transfers between devices, left(): return lax.ppermute(value, 'pb', line(-1, sources))  16.8 us
    ppermute x7, starting transfers between devices, left(): return lax.ppermute(value, 'pb', line(-1, sources))  14.1 us
    pallas_call x1, Pallas kernels, attend_last(): pl.pallas_call(functools.partial(attend_kernel, wanted, len(arrays)), gri...  8.57 us
    ppermute x6, waiting for transfers between devices, across(): return lax.ppermute(value, 'fsdp', [(0, 1), (1, 0)])  8.1 us
    ppermute x1, waiting for transfers between devices, gathered_shards(): both = both + lax.ppermute(both, 'fsdp', [(0, 1), (1, 0)])  6.13 us
  transfers between devices with their start and end apart: 30, of which 14 were waited for; matrix products, arithmetic and copies ran while one was open for 3% of the time, Pallas kernels for 17%

profile of v1, /device:TPU:10, one launch (start us, length us, event | category | flops | bytes accessed | tf_op | source)
XLA Modules:
  0.0 177.1 jit_solution(16997437441294657442)
XLA Ops:
  0.0 1.4 constant_dynamic-slice_fusion.1
  1.6 1.9 %collective-permute-done.refs_1_ = bf16[256,1024]{1,0:T(8,128)(2,1)S(1)} collective-permute-done((bf16[256,1024]{1,0:T(8,128)(2,1)S(1)}, bf16[256,1024]{1,0:T(8,128)(2,1)S(1)}, u32[]{:S(2)}, u32[]{:S(2)}) %collective-permute-start) | collective-permute-done | bytes 524320 | tf_op jit(solution)/shard_map/ppermute | solution.py:179
  4.3 1.9 %collective-permute-start.6 = (bf16[256,1024]{1,0:T(8,128)(2,1)S(1)}, bf16[256,1024]{1,0:T(8,128)(2,1)S(1)}, u32[]{:S(2)}, u32[]{:S(2)}) collective-permute-start(bf16[256,1024]{1,0:T(8,128)(2,1)S(1)} %pad_maximum_fusion.1.refs_0_), channel_id=1, source_target_pairs={{4,0},{6,2},{8,4},{10,6},{12,8},{14,10},{5,1},{7,3},{9,5},{11,7},{... | collective-permute-start | bytes 1572872 | tf_op jit(solution)/shard_map/ppermute | solution.py:184
  6.2 3.9 %collective-permute-start.7 = (bf16[256,1024]{1,0:T(8,128)(2,1)S(1)}, bf16[256,1024]{1,0:T(8,128)(2,1)}, u32[]{:S(2)}, u32[]{:S(2)}) collective-permute-start(bf16[256,1024]{1,0:T(8,128)(2,1)S(1)} %pad_maximum_fusion.1.refs_0_), channel_id=1, source_target_pairs={{0,4},{2,6},{4,8},{6,10},{8,12},{10,14},{1,5},{3,7},{5,9},{7,11},{... | collective-permute-start | bytes 1572872 | tf_op jit(solution)/shard_map/ppermute | solution.py:187
  10.2 1.6 collective-permute-start.5
  11.7 1.7 fusion.3
  13.8 6.3 %collective-permute-done.6 = bf16[256,1024]{1,0:T(8,128)(2,1)S(1)} collective-permute-done((bf16[256,1024]{1,0:T(8,128)(2,1)S(1)}, bf16[256,1024]{1,0:T(8,128)(2,1)S(1)}, u32[]{:S(2)}, u32[]{:S(2)}) %collective-permute-start.6) | collective-permute-done | bytes 524320 | tf_op jit(solution)/shard_map/ppermute | solution.py:184
  20.1 2.2 %collective-permute-start.3 = (bf16[256,1024]{1,0:T(8,128)(2,1)S(1)}, bf16[256,1024]{1,0:T(8,128)(2,1)}, u32[]{:S(2)}, u32[]{:S(2)}) collective-permute-start(bf16[256,1024]{1,0:T(8,128)(2,1)S(1)} %collective-permute-done.refs_1_), channel_id=1, source_target_pairs={{4,0},{6,2},{8,4},{10,6},{12,8},{14,10},{5,1},{7,3},{9,5},{11,7},{... | collective-permute-start | bytes 1572872 | tf_op jit(solution)/shard_map/ppermute | solution.py:184
  22.3 3.6 %collective-permute-start.4 = (bf16[256,1024]{1,0:T(8,128)(2,1)S(1)}, bf16[256,1024]{1,0:T(8,128)(2,1)S(1)}, u32[]{:S(2)}, u32[]{:S(2)}) collective-permute-start(bf16[256,1024]{1,0:T(8,128)(2,1)S(1)} %collective-permute-done.refs_1_), channel_id=1, source_target_pairs={{0,4},{2,6},{4,8},{6,10},{8,12},{10,14},{1,5},{3,7},{5,9},{7,11},{... | collective-permute-start | bytes 1572872 | tf_op jit(solution)/shard_map/ppermute | solution.py:187
  26.2 3.0 %collective-permute-done.5.refs_3_ = bf16[256,1024]{1,0:T(8,128)(2,1)S(1)} collective-permute-done((bf16[256,1024]{1,0:T(8,128)(2,1)S(1)}, bf16[256,1024]{1,0:T(8,128)(2,1)S(1)}, u32[]{:S(2)}, u32[]{:S(2)}) %collective-permute-start.5) | collective-permute-done | bytes 524320 | tf_op jit(solution)/shard_map/ppermute | solution.py:190
  29.2 2.3 %collective-permute-start.10 = (bf16[256,1024]{1,0:T(8,128)(2,1)S(1)}, bf16[256,1024]{1,0:T(8,128)(2,1)S(1)}, u32[]{:S(2)}, u32[]{:S(2)}) collective-permute-start(bf16[256,1024]{1,0:T(8,128)(2,1)S(1)} %collective-permute-done.6), channel_id=1, source_target_pairs={{4,0},{6,2},{8,4},{10,6},{5,1},{7,3},{9,5},{11,7},{20,16},{22,18},... | collective-permute-start | bytes 1572872 | tf_op jit(solution)/shard_map/ppermute | solution.py:184
  32.1 4.9 %collective-permute-done.3.refs_11_ = bf16[256,1024]{1,0:T(8,128)(2,1)} collective-permute-done((bf16[256,1024]{1,0:T(8,128)(2,1)S(1)}, bf16[256,1024]{1,0:T(8,128)(2,1)}, u32[]{:S(2)}, u32[]{:S(2)}) %collective-permute-start.3) | collective-permute-done | bytes 524320 | tf_op jit(solution)/shard_map/ppermute | solution.py:184
  36.9 1.5 collective-permute-start.20
  38.4 2.3 %collective-permute-start.11 = (bf16[256,1024]{1,0:T(8,128)(2,1)}, bf16[256,1024]{1,0:T(8,128)(2,1)S(1)}, u32[]{:S(2)}, u32[]{:S(2)}) collective-permute-start(bf16[256,1024]{1,0:T(8,128)(2,1)} %collective-permute-done.7), channel_id=1, source_target_pairs={{4,8},{6,10},{8,12},{10,14},{5,9},{7,11},{9,13},{11,15},{20,24},{2... | collective-permute-start | bytes 1572872 | tf_op jit(solution)/shard_map/ppermute | solution.py:187
  40.7 1.2 broadcast_select_fusion.1
  41.9 6.1 %collective-permute-done.20 = f32[32,1152]{1,0:T(8,128)S(1)} collective-permute-done((f32[32,1152]{1,0:T(8,128)S(1)}, f32[32,1152]{1,0:T(8,128)S(1)}, u32[]{:S(2)}, u32[]{:S(2)}) %collective-permute-start.20) | collective-permute-done | bytes 147488 | tf_op jit(solution)/shard_map/ppermute | solution.py:514
  48.6 1.9 %collective-permute-start.12 = (bf16[256,1024]{1,0:T(8,128)(2,1)S(1)}, bf16[256,1024]{1,0:T(8,128)(2,1)S(1)}, u32[]{:S(2)}, u32[]{:S(2)}) collective-permute-start(bf16[256,1024]{1,0:T(8,128)(2,1)S(1)} %get-tuple-element.43), channel_id=1, source_target_pairs={{4,0},{6,2},{8,4},{10,6},{12,8},{14,10},{5,1},{7,3},{9,5},{11,7},{... | collective-permute-start | bytes 1572872 | tf_op jit(solution)/shard_map/ppermute | solution.py:184
  50.5 4.6 %collective-permute-start.13 = (bf16[256,1024]{1,0:T(8,128)(2,1)S(1)}, bf16[256,1024]{1,0:T(8,128)(2,1)S(1)}, u32[]{:S(2)}, u32[]{:S(2)}) collective-permute-start(bf16[256,1024]{1,0:T(8,128)(2,1)S(1)} %get-tuple-element.41), channel_id=1, source_target_pairs={{0,4},{2,6},{4,8},{6,10},{8,12},{10,14},{1,5},{3,7},{5,9},{7,11},{... | collective-permute-start | bytes 1572872 | tf_op jit(solution)/shard_map/ppermute | solution.py:187
  55.2 5.1 %collective-permute-done.9.refs_7_ = bf16[256,1024]{1,0:T(8,128)(2,1)S(1)} collective-permute-done((bf16[256,1024]{1,0:T(8,128)(2,1)S(1)}, bf16[256,1024]{1,0:T(8,128)(2,1)S(1)}, u32[]{:S(2)}, u32[]{:S(2)}) %collective-permute-start.9) | collective-permute-done | bytes 524320 | tf_op jit(solution)/shard_map/ppermute | solution.py:190
  60.4 3.0 %collective-permute-done.12.refs_9_.refs_3_ = bf16[256,1024]{1,0:T(8,128)(2,1)S(1)} collective-permute-done((bf16[256,1024]{1,0:T(8,128)(2,1)S(1)}, bf16[256,1024]{1,0:T(8,128)(2,1)S(1)}, u32[]{:S(2)}, u32[]{:S(2)}) %collective-permute-start.12) | collective-permute-done | bytes 524320 | tf_op jit(solution)/shard_map/ppermute | solution.py:184
  63.4 1.3 collective-permute-done.13.refs_12_.refs_4_
  64.7 1.5 collective-permute-start.14
  66.2 0.7 collective-permute-start.15
  66.9 1.9 %collective-permute-start.17 = (bf16[256,1024]{1,0:T(8,128)(2,1)S(1)}, bf16[256,1024]{1,0:T(8,128)(2,1)S(1)}, u32[]{:S(2)}, u32[]{:S(2)}) collective-permute-start(bf16[256,1024]{1,0:T(8,128)(2,1)S(1)} %collective-permute-done.12.refs_9_.refs_3_), channel_id=1, source_target_pairs={{4,0},{6,2},{8,4},{10,6},{5,1},{7,3},{9,5},{11,7},{20,16},{22,18},... | collective-permute-start | bytes 1572872 | tf_op jit(solution)/shard_map/ppermute | solution.py:184
  68.8 5.9 %collective-permute-start.18 = (bf16[256,1024]{1,0:T(8,128)(2,1)S(1)}, bf16[256,1024]{1,0:T(8,128)(2,1)S(1)}, u32[]{:S(2)}, u32[]{:S(2)}) collective-permute-start(bf16[256,1024]{1,0:T(8,128)(2,1)S(1)} %collective-permute-done.13.refs_12_.refs_4_), channel_id=1, source_target_pairs={{4,8},{6,10},{8,12},{10,14},{5,9},{7,11},{9,13},{11,15},{20,24},{2... | collective-permute-start | bytes 1572872 | tf_op jit(solution)/shard_map/ppermute | solution.py:187
  74.8 1.1 select_select_fusion.1.refs_8_
  76.0 2.5 %collective-permute-done.14 = bf16[256,1024]{1,0:T(8,128)(2,1)S(1)} collective-permute-done((bf16[256,1024]{1,0:T(8,128)(2,1)S(1)}, bf16[256,1024]{1,0:T(8,128)(2,1)S(1)}, u32[]{:S(2)}, u32[]{:S(2)}) %collective-permute-start.14) | collective-permute-done | bytes 524320 | tf_op jit(solution)/shard_map/ppermute | solution.py:184
  78.5 1.2 collective-permute-start.16
  80.5 21.2 %all-gather = bf16[256,1024]{1,0:T(8,128)(2,1)S(1)} all-gather(bf16[32,1024]{1,0:T(8,128)(2,1)S(1)} %fusion.5), channel_id=2, replica_groups=mesh['section'=2,'pb'=8,'fsdp'=2] {'pb'}, dimensions={0}, use_global_device_ids=true | all-gather | bytes 589824 | tf_op jit(solution)/shard_map/all_gather | solution.py:517
  102.5 2.4 %collective-permute-start.22 = (bf16[256,1024]{1,0:T(8,128)(2,1)S(1)}, bf16[256,1024]{1,0:T(8,128)(2,1)S(1)}, u32[]{:S(2)}, u32[]{:S(2)}) collective-permute-start(bf16[256,1024]{1,0:T(8,128)(2,1)S(1)} %collective-permute-done.17.refs_2_.refs_9_), channel_id=1, source_target_pairs={{4,0},{6,2},{5,1},{7,3},{20,16},{22,18},{21,17},{23,19}} | collective-permute-start | bytes 1572872 | tf_op jit(solution)/shard_map/ppermute | solution.py:184
  104.9 0.7 collective-permute-start.23
  105.6 16.3 %project.2.refs_0_ = f32[4,512,1024]{2,1,0:T(8,128)} custom-call(s32[11]{0:T(128)S(1)} %concatenate.27.info, bf16[4,256,4096]{2,1,0:T(8,128)(2,1)} %refs_1_.1, bf16[4,256,4096]{2,1,0:T(8,128)(2,1)} %collective-permute-done.1.other_rows.refs_2_.refs_3_, bf16[256,1024]{1,0:T(8,128)(2,1)S(1)} %pad_maximum_fusion.1.refs_0_, ...), custom_call_target="tpu_custom_call" | custom-call | flops 10737418240 | bytes 25165824 | tf_op jit(solution)/shard_map/project/pallas_call | solution.py:322
  121.9 1.0 copy-done.1
  122.9 13.8 %project.3.refs_4_ = f32[4,512,1024]{2,1,0:T(8,128)} custom-call(s32[5]{0:T(128)S(1)} %concatenate.26.info, bf16[4,256,4096]{2,1,0:T(8,128)(2,1)} %refs_1_.1, bf16[4,256,4096]{2,1,0:T(8,128)(2,1)} %collective-permute-done.1.other_rows.refs_2_.refs_3_, f32[4,512,1024]{2,1,0:T(8,128)} %project.2.refs_0_, ...), custom_call_target="tpu_custom_call", output_to_operand_aliasing={{}: (3, {})} | custom-call | flops 4294967296 | bytes 25165824 | tf_op jit(solution)/shard_map/project/pallas_call | solution.py:322
  136.8 8.6 %attend.1 = (f32[32,640]{1,0:T(8,128)S(1)}, f32[32,640]{1,0:T(8,128)S(1)}, f32[32,640]{1,0:T(8,128)S(1)}, f32[32,640]{1,0:T(8,128)S(1)}) custom-call(s32[3]{0:T(128)S(1)} %pad_add_fusion.1.info, bf16[4,256,4096]{2,1,0:T(8,128)(2,1)} %refs_1_.1, bf16[4,256,4096]{2,1,0:T(8,128)(2,1)} %refs_1_.1, ...), custom_call_target="tpu_custom_call" | custom-call | flops 2684354560 | bytes 10485760 | tf_op jit(solution)/shard_map/attend/pallas_call | solution.py:422
  146.0 3.8 %collective-permute-start.24 = (f32[32,640]{1,0:T(8,128)S(1)}, f32[32,640]{1,0:T(8,128)S(1)}, u32[]{:S(2)}, u32[]{:S(2)}) collective-permute-start(f32[32,640]{1,0:T(8,128)S(1)} %get-tuple-element.38), channel_id=1, source_target_pairs={{0,4},{2,6},{4,8},{6,10},{8,12},{10,14},{12,0},{14,2},{1,5},{3,7},... | collective-permute-start | bytes 245768 | tf_op jit(solution)/shard_map/ppermute | solution.py:539
  149.8 1.5 collective-permute-start.26
  151.3 3.7 %collective-permute-done.24.refs_1_ = f32[32,640]{1,0:T(8,128)S(1)} collective-permute-done((f32[32,640]{1,0:T(8,128)S(1)}, f32[32,640]{1,0:T(8,128)S(1)}, u32[]{:S(2)}, u32[]{:S(2)}) %collective-permute-start.24) | collective-permute-done | bytes 81952 | tf_op jit(solution)/shard_map/ppermute | solution.py:539
  155.0 1.7 collective-permute-done.25.refs_2_
  157.4 2.1 %merge.1 = bf16[32,512]{1,0:T(8,128)(2,1)} custom-call(f32[32,640]{1,0:T(8,128)} %copy-done.2, f32[32,640]{1,0:T(8,128)} %copy-done.5, f32[32,640]{1,0:T(8,128)} %copy-done.6, f32[32,640]{1,0:T(8,128)} %copy-done.7), custom_call_target="tpu_custom_call" | custom-call | flops 163840 | bytes 327680 | tf_op jit(solution)/shard_map/merge/pallas_call | solution.py:474
  159.4 1.9 %collective-permute-start.27 = (bf16[32,512]{1,0:T(8,128)(2,1)}, bf16[32,512]{1,0:T(8,128)(2,1)S(1)}, u32[]{:S(2)}, u32[]{:S(2)}) collective-permute-start(bf16[32,512]{1,0:T(8,128)(2,1)} %merge.1), channel_id=1, source_target_pairs={{0,0},{1,8},{2,1},{3,9},{4,2},{5,10},{6,3},{7,11},{8,4},{9,12},{10... | collective-permute-start | bytes 98312 | tf_op jit(solution)/shard_map/ppermute | solution.py:550
  161.3 3.7 %collective-permute-start.28 = (bf16[32,512]{1,0:T(8,128)(2,1)}, bf16[32,512]{1,0:T(8,128)(2,1)S(1)}, u32[]{:S(2)}, u32[]{:S(2)}) collective-permute-start(bf16[32,512]{1,0:T(8,128)(2,1)} %merge.1), channel_id=1, source_target_pairs={{0,1},{1,9},{2,0},{3,8},{4,3},{5,11},{6,2},{7,10},{8,5},{9,13},{10... | collective-permute-start | bytes 98312 | tf_op jit(solution)/shard_map/ppermute | solution.py:550
  165.1 0.7 collective-permute-done.27
  165.8 2.4 %collective-permute-done.28 = bf16[32,512]{1,0:T(8,128)(2,1)S(1)} collective-permute-done((bf16[32,512]{1,0:T(8,128)(2,1)}, bf16[32,512]{1,0:T(8,128)(2,1)S(1)}, u32[]{:S(2)}, u32[]{:S(2)}) %collective-permute-start.28) | collective-permute-done | bytes 32800 | tf_op jit(solution)/shard_map/ppermute | solution.py:550
  168.2 3.0 %convolution_convert_fusion = bf16[32,2048]{1,0:T(8,128)(2,1)S(1)} fusion(bf16[1024,2048]{1,0:T(8,128)(2,1)} %param.13, bf16[32,512]{1,0:T(8,128)(2,1)S(1)} %get-tuple-element.49, bf16[32,512]{1,0:T(8,128)(2,1)S(1)} %get-tuple-element.48), kind=kOutput, calls=%fused_computation | convolution fusion | flops 134414336 | bytes 4390912 | tf_op jit(solution)/shard_map/dot_general | solution.py:554
  171.2 1.6 collective-permute-start.29
  172.8 3.6 %collective-permute-done.29 = bf16[32,2048]{1,0:T(8,128)(2,1)S(1)} collective-permute-done((bf16[32,2048]{1,0:T(8,128)(2,1)S(1)}, bf16[32,2048]{1,0:T(8,128)(2,1)S(1)}, u32[]{:S(2)}, u32[]{:S(2)}) %collective-permute-start.29) | collective-permute-done | bytes 131104 | tf_op jit(solution)/shard_map/ppermute | solution.py:555
  176.4 0.7 fusion.2
  (63 shorter events, 5.6 us)
Async XLA Ops:
  0.0 10.1 %copy-start.8 = (bf16[2048]{0:T(1024)(128)(2,1)S(1)}, bf16[2048]{0:T(1024)(128)(2,1)}, u32[]{:S(2)}) copy-start(bf16[2048]{0:T(1024)(128)(2,1)} %param.9) | copy-start | bytes 12292
  0.0 11.7 %copy-start.3 = (bf16[2048,1024]{1,0:T(8,128)(2,1)S(1)}, bf16[2048,1024]{1,0:T(8,128)(2,1)}, u32[]{:S(2)}) copy-start(bf16[2048,1024]{1,0:T(8,128)(2,1)} %param.10) | copy-start | bytes 12582916
  0.0 13.4 %copy-start.9 = (s32[8,16]{1,0:T(8,128)S(1)}, s32[8,16]{1,0:T(8,128)}, u32[]{:S(2)}) copy-start(s32[8,16]{1,0:T(8,128)} %param.15) | copy-start | bytes 1540
  0.0 13.6 %copy-start.4 = (bf16[1,32,2048]{2,1,0:T(8,128)(2,1)S(1)}, bf16[1,32,2048]{2,1,0:T(8,128)(2,1)}, u32[]{:S(2)}) copy-start(bf16[1,32,2048]{2,1,0:T(8,128)(2,1)} %param.8) | copy-start | bytes 393220
  1.5 2.0 %collective-permute-start = (bf16[256,1024]{1,0:T(8,128)(2,1)S(1)}, bf16[256,1024]{1,0:T(8,128)(2,1)S(1)}, u32[]{:S(2)}, u32[]{:S(2)}) collective-permute-start(bf16[256,1024]{1,0:T(8,128)(2,1)S(1)} %pad_maximum_fusion), channel_id=1, source_target_pairs={{0,2},{2,0},{4,6},{6,4},{8,10},{10,8},{12,14},{14,12},{1,3},{3,1},... | collective-permute-start | bytes 1572872 | tf_op jit(solution)/shard_map/ppermute | solution.py:179
  3.5 102.1 %collective-permute-start.1 = (bf16[4,256,4096]{2,1,0:T(8,128)(2,1)}, bf16[4,256,4096]{2,1,0:T(8,128)(2,1)}, u32[]{:S(2)}, u32[]{:S(2)}) collective-permute-start(bf16[4,256,4096]{2,1,0:T(8,128)(2,1)} %refs_1_.1), channel_id=1, source_target_pairs={{0,2},{2,0},{4,6},{6,4},{8,10},{10,8},{12,14},{14,12},{1,3},{3,1},... | collective-permute-start | bytes 25165832 | tf_op jit(solution)/shard_map/ppermute | solution.py:179
  3.7 27.9 %collective-permute-start.2 = (bf16[256,1024]{1,0:T(8,128)(2,1)S(1)}, bf16[256,1024]{1,0:T(8,128)(2,1)S(1)}, u32[]{:S(2)}, u32[]{:S(2)}) collective-permute-start(bf16[256,1024]{1,0:T(8,128)(2,1)S(1)} %pad_maximum_fusion.1.refs_0_), channel_id=1, source_target_pairs={{0,1},{1,0},{2,3},{3,2},{4,5},{5,4},{6,7},{7,6},{8,9},{9,8},{10,11... | collective-permute-start | bytes 1572872 | tf_op jit(solution)/shard_map/ppermute | solution.py:190
  4.3 15.8 %collective-permute-start.6 = (bf16[256,1024]{1,0:T(8,128)(2,1)S(1)}, bf16[256,1024]{1,0:T(8,128)(2,1)S(1)}, u32[]{:S(2)}, u32[]{:S(2)}) collective-permute-start(bf16[256,1024]{1,0:T(8,128)(2,1)S(1)} %pad_maximum_fusion.1.refs_0_), channel_id=1, source_target_pairs={{4,0},{6,2},{8,4},{10,6},{12,8},{14,10},{5,1},{7,3},{9,5},{11,7},{... | collective-permute-start | bytes 1572872 | tf_op jit(solution)/shard_map/ppermute | solution.py:184
  6.2 16.1 %collective-permute-start.7 = (bf16[256,1024]{1,0:T(8,128)(2,1)S(1)}, bf16[256,1024]{1,0:T(8,128)(2,1)}, u32[]{:S(2)}, u32[]{:S(2)}) collective-permute-start(bf16[256,1024]{1,0:T(8,128)(2,1)S(1)} %pad_maximum_fusion.1.refs_0_), channel_id=1, source_target_pairs={{0,4},{2,6},{4,8},{6,10},{8,12},{10,14},{1,5},{3,7},{5,9},{7,11},{... | collective-permute-start | bytes 1572872 | tf_op jit(solution)/shard_map/ppermute | solution.py:187
  10.2 19.0 %collective-permute-start.5 = (bf16[256,1024]{1,0:T(8,128)(2,1)S(1)}, bf16[256,1024]{1,0:T(8,128)(2,1)S(1)}, u32[]{:S(2)}, u32[]{:S(2)}) collective-permute-start(bf16[256,1024]{1,0:T(8,128)(2,1)S(1)} %collective-permute-done.refs_1_), channel_id=1, source_target_pairs={{0,1},{1,0},{2,3},{3,2},{4,5},{5,4},{6,7},{7,6},{8,9},{9,8},{10,11... | collective-permute-start | bytes 1572872 | tf_op jit(solution)/shard_map/ppermute | solution.py:190
  20.1 16.8 %collective-permute-start.3 = (bf16[256,1024]{1,0:T(8,128)(2,1)S(1)}, bf16[256,1024]{1,0:T(8,128)(2,1)}, u32[]{:S(2)}, u32[]{:S(2)}) collective-permute-start(bf16[256,1024]{1,0:T(8,128)(2,1)S(1)} %collective-permute-done.refs_1_), channel_id=1, source_target_pairs={{4,0},{6,2},{8,4},{10,6},{12,8},{14,10},{5,1},{7,3},{9,5},{11,7},{... | collective-permute-start | bytes 1572872 | tf_op jit(solution)/shard_map/ppermute | solution.py:184
  22.3 16.1 %collective-permute-start.4 = (bf16[256,1024]{1,0:T(8,128)(2,1)S(1)}, bf16[256,1024]{1,0:T(8,128)(2,1)S(1)}, u32[]{:S(2)}, u32[]{:S(2)}) collective-permute-start(bf16[256,1024]{1,0:T(8,128)(2,1)S(1)} %collective-permute-done.refs_1_), channel_id=1, source_target_pairs={{0,4},{2,6},{4,8},{6,10},{8,12},{10,14},{1,5},{3,7},{5,9},{7,11},{... | collective-permute-start | bytes 1572872 | tf_op jit(solution)/shard_map/ppermute | solution.py:187
  29.2 21.3 %collective-permute-start.10 = (bf16[256,1024]{1,0:T(8,128)(2,1)S(1)}, bf16[256,1024]{1,0:T(8,128)(2,1)S(1)}, u32[]{:S(2)}, u32[]{:S(2)}) collective-permute-start(bf16[256,1024]{1,0:T(8,128)(2,1)S(1)} %collective-permute-done.6), channel_id=1, source_target_pairs={{4,0},{6,2},{8,4},{10,6},{5,1},{7,3},{9,5},{11,7},{20,16},{22,18},... | collective-permute-start | bytes 1572872 | tf_op jit(solution)/shard_map/ppermute | solution.py:184
  31.6 17.0 %collective-permute-start.8 = (bf16[256,1024]{1,0:T(8,128)(2,1)S(1)}, bf16[256,1024]{1,0:T(8,128)(2,1)S(1)}, u32[]{:S(2)}, u32[]{:S(2)}) collective-permute-start(bf16[256,1024]{1,0:T(8,128)(2,1)S(1)} %broadcast_select_fusion.4.refs_4_), channel_id=1, source_target_pairs={{0,1},{1,0},{2,3},{3,2},{4,5},{5,4},{6,7},{7,6},{8,9},{9,8},{10,11... | collective-permute-start | bytes 1572872 | tf_op jit(solution)/shard_map/ppermute | solution.py:190
  36.9 11.1 %collective-permute-start.20 = (f32[32,1152]{1,0:T(8,128)S(1)}, f32[32,1152]{1,0:T(8,128)S(1)}, u32[]{:S(2)}, u32[]{:S(2)}) collective-permute-start(f32[32,1152]{1,0:T(8,128)S(1)} %pad_maximum_fusion.2), channel_id=1, source_target_pairs={{0,1},{1,0},{2,3},{3,2},{4,5},{5,4},{6,7},{7,6},{8,9},{9,8},{10,11... | collective-permute-start | bytes 442376 | tf_op jit(solution)/shard_map/ppermute | solution.py:514
  38.4 16.8 %collective-permute-start.11 = (bf16[256,1024]{1,0:T(8,128)(2,1)}, bf16[256,1024]{1,0:T(8,128)(2,1)S(1)}, u32[]{:S(2)}, u32[]{:S(2)}) collective-permute-start(bf16[256,1024]{1,0:T(8,128)(2,1)} %collective-permute-done.7), channel_id=1, source_target_pairs={{4,8},{6,10},{8,12},{10,14},{5,9},{7,11},{9,13},{11,15},{20,24},{2... | collective-permute-start | bytes 1572872 | tf_op jit(solution)/shard_map/ppermute | solution.py:187
  48.1 12.3 %collective-permute-start.9 = (bf16[256,1024]{1,0:T(8,128)(2,1)S(1)}, bf16[256,1024]{1,0:T(8,128)(2,1)S(1)}, u32[]{:S(2)}, u32[]{:S(2)}) collective-permute-start(bf16[256,1024]{1,0:T(8,128)(2,1)S(1)} %get-tuple-element.42.refs_5_), channel_id=1, source_target_pairs={{0,1},{1,0},{2,3},{3,2},{4,5},{5,4},{6,7},{7,6},{8,9},{9,8},{10,11... | collective-permute-start | bytes 1572872 | tf_op jit(solution)/shard_map/ppermute | solution.py:190
  48.6 14.8 %collective-permute-start.12 = (bf16[256,1024]{1,0:T(8,128)(2,1)S(1)}, bf16[256,1024]{1,0:T(8,128)(2,1)S(1)}, u32[]{:S(2)}, u32[]{:S(2)}) collective-permute-start(bf16[256,1024]{1,0:T(8,128)(2,1)S(1)} %get-tuple-element.43), channel_id=1, source_target_pairs={{4,0},{6,2},{8,4},{10,6},{12,8},{14,10},{5,1},{7,3},{9,5},{11,7},{... | collective-permute-start | bytes 1572872 | tf_op jit(solution)/shard_map/ppermute | solution.py:184
  50.5 14.2 %collective-permute-start.13 = (bf16[256,1024]{1,0:T(8,128)(2,1)S(1)}, bf16[256,1024]{1,0:T(8,128)(2,1)S(1)}, u32[]{:S(2)}, u32[]{:S(2)}) collective-permute-start(bf16[256,1024]{1,0:T(8,128)(2,1)S(1)} %get-tuple-element.41), channel_id=1, source_target_pairs={{0,4},{2,6},{4,8},{6,10},{8,12},{10,14},{1,5},{3,7},{5,9},{7,11},{... | collective-permute-start | bytes 1572872 | tf_op jit(solution)/shard_map/ppermute | solution.py:187
  64.7 40.9 %copy-start = (bf16[256,1024]{1,0:T(8,128)(2,1)}, bf16[256,1024]{1,0:T(8,128)(2,1)S(1)}, u32[]{:S(2)}) copy-start(bf16[256,1024]{1,0:T(8,128)(2,1)S(1)} %collective-permute-done.13.refs_12_.refs_4_) | copy-start | bytes 1572868
  64.7 13.8 %collective-permute-start.14 = (bf16[256,1024]{1,0:T(8,128)(2,1)S(1)}, bf16[256,1024]{1,0:T(8,128)(2,1)S(1)}, u32[]{:S(2)}, u32[]{:S(2)}) collective-permute-start(bf16[256,1024]{1,0:T(8,128)(2,1)S(1)} %collective-permute-done.10), channel_id=1, source_target_pairs={{4,0},{6,2},{5,1},{7,3},{20,16},{22,18},{21,17},{23,19}} | collective-permute-start | bytes 1572872 | tf_op jit(solution)/shard_map/ppermute | solution.py:184
  66.2 13.6 %collective-permute-start.15 = (bf16[256,1024]{1,0:T(8,128)(2,1)S(1)}, bf16[256,1024]{1,0:T(8,128)(2,1)S(1)}, u32[]{:S(2)}, u32[]{:S(2)}) collective-permute-start(bf16[256,1024]{1,0:T(8,128)(2,1)S(1)} %collective-permute-done.11), channel_id=1, source_target_pairs={{8,12},{10,14},{9,13},{11,15},{24,28},{26,30},{25,29},{27,31}} | collective-permute-start | bytes 1572872 | tf_op jit(solution)/shard_map/ppermute | solution.py:187
  66.9 34.9 %collective-permute-start.17 = (bf16[256,1024]{1,0:T(8,128)(2,1)S(1)}, bf16[256,1024]{1,0:T(8,128)(2,1)S(1)}, u32[]{:S(2)}, u32[]{:S(2)}) collective-permute-start(bf16[256,1024]{1,0:T(8,128)(2,1)S(1)} %collective-permute-done.12.refs_9_.refs_3_), channel_id=1, source_target_pairs={{4,0},{6,2},{8,4},{10,6},{5,1},{7,3},{9,5},{11,7},{20,16},{22,18},... | collective-permute-start | bytes 1572872 | tf_op jit(solution)/shard_map/ppermute | solution.py:184
  68.8 33.0 %collective-permute-start.18 = (bf16[256,1024]{1,0:T(8,128)(2,1)S(1)}, bf16[256,1024]{1,0:T(8,128)(2,1)S(1)}, u32[]{:S(2)}, u32[]{:S(2)}) collective-permute-start(bf16[256,1024]{1,0:T(8,128)(2,1)S(1)} %collective-permute-done.13.refs_12_.refs_4_), channel_id=1, source_target_pairs={{4,8},{6,10},{8,12},{10,14},{5,9},{7,11},{9,13},{11,15},{20,24},{2... | collective-permute-start | bytes 1572872 | tf_op jit(solution)/shard_map/ppermute | solution.py:187
  78.5 23.3 %collective-permute-start.16 = (bf16[256,1024]{1,0:T(8,128)(2,1)S(1)}, bf16[256,1024]{1,0:T(8,128)(2,1)S(1)}, u32[]{:S(2)}, u32[]{:S(2)}) collective-permute-start(bf16[256,1024]{1,0:T(8,128)(2,1)S(1)} %select_select_fusion.1.refs_8_), channel_id=1, source_target_pairs={{0,1},{1,0},{2,3},{3,2},{4,5},{5,4},{6,7},{7,6},{8,9},{9,8},{10,11... | collective-permute-start | bytes 1572872 | tf_op jit(solution)/shard_map/ppermute | solution.py:190
  79.7 22.0 %collective-permute-start.19 = (bf16[256,1024]{1,0:T(8,128)(2,1)S(1)}, bf16[256,1024]{1,0:T(8,128)(2,1)S(1)}, u32[]{:S(2)}, u32[]{:S(2)}) collective-permute-start(bf16[256,1024]{1,0:T(8,128)(2,1)S(1)} %broadcast_select_fusion), channel_id=1, source_target_pairs={{0,1},{1,0},{2,3},{3,2},{12,13},{13,12},{14,15},{15,14},{16,17},{1... | collective-permute-start | bytes 1572872 | tf_op jit(solution)/shard_map/ppermute | solution.py:212
  101.9 34.8 %collective-permute-start.21 = (bf16[256,1024]{1,0:T(8,128)(2,1)S(1)}, bf16[256,1024]{1,0:T(8,128)(2,1)S(1)}, u32[]{:S(2)}, u32[]{:S(2)}) collective-permute-start(bf16[256,1024]{1,0:T(8,128)(2,1)S(1)} %select_select_fusion.refs_1_), channel_id=1, source_target_pairs={{0,1},{1,0},{2,3},{3,2},{4,5},{5,4},{6,7},{7,6},{8,9},{9,8},{10,11... | collective-permute-start | bytes 1572872 | tf_op jit(solution)/shard_map/ppermute | solution.py:190
  102.5 34.2 %collective-permute-start.22 = (bf16[256,1024]{1,0:T(8,128)(2,1)S(1)}, bf16[256,1024]{1,0:T(8,128)(2,1)S(1)}, u32[]{:S(2)}, u32[]{:S(2)}) collective-permute-start(bf16[256,1024]{1,0:T(8,128)(2,1)S(1)} %collective-permute-done.17.refs_2_.refs_9_), channel_id=1, source_target_pairs={{4,0},{6,2},{5,1},{7,3},{20,16},{22,18},{21,17},{23,19}} | collective-permute-start | bytes 1572872 | tf_op jit(solution)/shard_map/ppermute | solution.py:184
  104.9 31.8 %collective-permute-start.23 = (bf16[256,1024]{1,0:T(8,128)(2,1)S(1)}, bf16[256,1024]{1,0:T(8,128)(2,1)S(1)}, u32[]{:S(2)}, u32[]{:S(2)}) collective-permute-start(bf16[256,1024]{1,0:T(8,128)(2,1)S(1)} %collective-permute-done.18.refs_5_.refs_10_), channel_id=1, source_target_pairs={{8,12},{10,14},{9,13},{11,15},{24,28},{26,30},{25,29},{27,31}} | collective-permute-start | bytes 1572872 | tf_op jit(solution)/shard_map/ppermute | solution.py:187
  121.9 1.0 copy-start.1
  145.4 0.6 copy-start.2
  146.0 8.9 %collective-permute-start.24 = (f32[32,640]{1,0:T(8,128)S(1)}, f32[32,640]{1,0:T(8,128)S(1)}, u32[]{:S(2)}, u32[]{:S(2)}) collective-permute-start(f32[32,640]{1,0:T(8,128)S(1)} %get-tuple-element.38), channel_id=1, source_target_pairs={{0,4},{2,6},{4,8},{6,10},{8,12},{10,14},{12,0},{14,2},{1,5},{3,7},... | collective-permute-start | bytes 245768 | tf_op jit(solution)/shard_map/ppermute | solution.py:539
  149.8 6.9 %collective-permute-start.25 = (f32[32,640]{1,0:T(8,128)S(1)}, f32[32,640]{1,0:T(8,128)S(1)}, u32[]{:S(2)}, u32[]{:S(2)}) collective-permute-start(f32[32,640]{1,0:T(8,128)S(1)} %get-tuple-element.39), channel_id=1, source_target_pairs={{0,8},{2,10},{4,12},{6,14},{8,0},{10,2},{12,4},{14,6},{1,9},{3,11}... | collective-permute-start | bytes 245768 | tf_op jit(solution)/shard_map/ppermute | solution.py:539
  149.8 6.9 %collective-permute-start.26 = (f32[32,640]{1,0:T(8,128)S(1)}, f32[32,640]{1,0:T(8,128)S(1)}, u32[]{:S(2)}, u32[]{:S(2)}) collective-permute-start(f32[32,640]{1,0:T(8,128)S(1)} %get-tuple-element.40), channel_id=1, source_target_pairs={{0,12},{2,14},{4,0},{6,2},{8,4},{10,6},{12,8},{14,10},{1,13},{3,15... | collective-permute-start | bytes 245768 | tf_op jit(solution)/shard_map/ppermute | solution.py:539
  155.0 1.7 copy-start.5
  156.7 0.6 copy-start.6
  156.7 0.7 copy-start.7
  159.4 6.3 %collective-permute-start.27 = (bf16[32,512]{1,0:T(8,128)(2,1)}, bf16[32,512]{1,0:T(8,128)(2,1)S(1)}, u32[]{:S(2)}, u32[]{:S(2)}) collective-permute-start(bf16[32,512]{1,0:T(8,128)(2,1)} %merge.1), channel_id=1, source_target_pairs={{0,0},{1,8},{2,1},{3,9},{4,2},{5,10},{6,3},{7,11},{8,4},{9,12},{10... | collective-permute-start | bytes 98312 | tf_op jit(solution)/shard_map/ppermute | solution.py:550
  161.3 6.9 %collective-permute-start.28 = (bf16[32,512]{1,0:T(8,128)(2,1)}, bf16[32,512]{1,0:T(8,128)(2,1)S(1)}, u32[]{:S(2)}, u32[]{:S(2)}) collective-permute-start(bf16[32,512]{1,0:T(8,128)(2,1)} %merge.1), channel_id=1, source_target_pairs={{0,1},{1,9},{2,0},{3,8},{4,3},{5,11},{6,2},{7,10},{8,5},{9,13},{10... | collective-permute-start | bytes 98312 | tf_op jit(solution)/shard_map/ppermute | solution.py:550
  171.2 5.2 %collective-permute-start.29 = (bf16[32,2048]{1,0:T(8,128)(2,1)S(1)}, bf16[32,2048]{1,0:T(8,128)(2,1)S(1)}, u32[]{:S(2)}, u32[]{:S(2)}) collective-permute-start(bf16[32,2048]{1,0:T(8,128)(2,1)S(1)} %convolution_convert_fusion), channel_id=1, source_target_pairs={{0,16},{16,0},{1,17},{17,1},{2,18},{18,2},{3,19},{19,3},{4,20},{20... | collective-permute-start | bytes 393224 | tf_op jit(solution)/shard_map/ppermute | solution.py:555

commit v2 on v1

--- a/solution.py
+++ b/solution.py
@@ -156,6 +156,7 @@
 
 
 CHIPS = 4
+VMEM_LIMIT = 56 * 2**20
 PIECE = 256
 
 
@@ -163,8 +164,21 @@
     return [(2 * z + c, 2 * (z + step) + c) for z in sources for c in range(2)]
 
 
+def nothing(*refs):
+    pass
+
+
 def after(values, done):
-    return lax.optimization_barrier((tuple(values), tuple(done)))[0]
+    anywhere = pl.BlockSpec(memory_space=pl.ANY)
+    count = len(values)
+    return pl.pallas_call(
+        nothing,
+        in_specs=[anywhere] * (count + len(done)),
+        out_specs=[anywhere] * count,
+        out_shape=[jax.ShapeDtypeStruct(value.shape, value.dtype) for value in values],
+        input_output_aliases={k: k for k in range(count)},
+        name="after",
+    )(*values, *done)
 
 
 def by_chip(z, options):
@@ -179,69 +193,84 @@
     return lax.ppermute(value, "pb", [(p, p ^ 1) for p in range(2 * CHIPS)])
 
 
-def gather_pieces(own, partner, z):
+def gather_pieces(own, partner, z, add_pieces, terms, pair_of, questions, other_rows):
     def left(value, sources):
         return lax.ppermute(value, "pb", line(-1, sources))
 
     def right(value, sources):
         return lax.ppermute(value, "pb", line(1, sources))
 
+    def outward(value):
+        return lax.ppermute(value, "pb", line(-1, (1,)) + line(1, (2,)))
+
     def across(value):
         return lax.ppermute(value, "fsdp", [(0, 1), (1, 0)])
 
-    l_a1, r_a1, x_b = left(own, (1, 2, 3)), right(own, (0, 1, 2)), across(partner)
-    l_b1, r_b1, x_a = left(partner, (1, 2, 3)), right(partner, (0, 1, 2)), across(own)
-
-    l_a1, r_a1 = after((l_a1, r_a1), (x_b,))
-    a1 = jnp.where(z < 2, l_a1, r_a1)
-    l_a2, r_a2, x_a1 = left(l_a1, (1, 2)), right(r_a1, (1, 2)), across(a1)
-
-    l_b1, r_b1, x_b = after((l_b1, r_b1, x_b), (x_a,))
-    b1 = jnp.where(z < 2, l_b1, r_b1)
+    here, second, third, fourth = (0, 1, 2, 3), (1, 2, 1, 2), (2, 0, 3, 1), (3, 3, 0, 0)
+
+    x_b = across(own)
+    l_b1, r_b1 = left(own, (1, 2, 3)), right(own, (0, 1, 2))
+    l_a1, r_a1 = left(partner, (1, 2, 3)), right(partner, (0, 1, 2))
+    x_a = across(partner)
+
+    both = terms + across(terms)
+    pair = pair_of(both)
+
     l_b2 = left(jnp.where(z == 3, x_b, l_b1), (1, 2, 3))
     r_b2 = right(jnp.where(z == 0, x_b, r_b1), (0, 1, 2))
-    x_b1 = across(b1)
-
-    l_a2, r_a2 = after((l_a2, r_a2), (x_a1,))
+    l_a2, r_a2 = left(l_a1, (1, 2)), right(r_a1, (1, 2))
+    ab1 = jnp.where(z < 2, jnp.concatenate([l_a1, l_b1]), jnp.concatenate([r_a1, r_b1]))
+    (ab1,) = after((ab1,), (x_a,))
+    x_ab1 = across(ab1)
+
+    l_b3, r_b3 = left(l_b2, (1, 2)), right(r_b2, (1, 2))
+    end_a3 = outward(jnp.where(z < 2, l_a2, r_a2))
     a2 = by_chip(z, (l_a2, r_a1, l_a1, r_a2))
-    l_a3, r_a3, x_a2 = left(l_a2, (1,)), right(r_a2, (2,)), across(a2)
-
-    l_b2, r_b2 = after((l_b2, r_b2), (x_b1,))
-    l_b3, r_b3 = left(l_b2, (1, 2)), right(r_b2, (1, 2))
-    ends = [(4 * k + 2 * c + x, 4 * k + 2 * c + 1 - x) for k in (0, 3) for c in range(2) for x in range(2)]
-    x_b2 = lax.ppermute(jnp.where(z == 0, l_b2, r_b2), ("pb", "fsdp"), ends)
-
-    l_a3, r_a3 = after((l_a3, r_a3), (x_a2,))
-    a3 = by_chip(z, (l_a3, l_a2, r_a2, r_a3))
+    ab2 = jnp.concatenate([a2, jnp.where(z < 2, l_b2, r_b2)])
+    x_ab2 = across(ab2)
+
+    def all_z(piece, part=0):
+        return ((piece, part),) * 4
+
+    def each_z(*pieces):
+        return tuple((piece, 0) for piece in pieces)
+
+    sums, token = add_pieces(
+        [
+            (all_z(own), here, 0, 0),
+            (all_z(partner), here, 0, 1),
+            (all_z(x_b), here, 1, 0),
+            (all_z(x_a), here, 1, 1),
+            (all_z(ab1, 0), second, 0, 1),
+            (all_z(ab1, 1), second, 0, 0),
+            (all_z(x_ab1, 0), second, 1, 1),
+            (all_z(x_ab1, 1), second, 1, 0),
+            (all_z(ab2, 0), third, 0, 1),
+            (each_z(l_b2, r_b1, l_b1, r_b2), third, 0, 0),
+        ],
+        None,
+    )
+
+    end_a3, l_b3, r_b3 = after((end_a3, l_b3, r_b3), (token,))
+    a3 = by_chip(z, (end_a3, l_a2, r_a2, end_a3))
     x_a3 = across(a3)
-
-    l_b3, r_b3 = after((l_b3, r_b3), (x_b2,))
-    l_b4, r_b4 = left(l_b3, (1,)), right(r_b3, (2,))
-
-    here = (0, 1, 2, 3)
-    early = [
-        ((own,) * 4, here, 0, 0),
-        ((partner,) * 4, here, 0, 1),
-        ((x_a,) * 4, here, 1, 0),
-        ((x_b,) * 4, here, 1, 1),
-        ((a1,) * 4, (1, 2, 1, 2), 0, 0),
-        ((b1,) * 4, (1, 2, 1, 2), 0, 1),
-        ((x_a1,) * 4, (1, 2, 1, 2), 1, 0),
-        ((x_b1,) * 4, (1, 2, 1, 2), 1, 1),
-        ((a2,) * 4, (2, 0, 3, 1), 0, 0),
-        ((l_b2, r_b1, l_b1, r_b2), (2, 0, 3, 1), 0, 1),
+    end_b4 = outward(jnp.where(z < 2, l_b3, r_b3))
+    queries = spread_queries(after((pair,), (token,))[0], questions)
+
+    sums, token = add_pieces(
+        [
+            (all_z(a3), fourth, 0, 1),
+            (each_z(l_b3, l_b2, r_b2, r_b3), fourth, 0, 0),
+            (all_z(x_ab2, 0), third, 1, 1),
+            (((x_ab2, 1), (r_b2, 0), (l_b2, 0), (x_ab2, 1)), third, 1, 0),
+        ],
+        sums,
+    )
+    last = [
+        (all_z(x_a3), fourth, 1, 1),
+        (each_z(end_b4, l_b3, r_b3, end_b4), fourth, 1, 0),
     ]
-    later = [
-        ((a3,) * 4, (3, 3, 0, 0), 0, 0),
-        ((l_b3, l_b2, r_b2, r_b3), (3, 3, 0, 0), 0, 1),
-        ((x_a2,) * 4, (2, 0, 3, 1), 1, 0),
-        ((x_b2, r_b2, l_b2, x_b2), (2, 0, 3, 1), 1, 1),
-    ]
-    last = [
-        ((x_a3,) * 4, (3, 3, 0, 0), 1, 0),
-        ((l_b4, l_b3, r_b3, r_b4), (3, 3, 0, 0), 1, 1),
-    ]
-    return early, later, last
+    return sums, last, queries
 
 
 def feature_blocks(pieces, z, c, f):
@@ -258,51 +287,53 @@
     arrays, wanted = [], []
     for options, _, _, _ in pieces:
         spots = []
-        for option in options:
+        for option, part in options:
             at = next((k for k, seen in enumerate(arrays) if seen is option), None)
             if at is None:
                 at = len(arrays)
                 arrays.append(option)
-            spots.append(at)
+            spots.append((at, part))
         wanted.append(spots)
     return arrays, wanted
 
 
 def load_weights(wanted, z, sources, weights, sems):
+    def copy(slot, spot):
+        at, part = spot
+        return pltpu.make_async_copy(
+            sources[at].at[pl.ds(part * PIECE, PIECE)], weights.at[pl.ds(slot * PIECE, PIECE)], sems.at[slot]
+        )
+
     for slot, spots in enumerate(wanted):
-        target = weights.at[pl.ds(slot * PIECE, PIECE)]
-        for at in sorted(set(spots)):
-            zs = [k for k, spot in enumerate(spots) if spot == at]
-
-            def begin(at=at, slot=slot, target=target):
-                pltpu.make_async_copy(sources[at], target, sems.at[slot]).start()
-
+        for spot in sorted(set(spots)):
+            zs = [k for k, other in enumerate(spots) if other == spot]
+            begin = copy(slot, spot).start
             if len(zs) == CHIPS:
                 begin()
             else:
-                hit = functools.reduce(jnp.logical_or, [z == k for k in zs])
-                pl.when(hit)(begin)
+                pl.when(functools.reduce(jnp.logical_or, [z == k for k in zs]))(lambda begin=begin: begin())
     for slot, spots in enumerate(wanted):
-        target = weights.at[pl.ds(slot * PIECE, PIECE)]
-        pltpu.make_async_copy(sources[spots[0]], target, sems.at[slot]).wait()
-
-
-def project_kernel(wanted, amount, carried, info, own_rows, other_rows, *refs):
+        copy(slot, spots[0]).wait()
+
+
+def project_kernel(wanted, amount, carried, info, *refs):
     refs = list(refs)
+    count = len(wanted)
+    halves, refs = (refs[:count], refs[count : 2 * count]), refs[2 * count :]
     before = refs.pop(0) if carried else None
-    sources, (total, weights, sems) = refs[:amount], refs[amount:]
-    count = len(wanted)
-
-    @pl.when(pl.program_id(0) == 0)
+    sources, (total, token, weights, sems) = refs[:amount], refs[amount:]
+
+    question = pl.program_id(0)
+
+    @pl.when(question == 0)
     def _():
         load_weights(wanted, info[0], sources, weights, sems)
-
-    for half, rows in enumerate((own_rows, other_rows)):
-        here = pl.ds(half * rows.shape[1], rows.shape[1])
-        features = jnp.concatenate(
-            [rows[0, :, pl.ds(pl.multiple_of(info[1 + k] * PIECE, PIECE), PIECE)] for k in range(count)],
-            axis=1,
-        )
+        token[...] = jnp.zeros_like(token)
+
+    for half, blocks in enumerate(halves):
+        rows = blocks[0].shape[1]
+        here = pl.ds(half * rows, rows)
+        features = jnp.concatenate([block[0] for block in blocks], axis=1)
         part = jnp.dot(features, weights[...], preferred_element_type=jnp.float32)
         if carried:
             part = part + before[0, here, :]
@@ -311,40 +342,40 @@
 
 def project_pieces(info, pieces, own_rows, other_rows, before=None):
     questions, rows, width = own_rows.shape
-    columns = pieces[0][0][0].shape[1]
+    columns = pieces[0][0][0][0].shape[1]
     arrays, wanted = distinct(pieces)
     count = len(pieces)
     carried = before is not None
-    block = pl.BlockSpec((1, rows, width), lambda i, info: (i, 0, 0))
+    blocks = [pl.BlockSpec((1, rows, PIECE), lambda i, info, k=k: (i, 0, info[1 + k])) for k in range(count)]
     sums = pl.BlockSpec((1, 2 * rows, columns), lambda i, info: (i, 0, 0))
     anywhere = pl.BlockSpec(memory_space=pl.ANY)
-    flops = 2 * questions * 2 * rows * count * PIECE * columns
     return pl.pallas_call(
         functools.partial(project_kernel, wanted, len(arrays), carried),
         grid_spec=pltpu.PrefetchScalarGridSpec(
             num_scalar_prefetch=1,
             grid=(questions,),
-            in_specs=[block, block] + ([sums] if carried else []) + [anywhere] * len(arrays),
-            out_specs=sums,
+            in_specs=blocks + blocks + ([sums] if carried else []) + [anywhere] * len(arrays),
+            out_specs=[sums, pl.BlockSpec((8, 128), lambda i, info: (0, 0))],
             scratch_shapes=[
                 pltpu.VMEM((count * PIECE, columns), jnp.bfloat16),
                 pltpu.SemaphoreType.DMA((count,)),
             ],
         ),
-        out_shape=jax.ShapeDtypeStruct((questions, 2 * rows, columns), jnp.float32),
-        input_output_aliases={3: 0} if carried else {},
-        compiler_params=pltpu.CompilerParams(vmem_limit_bytes=48 * 2**20),
-        cost_estimate=pl.CostEstimate(
-            flops=flops, bytes_accessed=questions * rows * (4 * width + 8 * columns), transcendentals=0
-        ),
+        out_shape=[
+            jax.ShapeDtypeStruct((questions, 2 * rows, columns), jnp.float32),
+            jax.ShapeDtypeStruct((8, 128), jnp.float32),
+        ],
+        input_output_aliases={2 * count + 1: 0} if carried else {},
+        compiler_params=pltpu.CompilerParams(vmem_limit_bytes=VMEM_LIMIT),
+        cost_estimate=pl.CostEstimate(flops=1000, bytes_accessed=1000, transcendentals=0),
         name="project",
-    )(info, own_rows, other_rows, *([before] if carried else []), *arrays)
+    )(info, *([own_rows] * count), *([other_rows] * count), *([before] if carried else []), *arrays)
 
 
 def attend_kernel(wanted, amount, info, *refs):
     refs = list(refs)
     count = len(wanted)
-    own_blocks, other_blocks, refs = refs[:count], refs[count : 2 * count], refs[2 * count :]
+    halves, refs = (refs[:count], refs[count : 2 * count]), refs[2 * count :]
     before, queries, live, refs = refs[0], refs[1], refs[2], refs[3:]
     sources, refs = refs[:amount], refs[amount:]
     outs, (weights, sems) = refs[:CHIPS], refs[CHIPS:]
@@ -354,13 +385,13 @@
     def _():
         load_weights(wanted, info[0], sources, weights, sems)
 
-    halves = []
-    for half, blocks in enumerate((own_blocks, other_blocks)):
+    found = []
+    for half, blocks in enumerate(halves):
         rows = blocks[0].shape[1]
         features = jnp.concatenate([block[0] for block in blocks], axis=1)
         part = jnp.dot(features, weights[...], preferred_element_type=jnp.float32)
-        halves.append((part + before[0, pl.ds(half * rows, rows), :]).astype(jnp.bfloat16))
-    keyval = jnp.concatenate(halves, axis=0)
+        found.append((part + before[0, pl.ds(half * rows, rows), :]).astype(jnp.bfloat16))
+    keyval = jnp.concatenate(found, axis=0)
     width = keyval.shape[1] // 2
     answers = queries.shape[1]
     group = 4
@@ -403,7 +434,7 @@
 
 def attend_last(info, pieces, own_rows, other_rows, before, queries, live):
     questions, rows, width = own_rows.shape
-    columns = pieces[0][0][0].shape[1]
+    columns = pieces[0][0][0][0].shape[1]
     answers = queries.shape[1]
     arrays, wanted = distinct(pieces)
     count = len(pieces)
@@ -411,6 +442,12 @@
 
     def question(i, info):
         return lax.rem(i + info[0], questions)
+
+    def turned(i, info):
+        wanted = question(i, info)
+        pairs = questions // 2
+        return 2 * lax.rem(wanted // 2 + info[0] * (pairs - 1), pairs) + lax.rem(wanted, 2)
+
 
     blocks = [
         pl.BlockSpec((1, rows, PIECE), lambda i, info, k=k: (question(i, info), 0, info[1 + k]))
@@ -426,7 +463,11 @@
             grid=(questions,),
             in_specs=blocks
             + blocks
-            + [whole(2 * rows, columns), whole(answers, columns // 2), whole(1, 2 * rows)]
+            + [
+                whole(2 * rows, columns),
+                pl.BlockSpec((1, answers, columns // 2), lambda i, info: (turned(i, info), 0, 0)),
+                whole(1, 2 * rows),
+            ]
             + [anywhere] * len(arrays),
             out_specs=[pl.BlockSpec((answers, wide), lambda i, info: (0, 0))] * CHIPS,
             scratch_shapes=[
@@ -435,7 +476,7 @@
             ],
         ),
         out_shape=[jax.ShapeDtypeStruct((answers, wide), jnp.float32)] * CHIPS,
-        compiler_params=pltpu.CompilerParams(vmem_limit_bytes=48 * 2**20),
+        compiler_params=pltpu.CompilerParams(vmem_limit_bytes=VMEM_LIMIT),
         cost_estimate=pl.CostEstimate(
             flops=flops,
             bytes_accessed=questions * rows * (8 * columns + 4 * count * PIECE),
@@ -477,6 +518,28 @@
         cost_estimate=pl.CostEstimate(flops=8 * answers * wide, bytes_accessed=16 * answers * wide, transcendentals=512 * answers),
         name="merge",
     )(*parts)
+
+
+def query_terms(states, norm_gain, query_weight):
+    states_wide = states.astype(jnp.float32)
+    square_part = jnp.sum(states_wide * states_wide, axis=1, keepdims=True)
+    scaled = (states_wide * norm_gain.astype(jnp.float32)[None, :]).astype(jnp.bfloat16)
+    query_part = jnp.dot(scaled, query_weight, preferred_element_type=jnp.float32)
+    return jnp.concatenate([query_part, jnp.broadcast_to(square_part, (square_part.shape[0], 128))], axis=1)
+
+
+def spread_queries(pair, questions):
+    pairs = questions // 2
+    spread = []
+    for turn in range(pairs):
+        sends = []
+        for place in range(2):
+            for to in range(CHIPS):
+                chip = pairs * place + (to + turn) % pairs
+                for core in range(2):
+                    sends.append((2 * (2 * chip + core) + to // pairs, 2 * (2 * to + core) + place))
+        spread.append(lax.ppermute(pair, ("pb", "fsdp"), sends))
+    return spread
 
 
 def gathered_shards(
@@ -502,22 +565,25 @@
 
     own = core_columns(c)
     partner = core_swap(core_columns(1 - c))
-    early, later, last = gather_pieces(own, partner, z)
-    other_rows = core_swap(after((passage_states,), (partner,))[0])
-
-    own_states = decoder_states[0]
-    states_wide = own_states.astype(jnp.float32)
-    square_part = jnp.sum(states_wide * states_wide, axis=1, keepdims=True)
-    scaled = (states_wide * norm_gain.astype(jnp.float32)[None, :]).astype(jnp.bfloat16)
-    query_part = jnp.dot(scaled, query_weight, preferred_element_type=jnp.float32)
-    both = jnp.concatenate([query_part, jnp.broadcast_to(square_part, (square_part.shape[0], 128))], axis=1)
-    both = both + lax.ppermute(both, "fsdp", [(0, 1), (1, 0)])
-    query_raw, square_sum = both[:, :-128], both[:, -128:-127]
-    query = (query_raw * lax.rsqrt(square_sum / model_width + 1e-06)).astype(jnp.bfloat16)
-    every_query = lax.all_gather(query, "pb")
-    queries = lax.dynamic_slice(
-        every_query, (f * questions, 0, c * width), (questions, query.shape[0], width)
-    )
+    other_rows = core_swap(passage_states)
+
+    def info(pieces):
+        return jnp.concatenate([z[None], feature_blocks(pieces, z, c, f)]).astype(jnp.int32)
+
+    def add_pieces(pieces, sums):
+        return project_pieces(info(pieces), pieces, passage_states, other_rows, sums)
+
+    terms = query_terms(decoder_states[0], norm_gain, query_weight)
+
+    def pair_of(both):
+        query_raw, square_sum = both[:, :-128], both[:, -128:-127]
+        query = (query_raw * lax.rsqrt(square_sum / model_width + 1e-06)).astype(jnp.bfloat16)
+        mine = lax.dynamic_slice_in_dim(query, c * width, width, 1)
+        theirs = core_swap(lax.dynamic_slice_in_dim(query, (1 - c) * width, width, 1))
+        return jnp.stack([jnp.where(c == 0, mine, theirs), jnp.where(c == 0, theirs, mine)])
+
+    sums, last, queries = gather_pieces(own, partner, z, add_pieces, terms, pair_of, questions, other_rows)
+    queries = jnp.concatenate(queries, axis=0)
 
     blocks_here = rows // BLOCK
     mine = lax.dynamic_slice_in_dim(block_mask, f * questions, questions, 0)
@@ -527,11 +593,6 @@
     )
     live = jnp.repeat(live, BLOCK, axis=1)[:, None, :]
 
-    def info(pieces):
-        return jnp.concatenate([z[None], feature_blocks(pieces, z, c, f)]).astype(jnp.int32)
-
-    sums = project_pieces(info(early), early, passage_states, other_rows)
-    sums = project_pieces(info(later), later, passage_states, other_rows, sums)
     parts = attend_last(info(last), last, passage_states, other_rows, sums, queries, live)
     arrived = [parts[0]]
     for step in range(1, CHIPS):

time: 179 us -> 156 us (0.87)
  blocking collectives: 21.2 us -> 0 us
  waiting for transfers between devices: 46.5 us -> 33.2 us
  other arithmetic: 3.89 us -> 11.5 us
  Pallas kernels: 40.7 us -> 45.3 us
  starting transfers between devices: 55.6 us -> 52.1 us
  local copies, waits for them, and re-layouts: 4.16 us -> 6.07 us
    all_gather x1 -> x0, blocking collectives: 21.2 us -> none  [gathered_shards(): every_query = lax.all_gather(query, 'pb')]
    ppermute x2 -> x4, starting transfers between devices: 2.17 us -> 10.6 us  [the longest x2 6.63 us: spread_queries(): spread.append(lax.ppermute(pair, ('pb', 'fsdp'), sends))]
    ppermute x6, waiting for transfers between devices: 8.1 us -> 0.72 us  [across(): return lax.ppermute(value, 'fsdp', [(0, 1), (1, 0)])]
    ppermute x2 -> x4, waiting for transfers between devices: 6.13 us -> 0.01 us  [the longest x2 0.01 us: outward(): return lax.ppermute(value, 'pb', line(-1, (1,)) + line(1, (2,)))]
    ppermute x7 -> x5, starting transfers between devices: 21.8 us -> 15.9 us  [right(): return lax.ppermute(value, 'pb', line(1, sources))]
    select_n x2 -> x4, other arithmetic: 0.13 us -> 5.04 us  [the longest x1 2.47 us: gather_pieces(): jnp.where(z < 2, jnp.concatenate([l_a1, l_b1]), jnp.concatenate([r_a1, r_...]
    ppermute x7 -> x5, waiting for transfers between devices: 16.8 us -> 12.9 us  [left(): return lax.ppermute(value, 'pb', line(-1, sources))]
    ppermute x2, starting transfers between devices: 5.62 us -> 2.9 us  [gathered_shards(): received.append(lax.ppermute(attention, ('pb', 'fsdp'), sends))]
  transfers between devices with their start and end apart: 30 -> 29, of which waited for: 14 -> 14; matrix products, arithmetic and copies ran while one was open for 3% -> 11% of each run, Pallas kernels for 17% -> 21%
where the time goes in v2:
time: 156 us; the launch traced here: 155 us
  starting transfers between devices  52.1 us (33%)
  Pallas kernels  45.3 us (29%)
  waiting for transfers between devices  33.2 us (21%)
  other arithmetic  11.5 us (7%)
  local copies, waits for them, and re-layouts  6.07 us (4%)
  matrix products  6.02 us (4%)
    pallas_call x2, Pallas kernels, project_pieces(): pl.pallas_call(functools.partial(project_kernel, wanted, len(arrays), car...  32.4 us
    ppermute x5, starting transfers between devices, right(): return lax.ppermute(value, 'pb', line(1, sources))  15.9 us
    ppermute x5, waiting for transfers between devices, left(): return lax.ppermute(value, 'pb', line(-1, sources))  12.9 us
    ppermute x5, starting transfers between devices, left(): return lax.ppermute(value, 'pb', line(-1, sources))  11.5 us
    pallas_call x1, Pallas kernels, attend_last(): pl.pallas_call(functools.partial(attend_kernel, wanted, len(arrays)), gri...  10.9 us
    ppermute x3, waiting for transfers between devices, gathered_shards(): arrived.append(lax.ppermute(parts[step], 'pb', turn))  6.71 us
    ppermute x2, starting transfers between devices, spread_queries(): spread.append(lax.ppermute(pair, ('pb', 'fsdp'), sends))  6.63 us
    ppermute x2, waiting for transfers between devices, gathered_shards(): received.append(lax.ppermute(attention, ('pb', 'fsdp'), sends))  5.73 us
  transfers between devices with their start and end apart: 29, of which 14 were waited for; matrix products, arithmetic and copies ran while one was open for 11% of the time, Pallas kernels for 21%

profile of v2, /device:TPU:10, one launch (start us, length us, event | category | flops | bytes accessed | tf_op | source)
XLA Modules:
  0.0 154.8 jit_solution(13653736189375463452)
XLA Ops:
  0.0 1.3 constant_dynamic-slice_fusion.1
  2.6 1.9 %collective-permute-start.5 = (bf16[256,1024]{1,0:T(8,128)(2,1)S(1)}, bf16[256,1024]{1,0:T(8,128)(2,1)S(1)}, u32[]{:S(2)}, u32[]{:S(2)}) collective-permute-start(bf16[256,1024]{1,0:T(8,128)(2,1)S(1)} %pad_maximum_fusion.1.refs_20_), channel_id=1, source_target_pairs={{4,0},{6,2},{8,4},{10,6},{12,8},{14,10},{5,1},{7,3},{9,5},{11,7},{... | collective-permute-start | bytes 1572872 | tf_op jit(solution)/shard_map/ppermute | solution.py:198
  4.5 3.9 %collective-permute-start.7 = (bf16[256,1024]{1,0:T(8,128)(2,1)S(1)}, bf16[256,1024]{1,0:T(8,128)(2,1)S(1)}, u32[]{:S(2)}, u32[]{:S(2)}) collective-permute-start(bf16[256,1024]{1,0:T(8,128)(2,1)S(1)} %pad_maximum_fusion.1.refs_20_), channel_id=1, source_target_pairs={{0,4},{2,6},{4,8},{6,10},{8,12},{10,14},{1,5},{3,7},{5,9},{7,11},{... | collective-permute-start | bytes 1572872 | tf_op jit(solution)/shard_map/ppermute | solution.py:201
  8.7 3.0 %fusion.3 = f32[32,1024]{1,0:T(8,128)S(1)} fusion(bf16[2048,1024]{1,0:T(8,128)(2,1)} %param.10, bf16[1,32,2048]{2,1,0:T(8,128)(2,1)S(1)} %copy-done.17, f32[2048]{0:T(1024)S(1)} %convert_element_type.29), kind=kOutput, calls=%fused_computation.19 | convolution fusion | flops 134414336 | bytes 4464640 | tf_op jit(solution)/shard_map/dot_general | solution.py:527
  11.7 2.4 %collective-permute-done.1.refs_21_ = bf16[256,1024]{1,0:T(8,128)(2,1)} collective-permute-done((bf16[256,1024]{1,0:T(8,128)(2,1)S(1)}, bf16[256,1024]{1,0:T(8,128)(2,1)}, u32[]{:S(2)}, u32[]{:S(2)}) %collective-permute-start.1) | collective-permute-done | bytes 524320 | tf_op jit(solution)/shard_map/ppermute | solution.py:193
  14.0 2.3 %collective-permute-start.4 = (bf16[256,1024]{1,0:T(8,128)(2,1)}, bf16[256,1024]{1,0:T(8,128)(2,1)S(1)}, u32[]{:S(2)}, u32[]{:S(2)}) collective-permute-start(bf16[256,1024]{1,0:T(8,128)(2,1)} %collective-permute-done.1.refs_21_), channel_id=1, source_target_pairs={{4,0},{6,2},{8,4},{10,6},{12,8},{14,10},{5,1},{7,3},{9,5},{11,7},{... | collective-permute-start | bytes 1572872 | tf_op jit(solution)/shard_map/ppermute | solution.py:198
  16.4 3.5 %collective-permute-start.6 = (bf16[256,1024]{1,0:T(8,128)(2,1)}, bf16[256,1024]{1,0:T(8,128)(2,1)}, u32[]{:S(2)}, u32[]{:S(2)}) collective-permute-start(bf16[256,1024]{1,0:T(8,128)(2,1)} %collective-permute-done.1.refs_21_), channel_id=1, source_target_pairs={{0,4},{2,6},{4,8},{6,10},{8,12},{10,14},{1,5},{3,7},{5,9},{7,11},{... | collective-permute-start | bytes 1572872 | tf_op jit(solution)/shard_map/ppermute | solution.py:201
  20.0 1.2 broadcast_select_fusion
  21.2 3.0 %collective-permute-start.11 = (bf16[256,1024]{1,0:T(8,128)(2,1)}, bf16[256,1024]{1,0:T(8,128)(2,1)S(1)}, u32[]{:S(2)}, u32[]{:S(2)}) collective-permute-start(bf16[256,1024]{1,0:T(8,128)(2,1)} %get-tuple-element.28), channel_id=1, source_target_pairs={{4,0},{6,2},{8,4},{10,6},{12,8},{14,10},{5,1},{7,3},{9,5},{11,7},{... | collective-permute-start | bytes 1572872 | tf_op jit(solution)/shard_map/ppermute | solution.py:198
  24.2 0.8 collective-permute-start.3
  25.9 5.0 %collective-permute-done.4 = bf16[256,1024]{1,0:T(8,128)(2,1)S(1)} collective-permute-done((bf16[256,1024]{1,0:T(8,128)(2,1)}, bf16[256,1024]{1,0:T(8,128)(2,1)S(1)}, u32[]{:S(2)}, u32[]{:S(2)}) %collective-permute-start.4) | collective-permute-done | bytes 524320 | tf_op jit(solution)/shard_map/ppermute | solution.py:198
  32.7 3.5 %collective-permute-start.12 = (bf16[256,1024]{1,0:T(8,128)(2,1)}, bf16[256,1024]{1,0:T(8,128)(2,1)S(1)}, u32[]{:S(2)}, u32[]{:S(2)}) collective-permute-start(bf16[256,1024]{1,0:T(8,128)(2,1)} %get-tuple-element.27), channel_id=1, source_target_pairs={{0,4},{2,6},{4,8},{6,10},{8,12},{10,14},{1,5},{3,7},{5,9},{7,11},{... | collective-permute-start | bytes 1572872 | tf_op jit(solution)/shard_map/ppermute | solution.py:201
  36.2 2.5 %maximum_select_fusion.refs_0_ = bf16[512,1024]{1,0:T(8,128)(2,1)} fusion(bf16[256,1024]{1,0:T(8,128)(2,1)S(1)} %collective-permute-done.5.refs_29_, bf16[256,1024]{1,0:T(8,128)(2,1)S(1)} %collective-permute-done.4, bf16[256,1024]{1,0:T(8,128)(2,1)S(1)} %collective-permute-done.7.refs_28_, bf16[256,1024]{1,0:T(8,128)(2,1)} %collective-permute-done.6, pred[]{:T(512)S(6)} %lt.34), kind=kLoop, calls=%fused_computation.1 | loop fusion | flops 4718592 | bytes 3145729 | tf_op jit(solution)/shard_map/jit(_where)/select_n | solution.py:222
  39.2 0.8 copy-done.8
  40.0 1.0 collective-permute-start.8
  41.0 2.4 %collective-permute-start.10 = (bf16[256,1024]{1,0:T(8,128)(2,1)S(1)}, bf16[256,1024]{1,0:T(8,128)(2,1)S(1)}, u32[]{:S(2)}, u32[]{:S(2)}) collective-permute-start(bf16[256,1024]{1,0:T(8,128)(2,1)S(1)} %collective-permute-done.4), channel_id=1, source_target_pairs={{4,0},{6,2},{8,4},{10,6},{5,1},{7,3},{9,5},{11,7},{20,16},{22,18},... | collective-permute-start | bytes 1572872 | tf_op jit(solution)/shard_map/ppermute | solution.py:198
  43.4 3.5 %collective-permute-start.9 = (bf16[256,1024]{1,0:T(8,128)(2,1)}, bf16[256,1024]{1,0:T(8,128)(2,1)S(1)}, u32[]{:S(2)}, u32[]{:S(2)}) collective-permute-start(bf16[256,1024]{1,0:T(8,128)(2,1)} %collective-permute-done.6), channel_id=1, source_target_pairs={{4,8},{6,10},{8,12},{10,14},{5,9},{7,11},{9,13},{11,15},{20,24},{2... | collective-permute-start | bytes 1572872 | tf_op jit(solution)/shard_map/ppermute | solution.py:201
  47.1 0.8 collective-permute-done.12.refs_30_.refs_12_
  47.9 1.9 %collective-permute-start.14 = (bf16[256,1024]{1,0:T(8,128)(2,1)S(1)}, bf16[256,1024]{1,0:T(8,128)(2,1)S(1)}, u32[]{:S(2)}, u32[]{:S(2)}) collective-permute-start(bf16[256,1024]{1,0:T(8,128)(2,1)S(1)} %collective-permute-done.11.refs_27_.refs_11_), channel_id=1, source_target_pairs={{4,0},{6,2},{8,4},{10,6},{5,1},{7,3},{9,5},{11,7},{20,16},{22,18},... | collective-permute-start | bytes 1572872 | tf_op jit(solution)/shard_map/ppermute | solution.py:198
  49.8 7.9 %collective-permute-done.10 = bf16[256,1024]{1,0:T(8,128)(2,1)S(1)} collective-permute-done((bf16[256,1024]{1,0:T(8,128)(2,1)S(1)}, bf16[256,1024]{1,0:T(8,128)(2,1)S(1)}, u32[]{:S(2)}, u32[]{:S(2)}) %collective-permute-start.10) | collective-permute-done | bytes 524320 | tf_op jit(solution)/shard_map/ppermute | solution.py:198
  57.7 1.5 collective-permute-start.15
  59.6 1.4 broadcast_select_fusion.3
  61.0 2.1 %collective-permute-start.13 = (bf16[256,1024]{1,0:T(8,128)(2,1)S(1)}, bf16[256,1024]{1,0:T(8,128)(2,1)}, u32[]{:S(2)}, u32[]{:S(2)}) collective-permute-start(bf16[256,1024]{1,0:T(8,128)(2,1)S(1)} %get-tuple-element.25), channel_id=1, source_target_pairs={{4,0},{6,2},{8,12},{10,14},{5,1},{7,3},{9,13},{11,15},{20,16},{22,... | collective-permute-start | bytes 1572872 | tf_op jit(solution)/shard_map/ppermute | solution.py:204
  63.5 1.2 collective-permute-start.16
  64.8 19.2 %project.2 = (f32[4,512,1024]{2,1,0:T(8,128)}, f32[8,128]{1,0:T(8,128)}) custom-call(s32[11]{0:T(128)} %concatenate.38.info, bf16[4,256,4096]{2,1,0:T(8,128)(2,1)} %refs_1_.5, bf16[4,256,4096]{2,1,0:T(8,128)(2,1)} %refs_1_.5, bf16[4,256,4096]{2,1,0:T(8,128)(2,1)} %refs_1_.5, bf16[4,256,4096]{2,1,0:T(8,128)(2,1)} %refs_1_.5, bf16[4,256,4096]{2,1,0:T(8,128)(2,1)} %refs_1_.5, ...), custom_call_target="tpu_custom_call" | custom-call | flops 1000 | bytes 1000 | tf_op jit(solution)/shard_map/project/pallas_call | solution.py:352
  84.0 0.8 copy-done
  84.9 1.3 select_select_fusion.refs_9_
  86.2 1.2 collective-permute-start.21
  87.4 1.1 broadcast_select_fusion.2
  88.5 1.8 %collective-permute-start.22 = (bf16[256,1024]{1,0:T(8,128)(2,1)S(1)}, bf16[256,1024]{1,0:T(8,128)(2,1)S(1)}, u32[]{:S(2)}, u32[]{:S(2)}) collective-permute-start(bf16[256,1024]{1,0:T(8,128)(2,1)S(1)} %broadcast_select_fusion.2), channel_id=1, source_target_pairs={{4,0},{6,2},{8,12},{10,14},{5,1},{7,3},{9,13},{11,15},{20,16},{22,... | collective-permute-start | bytes 1572872 | tf_op jit(solution)/shard_map/ppermute | solution.py:204
  91.0 4.7 %collective-permute-start.20 = (bf16[2,32,512]{2,1,0:T(8,128)(2,1)}, bf16[2,32,512]{2,1,0:T(8,128)(2,1)S(1)}, u32[]{:S(2)}, u32[]{:S(2)}) collective-permute-start(bf16[2,32,512]{2,1,0:T(8,128)(2,1)} %after.5), channel_id=1, source_target_pairs={{4,0},{6,2},{0,4},{2,6},{5,8},{7,10},{1,12},{3,14},{12,1},{14,3},{... | collective-permute-start | bytes 196616 | tf_op jit(solution)/shard_map/ppermute | solution.py:541
  95.7 1.9 %collective-permute-start.19 = (bf16[2,32,512]{2,1,0:T(8,128)(2,1)}, bf16[2,32,512]{2,1,0:T(8,128)(2,1)S(1)}, u32[]{:S(2)}, u32[]{:S(2)}) collective-permute-start(bf16[2,32,512]{2,1,0:T(8,128)(2,1)} %after.5), channel_id=1, source_target_pairs={{0,0},{2,2},{4,4},{6,6},{1,8},{3,10},{5,12},{7,14},{8,1},{10,3},{1... | collective-permute-start | bytes 196616 | tf_op jit(solution)/shard_map/ppermute | solution.py:541
  98.3 13.2 %project.3 = (f32[4,512,1024]{2,1,0:T(8,128)}, f32[8,128]{1,0:T(8,128)}) custom-call(s32[5]{0:T(128)} %concatenate.37.info, bf16[4,256,4096]{2,1,0:T(8,128)(2,1)} %refs_1_.5, bf16[4,256,4096]{2,1,0:T(8,128)(2,1)} %refs_1_.5, bf16[4,256,4096]{2,1,0:T(8,128)(2,1)} %refs_1_.5, bf16[4,256,4096]{2,1,0:T(8,128)(2,1)} %refs_1_.5, ...), custom_call_target="tpu_custom_call", output_to_operand_aliasing={{0}: (9, {})} | custom-call | flops 1000 | bytes 1000 | tf_op jit(solution)/shard_map/project/pallas_call | solution.py:352
  112.3 0.8 broadcast_in_dim.20
  113.2 10.9 %attend.1 = (f32[32,640]{1,0:T(8,128)}, f32[32,640]{1,0:T(8,128)}, f32[32,640]{1,0:T(8,128)}, f32[32,640]{1,0:T(8,128)}) custom-call(s32[3]{0:T(128)} %pad_add_fusion.1.info, bf16[4,256,4096]{2,1,0:T(8,128)(2,1)} %refs_1_.5, bf16[4,256,4096]{2,1,0:T(8,128)(2,1)} %refs_1_.5, ...), custom_call_target="tpu_custom_call" | custom-call | flops 2684354560 | bytes 10485760 | tf_op jit(solution)/shard_map/attend/pallas_call | solution.py:459
  124.2 3.8 %collective-permute-start.24 = (f32[32,640]{1,0:T(8,128)}, f32[32,640]{1,0:T(8,128)S(1)}, u32[]{:S(2)}, u32[]{:S(2)}) collective-permute-start(f32[32,640]{1,0:T(8,128)} %get-tuple-element.23), channel_id=1, source_target_pairs={{0,8},{2,10},{4,12},{6,14},{8,0},{10,2},{12,4},{14,6},{1,9},{3,11}... | collective-permute-start | bytes 245768 | tf_op jit(solution)/shard_map/ppermute | solution.py:600
  128.0 1.1 collective-permute-done.23.refs_1_
  129.1 3.6 %collective-permute-done.24.refs_2_ = f32[32,640]{1,0:T(8,128)S(1)} collective-permute-done((f32[32,640]{1,0:T(8,128)}, f32[32,640]{1,0:T(8,128)S(1)}, u32[]{:S(2)}, u32[]{:S(2)}) %collective-permute-start.24) | collective-permute-done | bytes 81952 | tf_op jit(solution)/shard_map/ppermute | solution.py:600
  132.7 2.0 %collective-permute-done.25.refs_3_ = f32[32,640]{1,0:T(8,128)S(1)} collective-permute-done((f32[32,640]{1,0:T(8,128)}, f32[32,640]{1,0:T(8,128)S(1)}, u32[]{:S(2)}, u32[]{:S(2)}) %collective-permute-start.25) | collective-permute-done | bytes 81952 | tf_op jit(solution)/shard_map/ppermute | solution.py:600
  135.3 2.1 %merge.1 = bf16[32,512]{1,0:T(8,128)(2,1)} custom-call(f32[32,640]{1,0:T(8,128)} %get-tuple-element.21.refs_0_, f32[32,640]{1,0:T(8,128)} %copy-done.18, f32[32,640]{1,0:T(8,128)} %copy-done.19, f32[32,640]{1,0:T(8,128)} %copy-done.20), custom_call_target="tpu_custom_call" | custom-call | flops 163840 | bytes 327680 | tf_op jit(solution)/shard_map/merge/pallas_call | solution.py:515
  137.4 1.9 %collective-permute-start.26 = (bf16[32,512]{1,0:T(8,128)(2,1)}, bf16[32,512]{1,0:T(8,128)(2,1)S(1)}, u32[]{:S(2)}, u32[]{:S(2)}) collective-permute-start(bf16[32,512]{1,0:T(8,128)(2,1)} %merge.1), channel_id=1, source_target_pairs={{0,0},{1,8},{2,1},{3,9},{4,2},{5,10},{6,3},{7,11},{8,4},{9,12},{10... | collective-permute-start | bytes 98312 | tf_op jit(solution)/shard_map/ppermute | solution.py:611
  139.3 1.0 collective-permute-start.27
  140.3 4.9 %collective-permute-done.26 = bf16[32,512]{1,0:T(8,128)(2,1)S(1)} collective-permute-done((bf16[32,512]{1,0:T(8,128)(2,1)}, bf16[32,512]{1,0:T(8,128)(2,1)S(1)}, u32[]{:S(2)}, u32[]{:S(2)}) %collective-permute-start.26) | collective-permute-done | bytes 32800 | tf_op jit(solution)/shard_map/ppermute | solution.py:611
  145.2 0.8 collective-permute-done.27
  146.0 3.0 %convolution_convert_fusion = bf16[32,2048]{1,0:T(8,128)(2,1)S(1)} fusion(bf16[1024,2048]{1,0:T(8,128)(2,1)} %param.13, bf16[32,512]{1,0:T(8,128)(2,1)S(1)} %get-tuple-element.36, bf16[32,512]{1,0:T(8,128)(2,1)S(1)} %get-tuple-element.35), kind=kOutput, calls=%fused_computation | convolution fusion | flops 134414336 | bytes 4390912 | tf_op jit(solution)/shard_map/dot_general | solution.py:615
  149.1 1.6 %collective-permute-start.28 = (bf16[32,2048]{1,0:T(8,128)(2,1)S(1)}, bf16[32,2048]{1,0:T(8,128)(2,1)S(1)}, u32[]{:S(2)}, u32[]{:S(2)}) collective-permute-start(bf16[32,2048]{1,0:T(8,128)(2,1)S(1)} %convolution_convert_fusion), channel_id=1, source_target_pairs={{0,16},{16,0},{1,17},{17,1},{2,18},{18,2},{3,19},{19,3},{4,20},{20... | collective-permute-start | bytes 393224 | tf_op jit(solution)/shard_map/ppermute | solution.py:616
  150.6 3.4 %collective-permute-done.28 = bf16[32,2048]{1,0:T(8,128)(2,1)S(1)} collective-permute-done((bf16[32,2048]{1,0:T(8,128)(2,1)S(1)}, bf16[32,2048]{1,0:T(8,128)(2,1)S(1)}, u32[]{:S(2)}, u32[]{:S(2)}) %collective-permute-start.28) | collective-permute-done | bytes 131104 | tf_op jit(solution)/shard_map/ppermute | solution.py:616
  154.1 0.7 fusion.2
  (94 shorter events, 8.7 us)
Async XLA Ops:
  0.0 8.5 %copy-start.21 = (bf16[2048]{0:T(1024)(128)(2,1)S(1)}, bf16[2048]{0:T(1024)(128)(2,1)}, u32[]{:S(2)}) copy-start(bf16[2048]{0:T(1024)(128)(2,1)} %param.9) | copy-start | bytes 12292
  0.0 8.5 %copy-start.17 = (bf16[1,32,2048]{2,1,0:T(8,128)(2,1)S(1)}, bf16[1,32,2048]{2,1,0:T(8,128)(2,1)}, u32[]{:S(2)}) copy-start(bf16[1,32,2048]{2,1,0:T(8,128)(2,1)} %param.8) | copy-start | bytes 393220
  0.0 64.7 %collective-permute-start = (bf16[4,256,4096]{2,1,0:T(8,128)(2,1)}, bf16[4,256,4096]{2,1,0:T(8,128)(2,1)}, u32[]{:S(2)}, u32[]{:S(2)}) collective-permute-start(bf16[4,256,4096]{2,1,0:T(8,128)(2,1)} %refs_1_.5), channel_id=1, source_target_pairs={{0,2},{2,0},{4,6},{6,4},{8,10},{10,8},{12,14},{14,12},{1,3},{3,1},... | collective-permute-start | bytes 25165832 | tf_op jit(solution)/shard_map/ppermute | solution.py:193
  1.4 23.7 %copy-start.22 = (s32[8,16]{1,0:T(8,128)S(1)}, s32[8,16]{1,0:T(8,128)}, u32[]{:S(2)}) copy-start(s32[8,16]{1,0:T(8,128)} %param.15) | copy-start | bytes 1540
  1.4 12.6 %collective-permute-start.1 = (bf16[256,1024]{1,0:T(8,128)(2,1)S(1)}, bf16[256,1024]{1,0:T(8,128)(2,1)}, u32[]{:S(2)}, u32[]{:S(2)}) collective-permute-start(bf16[256,1024]{1,0:T(8,128)(2,1)S(1)} %pad_maximum_fusion.2), channel_id=1, source_target_pairs={{0,2},{2,0},{4,6},{6,4},{8,10},{10,8},{12,14},{14,12},{1,3},{3,1},... | collective-permute-start | bytes 1572872 | tf_op jit(solution)/shard_map/ppermute | solution.py:193
  2.0 30.8 %copy-start.9 = (bf16[256,1024]{1,0:T(8,128)(2,1)}, bf16[256,1024]{1,0:T(8,128)(2,1)S(1)}, u32[]{:S(2)}) copy-start(bf16[256,1024]{1,0:T(8,128)(2,1)S(1)} %pad_maximum_fusion.1.refs_20_) | copy-start | bytes 1572868
  2.0 14.4 %collective-permute-start.2 = (bf16[256,1024]{1,0:T(8,128)(2,1)S(1)}, bf16[256,1024]{1,0:T(8,128)(2,1)S(1)}, u32[]{:S(2)}, u32[]{:S(2)}) collective-permute-start(bf16[256,1024]{1,0:T(8,128)(2,1)S(1)} %pad_maximum_fusion.1.refs_20_), channel_id=1, source_target_pairs={{0,1},{1,0},{2,3},{3,2},{4,5},{5,4},{6,7},{7,6},{8,9},{9,8},{10,11... | collective-permute-start | bytes 1572872 | tf_op jit(solution)/shard_map/ppermute | solution.py:207
  2.6 17.3 %collective-permute-start.5 = (bf16[256,1024]{1,0:T(8,128)(2,1)S(1)}, bf16[256,1024]{1,0:T(8,128)(2,1)S(1)}, u32[]{:S(2)}, u32[]{:S(2)}) collective-permute-start(bf16[256,1024]{1,0:T(8,128)(2,1)S(1)} %pad_maximum_fusion.1.refs_20_), channel_id=1, source_target_pairs={{4,0},{6,2},{8,4},{10,6},{12,8},{14,10},{5,1},{7,3},{9,5},{11,7},{... | collective-permute-start | bytes 1572872 | tf_op jit(solution)/shard_map/ppermute | solution.py:198
  4.5 15.5 %collective-permute-start.7 = (bf16[256,1024]{1,0:T(8,128)(2,1)S(1)}, bf16[256,1024]{1,0:T(8,128)(2,1)S(1)}, u32[]{:S(2)}, u32[]{:S(2)}) collective-permute-start(bf16[256,1024]{1,0:T(8,128)(2,1)S(1)} %pad_maximum_fusion.1.refs_20_), channel_id=1, source_target_pairs={{0,4},{2,6},{4,8},{6,10},{8,12},{10,14},{1,5},{3,7},{5,9},{7,11},{... | collective-permute-start | bytes 1572872 | tf_op jit(solution)/shard_map/ppermute | solution.py:201
  14.0 16.9 %collective-permute-start.4 = (bf16[256,1024]{1,0:T(8,128)(2,1)}, bf16[256,1024]{1,0:T(8,128)(2,1)S(1)}, u32[]{:S(2)}, u32[]{:S(2)}) collective-permute-start(bf16[256,1024]{1,0:T(8,128)(2,1)} %collective-permute-done.1.refs_21_), channel_id=1, source_target_pairs={{4,0},{6,2},{8,4},{10,6},{12,8},{14,10},{5,1},{7,3},{9,5},{11,7},{... | collective-permute-start | bytes 1572872 | tf_op jit(solution)/shard_map/ppermute | solution.py:198
  16.4 4.8 %copy-start.7 = (bf16[256,1024]{1,0:T(8,128)(2,1)}, bf16[256,1024]{1,0:T(8,128)(2,1)S(1)}, u32[]{:S(2)}) copy-start(bf16[256,1024]{1,0:T(8,128)(2,1)S(1)} %collective-permute-done.2.refs_22_) | copy-start | bytes 1572868
  16.4 16.3 %collective-permute-start.6 = (bf16[256,1024]{1,0:T(8,128)(2,1)}, bf16[256,1024]{1,0:T(8,128)(2,1)}, u32[]{:S(2)}, u32[]{:S(2)}) collective-permute-start(bf16[256,1024]{1,0:T(8,128)(2,1)} %collective-permute-done.1.refs_21_), channel_id=1, source_target_pairs={{0,4},{2,6},{4,8},{6,10},{8,12},{10,14},{1,5},{3,7},{5,9},{7,11},{... | collective-permute-start | bytes 1572872 | tf_op jit(solution)/shard_map/ppermute | solution.py:201
  19.9 20.1 %copy-start.4 = (bf16[256,1024]{1,0:T(8,128)(2,1)}, bf16[256,1024]{1,0:T(8,128)(2,1)S(1)}, u32[]{:S(2)}) copy-start(bf16[256,1024]{1,0:T(8,128)(2,1)S(1)} %collective-permute-done.5.refs_29_) | copy-start | bytes 1572868
  20.0 20.0 %copy-start.5 = (bf16[256,1024]{1,0:T(8,128)(2,1)}, bf16[256,1024]{1,0:T(8,128)(2,1)S(1)}, u32[]{:S(2)}) copy-start(bf16[256,1024]{1,0:T(8,128)(2,1)S(1)} %collective-permute-done.7.refs_28_) | copy-start | bytes 1572868
  21.2 22.1 %collective-permute-start.11 = (bf16[256,1024]{1,0:T(8,128)(2,1)}, bf16[256,1024]{1,0:T(8,128)(2,1)S(1)}, u32[]{:S(2)}, u32[]{:S(2)}) collective-permute-start(bf16[256,1024]{1,0:T(8,128)(2,1)} %get-tuple-element.28), channel_id=1, source_target_pairs={{4,0},{6,2},{8,4},{10,6},{12,8},{14,10},{5,1},{7,3},{9,5},{11,7},{... | collective-permute-start | bytes 1572872 | tf_op jit(solution)/shard_map/ppermute | solution.py:198
  24.2 15.0 %collective-permute-start.3 = (bf16[256,1024]{1,0:T(8,128)(2,1)}, bf16[256,1024]{1,0:T(8,128)(2,1)S(1)}, u32[]{:S(2)}, u32[]{:S(2)}) collective-permute-start(bf16[256,1024]{1,0:T(8,128)(2,1)} %collective-permute-done.1.refs_21_), channel_id=1, source_target_pairs={{0,1},{1,0},{2,3},{3,2},{4,5},{5,4},{6,7},{7,6},{8,9},{9,8},{10,11... | collective-permute-start | bytes 1572872 | tf_op jit(solution)/shard_map/ppermute | solution.py:207
  30.9 18.9 %copy-start.11 = (bf16[256,1024]{1,0:T(8,128)(2,1)}, bf16[256,1024]{1,0:T(8,128)(2,1)S(1)}, u32[]{:S(2)}) copy-start(bf16[256,1024]{1,0:T(8,128)(2,1)S(1)} %collective-permute-done.4) | copy-start | bytes 1572868
  30.9 10.1 %collective-permute-start.17 = (f32[32,1152]{1,0:T(8,128)}, f32[32,1152]{1,0:T(8,128)S(1)}, u32[]{:S(2)}, u32[]{:S(2)}) collective-permute-start(f32[32,1152]{1,0:T(8,128)} %pad_maximum_fusion.3), channel_id=1, source_target_pairs={{0,1},{1,0},{2,3},{3,2},{4,5},{5,4},{6,7},{7,6},{8,9},{9,8},{10,11... | collective-permute-start | bytes 442376 | tf_op jit(solution)/shard_map/ppermute | solution.py:207
  32.7 15.2 %collective-permute-start.12 = (bf16[256,1024]{1,0:T(8,128)(2,1)}, bf16[256,1024]{1,0:T(8,128)(2,1)S(1)}, u32[]{:S(2)}, u32[]{:S(2)}) collective-permute-start(bf16[256,1024]{1,0:T(8,128)(2,1)} %get-tuple-element.27), channel_id=1, source_target_pairs={{0,4},{2,6},{4,8},{6,10},{8,12},{10,14},{1,5},{3,7},{5,9},{7,11},{... | collective-permute-start | bytes 1572872 | tf_op jit(solution)/shard_map/ppermute | solution.py:201
  40.0 23.5 %collective-permute-start.8 = (bf16[512,1024]{1,0:T(8,128)(2,1)}, bf16[512,1024]{1,0:T(8,128)(2,1)S(1)}, u32[]{:S(2)}, u32[]{:S(2)}) collective-permute-start(bf16[512,1024]{1,0:T(8,128)(2,1)} %after.3.refs_24_), channel_id=1, source_target_pairs={{0,1},{1,0},{2,3},{3,2},{4,5},{5,4},{6,7},{7,6},{8,9},{9,8},{10,11... | collective-permute-start | bytes 3145736 | tf_op jit(solution)/shard_map/ppermute | solution.py:207
  41.0 16.7 %collective-permute-start.10 = (bf16[256,1024]{1,0:T(8,128)(2,1)S(1)}, bf16[256,1024]{1,0:T(8,128)(2,1)S(1)}, u32[]{:S(2)}, u32[]{:S(2)}) collective-permute-start(bf16[256,1024]{1,0:T(8,128)(2,1)S(1)} %collective-permute-done.4), channel_id=1, source_target_pairs={{4,0},{6,2},{8,4},{10,6},{5,1},{7,3},{9,5},{11,7},{20,16},{22,18},... | collective-permute-start | bytes 1572872 | tf_op jit(solution)/shard_map/ppermute | solution.py:198
  43.4 21.3 %copy-start.2 = (bf16[256,1024]{1,0:T(8,128)(2,1)}, bf16[256,1024]{1,0:T(8,128)(2,1)S(1)}, u32[]{:S(2)}) copy-start(bf16[256,1024]{1,0:T(8,128)(2,1)S(1)} %collective-permute-done.11.refs_27_.refs_11_) | copy-start | bytes 1572868
  43.4 16.2 %collective-permute-start.9 = (bf16[256,1024]{1,0:T(8,128)(2,1)}, bf16[256,1024]{1,0:T(8,128)(2,1)S(1)}, u32[]{:S(2)}, u32[]{:S(2)}) collective-permute-start(bf16[256,1024]{1,0:T(8,128)(2,1)} %collective-permute-done.6), channel_id=1, source_target_pairs={{4,8},{6,10},{8,12},{10,14},{5,9},{7,11},{9,13},{11,15},{20,24},{2... | collective-permute-start | bytes 1572872 | tf_op jit(solution)/shard_map/ppermute | solution.py:201
  47.9 16.8 %copy-start.3 = (bf16[256,1024]{1,0:T(8,128)(2,1)}, bf16[256,1024]{1,0:T(8,128)(2,1)S(1)}, u32[]{:S(2)}) copy-start(bf16[256,1024]{1,0:T(8,128)(2,1)S(1)} %collective-permute-done.12.refs_30_.refs_12_) | copy-start | bytes 1572868
  47.9 36.0 %collective-permute-start.14 = (bf16[256,1024]{1,0:T(8,128)(2,1)S(1)}, bf16[256,1024]{1,0:T(8,128)(2,1)S(1)}, u32[]{:S(2)}, u32[]{:S(2)}) collective-permute-start(bf16[256,1024]{1,0:T(8,128)(2,1)S(1)} %collective-permute-done.11.refs_27_.refs_11_), channel_id=1, source_target_pairs={{4,0},{6,2},{8,4},{10,6},{5,1},{7,3},{9,5},{11,7},{20,16},{22,18},... | collective-permute-start | bytes 1572872 | tf_op jit(solution)/shard_map/ppermute | solution.py:198
  57.7 5.4 %copy-start.12 = (bf16[256,1024]{1,0:T(8,128)(2,1)}, bf16[256,1024]{1,0:T(8,128)(2,1)S(1)}, u32[]{:S(2)}) copy-start(bf16[256,1024]{1,0:T(8,128)(2,1)S(1)} %collective-permute-done.10) | copy-start | bytes 1572868
  57.7 26.2 %collective-permute-start.15 = (bf16[256,1024]{1,0:T(8,128)(2,1)S(1)}, bf16[256,1024]{1,0:T(8,128)(2,1)S(1)}, u32[]{:S(2)}, u32[]{:S(2)}) collective-permute-start(bf16[256,1024]{1,0:T(8,128)(2,1)S(1)} %collective-permute-done.12.refs_30_.refs_12_), channel_id=1, source_target_pairs={{4,8},{6,10},{8,12},{10,14},{5,9},{7,11},{9,13},{11,15},{20,24},{2... | collective-permute-start | bytes 1572872 | tf_op jit(solution)/shard_map/ppermute | solution.py:201
  59.6 3.8 %copy-start.13 = (bf16[256,1024]{1,0:T(8,128)(2,1)}, bf16[256,1024]{1,0:T(8,128)(2,1)S(1)}, u32[]{:S(2)}) copy-start(bf16[256,1024]{1,0:T(8,128)(2,1)S(1)} %collective-permute-done.9) | copy-start | bytes 1572868
  61.0 23.0 %collective-permute-start.13 = (bf16[256,1024]{1,0:T(8,128)(2,1)S(1)}, bf16[256,1024]{1,0:T(8,128)(2,1)}, u32[]{:S(2)}, u32[]{:S(2)}) collective-permute-start(bf16[256,1024]{1,0:T(8,128)(2,1)S(1)} %get-tuple-element.25), channel_id=1, source_target_pairs={{4,0},{6,2},{8,12},{10,14},{5,1},{7,3},{9,13},{11,15},{20,16},{22,... | collective-permute-start | bytes 1572872 | tf_op jit(solution)/shard_map/ppermute | solution.py:204
  63.3 1.4 copy-start.6
  63.5 1.2 copy-start.14
  63.5 34.8 %collective-permute-start.16 = (bf16[512,1024]{1,0:T(8,128)(2,1)S(1)}, bf16[512,1024]{1,0:T(8,128)(2,1)}, u32[]{:S(2)}, u32[]{:S(2)}) collective-permute-start(bf16[512,1024]{1,0:T(8,128)(2,1)S(1)} %pad_maximum_fusion.refs_26_), channel_id=1, source_target_pairs={{0,1},{1,0},{2,3},{3,2},{4,5},{5,4},{6,7},{7,6},{8,9},{9,8},{10,11... | collective-permute-start | bytes 3145736 | tf_op jit(solution)/shard_map/ppermute | solution.py:207
  64.7 25.6 %collective-permute-start.18 = (bf16[32,512]{1,0:T(8,128)(2,1)S(1)}, bf16[32,512]{1,0:T(8,128)(2,1)S(1)}, u32[]{:S(2)}, u32[]{:S(2)}) collective-permute-start(bf16[32,512]{1,0:T(8,128)(2,1)S(1)} %constant_dynamic-slice_fusion), channel_id=1, source_target_pairs={{0,2},{2,0},{4,6},{6,4},{8,10},{10,8},{12,14},{14,12},{1,3},{3,1},... | collective-permute-start | bytes 98312 | tf_op jit(solution)/shard_map/ppermute | solution.py:193
  84.0 1.0 copy-start.1
  86.2 12.1 %copy-start.10 = (bf16[256,1024]{1,0:T(8,128)(2,1)}, bf16[256,1024]{1,0:T(8,128)(2,1)S(1)}, u32[]{:S(2)}) copy-start(bf16[256,1024]{1,0:T(8,128)(2,1)S(1)} %select_select_fusion.refs_9_) | copy-start | bytes 1572868
  86.2 26.0 %collective-permute-start.21 = (bf16[256,1024]{1,0:T(8,128)(2,1)S(1)}, bf16[256,1024]{1,0:T(8,128)(2,1)S(1)}, u32[]{:S(2)}, u32[]{:S(2)}) collective-permute-start(bf16[256,1024]{1,0:T(8,128)(2,1)S(1)} %select_select_fusion.refs_9_), channel_id=1, source_target_pairs={{0,1},{1,0},{2,3},{3,2},{4,5},{5,4},{6,7},{7,6},{8,9},{9,8},{10,11... | collective-permute-start | bytes 1572872 | tf_op jit(solution)/shard_map/ppermute | solution.py:207
  88.5 23.8 %collective-permute-start.22 = (bf16[256,1024]{1,0:T(8,128)(2,1)S(1)}, bf16[256,1024]{1,0:T(8,128)(2,1)S(1)}, u32[]{:S(2)}, u32[]{:S(2)}) collective-permute-start(bf16[256,1024]{1,0:T(8,128)(2,1)S(1)} %broadcast_select_fusion.2), channel_id=1, source_target_pairs={{4,0},{6,2},{8,12},{10,14},{5,1},{7,3},{9,13},{11,15},{20,16},{22,... | collective-permute-start | bytes 1572872 | tf_op jit(solution)/shard_map/ppermute | solution.py:204
  91.0 20.5 %collective-permute-start.20 = (bf16[2,32,512]{2,1,0:T(8,128)(2,1)}, bf16[2,32,512]{2,1,0:T(8,128)(2,1)S(1)}, u32[]{:S(2)}, u32[]{:S(2)}) collective-permute-start(bf16[2,32,512]{2,1,0:T(8,128)(2,1)} %after.5), channel_id=1, source_target_pairs={{4,0},{6,2},{0,4},{2,6},{5,8},{7,10},{1,12},{3,14},{12,1},{14,3},{... | collective-permute-start | bytes 196616 | tf_op jit(solution)/shard_map/ppermute | solution.py:541
  95.7 15.8 %collective-permute-start.19 = (bf16[2,32,512]{2,1,0:T(8,128)(2,1)}, bf16[2,32,512]{2,1,0:T(8,128)(2,1)S(1)}, u32[]{:S(2)}, u32[]{:S(2)}) collective-permute-start(bf16[2,32,512]{2,1,0:T(8,128)(2,1)} %after.5), channel_id=1, source_target_pairs={{0,0},{2,2},{4,4},{6,6},{1,8},{3,10},{5,12},{7,14},{8,1},{10,3},{1... | collective-permute-start | bytes 196616 | tf_op jit(solution)/shard_map/ppermute | solution.py:541
  112.3 1.0 copy-start.16
  124.1 5.0 %collective-permute-start.23 = (f32[32,640]{1,0:T(8,128)}, f32[32,640]{1,0:T(8,128)S(1)}, u32[]{:S(2)}, u32[]{:S(2)}) collective-permute-start(f32[32,640]{1,0:T(8,128)} %get-tuple-element.22), channel_id=1, source_target_pairs={{0,4},{2,6},{4,8},{6,10},{8,12},{10,14},{12,0},{14,2},{1,5},{3,7},... | collective-permute-start | bytes 245768 | tf_op jit(solution)/shard_map/ppermute | solution.py:600
  124.2 8.5 %collective-permute-start.24 = (f32[32,640]{1,0:T(8,128)}, f32[32,640]{1,0:T(8,128)S(1)}, u32[]{:S(2)}, u32[]{:S(2)}) collective-permute-start(f32[32,640]{1,0:T(8,128)} %get-tuple-element.23), channel_id=1, source_target_pairs={{0,8},{2,10},{4,12},{6,14},{8,0},{10,2},{12,4},{14,6},{1,9},{3,11}... | collective-permute-start | bytes 245768 | tf_op jit(solution)/shard_map/ppermute | solution.py:600
  128.0 6.7 %collective-permute-start.25 = (f32[32,640]{1,0:T(8,128)}, f32[32,640]{1,0:T(8,128)S(1)}, u32[]{:S(2)}, u32[]{:S(2)}) collective-permute-start(f32[32,640]{1,0:T(8,128)} %get-tuple-element.24), channel_id=1, source_target_pairs={{0,12},{2,14},{4,0},{6,2},{8,4},{10,6},{12,8},{14,10},{1,13},{3,15... | collective-permute-start | bytes 245768 | tf_op jit(solution)/shard_map/ppermute | solution.py:600
  129.1 5.6 %copy-start.18 = (f32[32,640]{1,0:T(8,128)}, f32[32,640]{1,0:T(8,128)S(1)}, u32[]{:S(2)}) copy-start(f32[32,640]{1,0:T(8,128)S(1)} %collective-permute-done.23.refs_1_) | copy-start | bytes 245764
  132.7 2.0 %copy-start.19 = (f32[32,640]{1,0:T(8,128)}, f32[32,640]{1,0:T(8,128)S(1)}, u32[]{:S(2)}) copy-start(f32[32,640]{1,0:T(8,128)S(1)} %collective-permute-done.24.refs_2_) | copy-start | bytes 245764
  137.4 7.8 %collective-permute-start.26 = (bf16[32,512]{1,0:T(8,128)(2,1)}, bf16[32,512]{1,0:T(8,128)(2,1)S(1)}, u32[]{:S(2)}, u32[]{:S(2)}) collective-permute-start(bf16[32,512]{1,0:T(8,128)(2,1)} %merge.1), channel_id=1, source_target_pairs={{0,0},{1,8},{2,1},{3,9},{4,2},{5,10},{6,3},{7,11},{8,4},{9,12},{10... | collective-permute-start | bytes 98312 | tf_op jit(solution)/shard_map/ppermute | solution.py:611
  139.3 6.7 %collective-permute-start.27 = (bf16[32,512]{1,0:T(8,128)(2,1)}, bf16[32,512]{1,0:T(8,128)(2,1)S(1)}, u32[]{:S(2)}, u32[]{:S(2)}) collective-permute-start(bf16[32,512]{1,0:T(8,128)(2,1)} %merge.1), channel_id=1, source_target_pairs={{0,1},{1,9},{2,0},{3,8},{4,3},{5,11},{6,2},{7,10},{8,5},{9,13},{10... | collective-permute-start | bytes 98312 | tf_op jit(solution)/shard_map/ppermute | solution.py:611
  149.1 5.0 %collective-permute-start.28 = (bf16[32,2048]{1,0:T(8,128)(2,1)S(1)}, bf16[32,2048]{1,0:T(8,128)(2,1)S(1)}, u32[]{:S(2)}, u32[]{:S(2)}) collective-permute-start(bf16[32,2048]{1,0:T(8,128)(2,1)S(1)} %convolution_convert_fusion), channel_id=1, source_target_pairs={{0,16},{16,0},{1,17},{17,1},{2,18},{18,2},{3,19},{19,3},{4,20},{20... | collective-permute-start | bytes 393224 | tf_op jit(solution)/shard_map/ppermute | solution.py:616
  (4 other events, 3.0 us)

commit v3 on v2

--- a/solution.py
+++ b/solution.py
@@ -177,6 +177,7 @@
         out_specs=[anywhere] * count,
         out_shape=[jax.ShapeDtypeStruct(value.shape, value.dtype) for value in values],
         input_output_aliases={k: k for k in range(count)},
+        compiler_params=pltpu.CompilerParams(vmem_limit_bytes=2**20),
         name="after",
     )(*values, *done)
 
@@ -378,7 +379,7 @@
     halves, refs = (refs[:count], refs[count : 2 * count]), refs[2 * count :]
     before, queries, live, refs = refs[0], refs[1], refs[2], refs[3:]
     sources, refs = refs[:amount], refs[amount:]
-    outs, (weights, sems) = refs[:CHIPS], refs[CHIPS:]
+    outs, (weights, sems) = refs[:-2], refs[-2:]
     step = pl.program_id(0)
 
     @pl.when(step == 0)
@@ -432,7 +433,7 @@
             out[...] = result
 
 
-def attend_last(info, pieces, own_rows, other_rows, before, queries, live):
+def attend_last(info, pieces, own_rows, other_rows, before, queries, live, first, amount):
     questions, rows, width = own_rows.shape
     columns = pieces[0][0][0][0].shape[1]
     answers = queries.shape[1]
@@ -441,7 +442,7 @@
     wide = columns // 2 + 128
 
     def question(i, info):
-        return lax.rem(i + info[0], questions)
+        return lax.rem(i + first + info[0], questions)
 
     def turned(i, info):
         wanted = question(i, info)
@@ -455,12 +456,12 @@
     ]
     whole = lambda *shape: pl.BlockSpec((1,) + shape, lambda i, info: (question(i, info), 0, 0))
     anywhere = pl.BlockSpec(memory_space=pl.ANY)
-    flops = 4 * questions * rows * count * PIECE * columns + 16 * questions * rows * answers * columns
+    flops = 4 * amount * rows * count * PIECE * columns + 16 * amount * rows * answers * columns
     return pl.pallas_call(
         functools.partial(attend_kernel, wanted, len(arrays)),
         grid_spec=pltpu.PrefetchScalarGridSpec(
             num_scalar_prefetch=1,
-            grid=(questions,),
+            grid=(amount,),
             in_specs=blocks
             + blocks
             + [
@@ -469,18 +470,18 @@
                 whole(1, 2 * rows),
             ]
             + [anywhere] * len(arrays),
-            out_specs=[pl.BlockSpec((answers, wide), lambda i, info: (0, 0))] * CHIPS,
+            out_specs=[pl.BlockSpec((answers, wide), lambda i, info: (0, 0))] * amount,
             scratch_shapes=[
                 pltpu.VMEM((count * PIECE, columns), jnp.bfloat16),
                 pltpu.SemaphoreType.DMA((count,)),
             ],
         ),
-        out_shape=[jax.ShapeDtypeStruct((answers, wide), jnp.float32)] * CHIPS,
+        out_shape=[jax.ShapeDtypeStruct((answers, wide), jnp.float32)] * amount,
         compiler_params=pltpu.CompilerParams(vmem_limit_bytes=VMEM_LIMIT),
         cost_estimate=pl.CostEstimate(
             flops=flops,
-            bytes_accessed=questions * rows * (8 * columns + 4 * count * PIECE),
-            transcendentals=questions * rows * answers * columns // HD,
+            bytes_accessed=amount * rows * (8 * columns + 4 * count * PIECE),
+            transcendentals=amount * rows * answers * columns // HD,
         ),
         name="attend",
     )(info, *([own_rows] * count), *([other_rows] * count), before, queries, live, *arrays)
@@ -516,6 +517,7 @@
         merge_kernel,
         out_shape=jax.ShapeDtypeStruct((answers, wide - 128), jnp.bfloat16),
         cost_estimate=pl.CostEstimate(flops=8 * answers * wide, bytes_accessed=16 * answers * wide, transcendentals=512 * answers),
+        compiler_params=pltpu.CompilerParams(vmem_limit_bytes=4 * 2**20),
         name="merge",
     )(*parts)
 
@@ -593,11 +595,16 @@
     )
     live = jnp.repeat(live, BLOCK, axis=1)[:, None, :]
 
-    parts = attend_last(info(last), last, passage_states, other_rows, sums, queries, live)
-    arrived = [parts[0]]
-    for step in range(1, CHIPS):
+    def partials(first, amount):
+        return attend_last(
+            info(last), last, passage_states, other_rows, sums, queries, live, first, amount
+        )
+
+    arrived = []
+    for step, part in enumerate(partials(1, CHIPS - 1), 1):
         turn = [(2 * k + core, 2 * ((k + step) % CHIPS) + core) for k in range(CHIPS) for core in range(2)]
-        arrived.append(lax.ppermute(parts[step], "pb", turn))
+        arrived.append(lax.ppermute(part, "pb", turn))
+    arrived += partials(0, 1)
     attention = merge(arrived)
 
     received = []

time: 156 us -> 151 us (0.968)
  other arithmetic: 11.5 us -> 6.89 us
  Pallas kernels: 45.3 us -> 47.9 us
  starting transfers between devices: 52.1 us -> 49.6 us
  waiting for transfers between devices: 33.2 us -> 31.2 us
    ppermute x3, waiting for transfers between devices: 6.71 us -> 1.36 us  [gathered_shards(): arrived.append(lax.ppermute(part, 'pb', turn))]
    pallas_call x1 -> x2, Pallas kernels: 10.9 us -> 15.1 us  [attend_last(): pl.pallas_call(functools.partial(attend_kernel, wanted, len(arrays)), gri...]
    ppermute x6, waiting for transfers between devices: 0.72 us -> 4.1 us  [across(): return lax.ppermute(value, 'fsdp', [(0, 1), (1, 0)])]
    pallas_call x1, Pallas kernels: 2.07 us -> 0.44 us  [merge(): pl.pallas_call(merge_kernel, out_shape=jax.ShapeDtypeStruct((answers, wid...]
    unnamed x46 -> x47, local copies, waits for them, and re-layouts: 2.66 us -> 3.88 us
  transfers between devices with their start and end apart: 29 -> 29, of which waited for: 14 -> 10; matrix products, arithmetic and copies ran while one was open for 11% -> 8% of each run, Pallas kernels for 21% -> 25%
where the time goes in v3:
time: 151 us; the launch traced here: 150 us
  starting transfers between devices  49.6 us (33%)
  Pallas kernels  47.9 us (32%)
  waiting for transfers between devices  31.2 us (21%)
  local copies, waits for them, and re-layouts  7.39 us (5%)
  other arithmetic  6.89 us (5%)
  matrix products  6.02 us (4%)
    pallas_call x2, Pallas kernels, project_pieces(): pl.pallas_call(functools.partial(project_kernel, wanted, len(arrays), car...  32.3 us
    ppermute x5, starting transfers between devices, right(): return lax.ppermute(value, 'pb', line(1, sources))  16.4 us
    pallas_call x2, Pallas kernels, attend_last(): pl.pallas_call(functools.partial(attend_kernel, wanted, len(arrays)), gri...  15.1 us
    ppermute x5, waiting for transfers between devices, left(): return lax.ppermute(value, 'pb', line(-1, sources))  14 us
    ppermute x5, starting transfers between devices, left(): return lax.ppermute(value, 'pb', line(-1, sources))  11 us
    ppermute x2, starting transfers between devices, spread_queries(): spread.append(lax.ppermute(pair, ('pb', 'fsdp'), sends))  6.04 us
    ppermute x2, waiting for transfers between devices, gathered_shards(): received.append(lax.ppermute(attention, ('pb', 'fsdp'), sends))  5.69 us
    ppermute x6, starting transfers between devices, across(): return lax.ppermute(value, 'fsdp', [(0, 1), (1, 0)])  4.39 us
  transfers between devices with their start and end apart: 29, of which 10 were waited for; matrix products, arithmetic and copies ran while one was open for 8% of the time, Pallas kernels for 25%

profile of v3, /device:TPU:10, one launch (start us, length us, event | category | flops | bytes accessed | tf_op | source)
XLA Modules:
  0.0 149.6 jit_solution(7116781300299672516)
XLA Ops:
  0.0 1.3 constant_dynamic-slice_fusion.1
  2.6 1.9 %collective-permute-start.5 = (bf16[256,1024]{1,0:T(8,128)(2,1)S(1)}, bf16[256,1024]{1,0:T(8,128)(2,1)S(1)}, u32[]{:S(2)}, u32[]{:S(2)}) collective-permute-start(bf16[256,1024]{1,0:T(8,128)(2,1)S(1)} %pad_maximum_fusion.1.refs_20_), channel_id=1, source_target_pairs={{4,0},{6,2},{8,4},{10,6},{12,8},{14,10},{5,1},{7,3},{9,5},{11,7},{... | collective-permute-start | bytes 1572872 | tf_op jit(solution)/shard_map/ppermute | solution.py:199
  4.5 3.9 %collective-permute-start.7 = (bf16[256,1024]{1,0:T(8,128)(2,1)S(1)}, bf16[256,1024]{1,0:T(8,128)(2,1)S(1)}, u32[]{:S(2)}, u32[]{:S(2)}) collective-permute-start(bf16[256,1024]{1,0:T(8,128)(2,1)S(1)} %pad_maximum_fusion.1.refs_20_), channel_id=1, source_target_pairs={{0,4},{2,6},{4,8},{6,10},{8,12},{10,14},{1,5},{3,7},{5,9},{7,11},{... | collective-permute-start | bytes 1572872 | tf_op jit(solution)/shard_map/ppermute | solution.py:202
  8.7 3.0 %fusion.3 = f32[32,1024]{1,0:T(8,128)S(1)} fusion(bf16[2048,1024]{1,0:T(8,128)(2,1)} %param.10, bf16[1,32,2048]{2,1,0:T(8,128)(2,1)S(1)} %copy-done.20, f32[2048]{0:T(1024)S(1)} %convert_element_type.29), kind=kOutput, calls=%fused_computation.19 | convolution fusion | flops 134414336 | bytes 4464640 | tf_op jit(solution)/shard_map/dot_general | solution.py:529
  11.7 2.4 %collective-permute-done.1.refs_21_ = bf16[256,1024]{1,0:T(8,128)(2,1)} collective-permute-done((bf16[256,1024]{1,0:T(8,128)(2,1)S(1)}, bf16[256,1024]{1,0:T(8,128)(2,1)}, u32[]{:S(2)}, u32[]{:S(2)}) %collective-permute-start.1) | collective-permute-done | bytes 524320 | tf_op jit(solution)/shard_map/ppermute | solution.py:194
  14.0 2.3 %collective-permute-start.4 = (bf16[256,1024]{1,0:T(8,128)(2,1)}, bf16[256,1024]{1,0:T(8,128)(2,1)}, u32[]{:S(2)}, u32[]{:S(2)}) collective-permute-start(bf16[256,1024]{1,0:T(8,128)(2,1)} %collective-permute-done.1.refs_21_), channel_id=1, source_target_pairs={{4,0},{6,2},{8,4},{10,6},{12,8},{14,10},{5,1},{7,3},{9,5},{11,7},{... | collective-permute-start | bytes 1572872 | tf_op jit(solution)/shard_map/ppermute | solution.py:199
  16.4 3.5 %collective-permute-start.6 = (bf16[256,1024]{1,0:T(8,128)(2,1)}, bf16[256,1024]{1,0:T(8,128)(2,1)}, u32[]{:S(2)}, u32[]{:S(2)}) collective-permute-start(bf16[256,1024]{1,0:T(8,128)(2,1)} %collective-permute-done.1.refs_21_), channel_id=1, source_target_pairs={{0,4},{2,6},{4,8},{6,10},{8,12},{10,14},{1,5},{3,7},{5,9},{7,11},{... | collective-permute-start | bytes 1572872 | tf_op jit(solution)/shard_map/ppermute | solution.py:202
  20.0 1.2 broadcast_select_fusion
  21.3 3.0 %collective-permute-start.11 = (bf16[256,1024]{1,0:T(8,128)(2,1)}, bf16[256,1024]{1,0:T(8,128)(2,1)S(1)}, u32[]{:S(2)}, u32[]{:S(2)}) collective-permute-start(bf16[256,1024]{1,0:T(8,128)(2,1)} %get-tuple-element.26), channel_id=1, source_target_pairs={{4,0},{6,2},{8,4},{10,6},{12,8},{14,10},{5,1},{7,3},{9,5},{11,7},{... | collective-permute-start | bytes 1572872 | tf_op jit(solution)/shard_map/ppermute | solution.py:199
  24.2 0.9 collective-permute-start.3
  25.2 0.7 pad_maximum_fusion.3
  25.9 5.1 %collective-permute-done.4 = bf16[256,1024]{1,0:T(8,128)(2,1)} collective-permute-done((bf16[256,1024]{1,0:T(8,128)(2,1)}, bf16[256,1024]{1,0:T(8,128)(2,1)}, u32[]{:S(2)}, u32[]{:S(2)}) %collective-permute-start.4) | collective-permute-done | bytes 524320 | tf_op jit(solution)/shard_map/ppermute | solution.py:199
  31.6 0.6 concatenate.38.info
  32.2 0.6 concatenate.39.info
  32.9 3.5 %collective-permute-start.12 = (bf16[256,1024]{1,0:T(8,128)(2,1)}, bf16[256,1024]{1,0:T(8,128)(2,1)S(1)}, u32[]{:S(2)}, u32[]{:S(2)}) collective-permute-start(bf16[256,1024]{1,0:T(8,128)(2,1)} %get-tuple-element.25), channel_id=1, source_target_pairs={{0,4},{2,6},{4,8},{6,10},{8,12},{10,14},{1,5},{3,7},{5,9},{7,11},{... | collective-permute-start | bytes 1572872 | tf_op jit(solution)/shard_map/ppermute | solution.py:202
  36.3 1.6 %maximum_select_fusion.refs_0_ = bf16[512,1024]{1,0:T(8,128)(2,1)S(1)} fusion(bf16[256,1024]{1,0:T(8,128)(2,1)S(1)} %collective-permute-done.5.refs_29_, bf16[256,1024]{1,0:T(8,128)(2,1)} %collective-permute-done.4, bf16[256,1024]{1,0:T(8,128)(2,1)S(1)} %collective-permute-done.7.refs_28_, bf16[256,1024]{1,0:T(8,128)(2,1)} %collective-permute-done.6, pred[]{:T(512)S(6)} %lt.34), kind=kLoop, calls=%fused_computation.1 | loop fusion | flops 4718592 | bytes 3145729 | tf_op jit(solution)/shard_map/jit(_where)/select_n | solution.py:223
  38.0 1.3 collective-permute-done.3.refs_1_.refs_23_
  39.7 2.8 %collective-permute-done.17 = f32[32,1152]{1,0:T(8,128)S(1)} collective-permute-done((f32[32,1152]{1,0:T(8,128)}, f32[32,1152]{1,0:T(8,128)S(1)}, u32[]{:S(2)}, u32[]{:S(2)}) %collective-permute-start.17) | collective-permute-done | bytes 147488 | tf_op jit(solution)/shard_map/ppermute | solution.py:208
  42.5 1.9 %collective-permute-start.10 = (bf16[256,1024]{1,0:T(8,128)(2,1)}, bf16[256,1024]{1,0:T(8,128)(2,1)S(1)}, u32[]{:S(2)}, u32[]{:S(2)}) collective-permute-start(bf16[256,1024]{1,0:T(8,128)(2,1)} %collective-permute-done.4), channel_id=1, source_target_pairs={{4,0},{6,2},{8,4},{10,6},{5,1},{7,3},{9,5},{11,7},{20,16},{22,18},... | collective-permute-start | bytes 1572872 | tf_op jit(solution)/shard_map/ppermute | solution.py:199
  44.4 4.0 %collective-permute-start.9 = (bf16[256,1024]{1,0:T(8,128)(2,1)}, bf16[256,1024]{1,0:T(8,128)(2,1)S(1)}, u32[]{:S(2)}, u32[]{:S(2)}) collective-permute-start(bf16[256,1024]{1,0:T(8,128)(2,1)} %collective-permute-done.6), channel_id=1, source_target_pairs={{4,8},{6,10},{8,12},{10,14},{5,9},{7,11},{9,13},{11,15},{20,24},{2... | collective-permute-start | bytes 1572872 | tf_op jit(solution)/shard_map/ppermute | solution.py:202
  48.6 1.9 %collective-permute-start.14 = (bf16[256,1024]{1,0:T(8,128)(2,1)S(1)}, bf16[256,1024]{1,0:T(8,128)(2,1)S(1)}, u32[]{:S(2)}, u32[]{:S(2)}) collective-permute-start(bf16[256,1024]{1,0:T(8,128)(2,1)S(1)} %collective-permute-done.11.refs_27_.refs_11_), channel_id=1, source_target_pairs={{4,0},{6,2},{8,4},{10,6},{5,1},{7,3},{9,5},{11,7},{20,16},{22,18},... | collective-permute-start | bytes 1572872 | tf_op jit(solution)/shard_map/ppermute | solution.py:199
  50.5 8.9 %collective-permute-done.10 = bf16[256,1024]{1,0:T(8,128)(2,1)S(1)} collective-permute-done((bf16[256,1024]{1,0:T(8,128)(2,1)}, bf16[256,1024]{1,0:T(8,128)(2,1)S(1)}, u32[]{:S(2)}, u32[]{:S(2)}) %collective-permute-start.10) | collective-permute-done | bytes 524320 | tf_op jit(solution)/shard_map/ppermute | solution.py:199
  59.4 1.6 %collective-permute-start.15 = (bf16[256,1024]{1,0:T(8,128)(2,1)S(1)}, bf16[256,1024]{1,0:T(8,128)(2,1)S(1)}, u32[]{:S(2)}, u32[]{:S(2)}) collective-permute-start(bf16[256,1024]{1,0:T(8,128)(2,1)S(1)} %collective-permute-done.12.refs_30_.refs_12_), channel_id=1, source_target_pairs={{4,8},{6,10},{8,12},{10,14},{5,9},{7,11},{9,13},{11,15},{20,24},{2... | collective-permute-start | bytes 1572872 | tf_op jit(solution)/shard_map/ppermute | solution.py:202
  61.0 1.2 broadcast_select_fusion.3
  62.2 1.3 collective-permute-start.13
  63.8 1.0 copy-done.18
  65.0 19.1 %project.2 = (f32[4,512,1024]{2,1,0:T(8,128)}, f32[8,128]{1,0:T(8,128)}) custom-call(s32[11]{0:T(128)} %concatenate.39.info, bf16[4,256,4096]{2,1,0:T(8,128)(2,1)} %refs_1_.7, bf16[4,256,4096]{2,1,0:T(8,128)(2,1)} %refs_1_.7, bf16[4,256,4096]{2,1,0:T(8,128)(2,1)} %refs_1_.7, bf16[4,256,4096]{2,1,0:T(8,128)(2,1)} %refs_1_.7, bf16[4,256,4096]{2,1,0:T(8,128)(2,1)} %refs_1_.7, ...), custom_call_target="tpu_custom_call" | custom-call | flops 1000 | bytes 1000 | tf_op jit(solution)/shard_map/project/pallas_call | solution.py:353
  84.2 0.7 copy-done.5
  85.0 2.0 %collective-permute-start.21 = (bf16[256,1024]{1,0:T(8,128)(2,1)S(1)}, bf16[256,1024]{1,0:T(8,128)(2,1)S(1)}, u32[]{:S(2)}, u32[]{:S(2)}) collective-permute-start(bf16[256,1024]{1,0:T(8,128)(2,1)S(1)} %select_select_fusion.refs_9_), channel_id=1, source_target_pairs={{0,1},{1,0},{2,3},{3,2},{4,5},{5,4},{6,7},{7,6},{8,9},{9,8},{10,11... | collective-permute-start | bytes 1572872 | tf_op jit(solution)/shard_map/ppermute | solution.py:208
  87.0 1.3 collective-permute-start.22
  88.4 4.8 %collective-permute-start.19 = (bf16[2,32,512]{2,1,0:T(8,128)(2,1)S(1)}, bf16[2,32,512]{2,1,0:T(8,128)(2,1)S(1)}, u32[]{:S(2)}, u32[]{:S(2)}) collective-permute-start(bf16[2,32,512]{2,1,0:T(8,128)(2,1)S(1)} %after.5), channel_id=1, source_target_pairs={{0,0},{2,2},{4,4},{6,6},{1,8},{3,10},{5,12},{7,14},{8,1},{10,3},{1... | collective-permute-start | bytes 196616 | tf_op jit(solution)/shard_map/ppermute | solution.py:543
  93.2 0.7 pad_add_fusion.1.info
  93.9 1.3 collective-permute-start.20
  95.1 1.0 copy-done.17
  96.1 13.2 %project.3 = (f32[4,512,1024]{2,1,0:T(8,128)}, f32[8,128]{1,0:T(8,128)}) custom-call(s32[5]{0:T(128)} %concatenate.38.info, bf16[4,256,4096]{2,1,0:T(8,128)(2,1)} %refs_1_.7, bf16[4,256,4096]{2,1,0:T(8,128)(2,1)} %refs_1_.7, bf16[4,256,4096]{2,1,0:T(8,128)(2,1)} %refs_1_.7, bf16[4,256,4096]{2,1,0:T(8,128)(2,1)} %refs_1_.7, ...), custom_call_target="tpu_custom_call", output_to_operand_aliasing={{0}: (9, {})} | custom-call | flops 1000 | bytes 1000 | tf_op jit(solution)/shard_map/project/pallas_call | solution.py:353
  109.5 0.8 broadcast_in_dim.10
  110.4 9.4 %attend.2 = (f32[32,640]{1,0:T(8,128)}, f32[32,640]{1,0:T(8,128)}, f32[32,640]{1,0:T(8,128)}) custom-call(s32[3]{0:T(128)} %pad_add_fusion.1.info, bf16[4,256,4096]{2,1,0:T(8,128)(2,1)} %refs_1_.7, bf16[4,256,4096]{2,1,0:T(8,128)(2,1)} %refs_1_.7, ...), custom_call_target="tpu_custom_call" | custom-call | flops 2013265920 | bytes 7864320 | tf_op jit(solution)/shard_map/attend/pallas_call | solution.py:460
  119.9 3.8 %collective-permute-start.24 = (f32[32,640]{1,0:T(8,128)}, f32[32,640]{1,0:T(8,128)S(1)}, u32[]{:S(2)}, u32[]{:S(2)}) collective-permute-start(f32[32,640]{1,0:T(8,128)} %get-tuple-element.21), channel_id=1, source_target_pairs={{0,8},{2,10},{4,12},{6,14},{8,0},{10,2},{12,4},{14,6},{1,9},{3,11}... | collective-permute-start | bytes 245768 | tf_op jit(solution)/shard_map/ppermute | solution.py:606
  123.7 5.7 %attend.3.refs_3_ = f32[32,640]{1,0:T(8,128)} custom-call(s32[3]{0:T(128)} %pad_add_fusion.1.info, bf16[4,256,4096]{2,1,0:T(8,128)(2,1)} %refs_1_.7, bf16[4,256,4096]{2,1,0:T(8,128)(2,1)} %refs_1_.7, ...), custom_call_target="tpu_custom_call" | custom-call | flops 671088640 | bytes 2621440 | tf_op jit(solution)/shard_map/attend/pallas_call | solution.py:460
  129.4 1.4 collective-permute-done.25.refs_2_
  130.8 0.9 copy-done.4
  132.1 2.7 %collective-permute-start.26 = (bf16[32,512]{1,0:T(8,128)(2,1)S(1)}, bf16[32,512]{1,0:T(8,128)(2,1)S(1)}, u32[]{:S(2)}, u32[]{:S(2)}) collective-permute-start(bf16[32,512]{1,0:T(8,128)(2,1)S(1)} %merge.1), channel_id=1, source_target_pairs={{0,0},{1,8},{2,1},{3,9},{4,2},{5,10},{6,3},{7,11},{8,4},{9,12},{10... | collective-permute-start | bytes 98312 | tf_op jit(solution)/shard_map/ppermute | solution.py:618
  135.2 3.3 %collective-permute-done.26 = bf16[32,512]{1,0:T(8,128)(2,1)S(1)} collective-permute-done((bf16[32,512]{1,0:T(8,128)(2,1)S(1)}, bf16[32,512]{1,0:T(8,128)(2,1)S(1)}, u32[]{:S(2)}, u32[]{:S(2)}) %collective-permute-start.26) | collective-permute-done | bytes 32800 | tf_op jit(solution)/shard_map/ppermute | solution.py:618
  138.5 2.4 %collective-permute-done.27 = bf16[32,512]{1,0:T(8,128)(2,1)S(1)} collective-permute-done((bf16[32,512]{1,0:T(8,128)(2,1)S(1)}, bf16[32,512]{1,0:T(8,128)(2,1)S(1)}, u32[]{:S(2)}, u32[]{:S(2)}) %collective-permute-start.27) | collective-permute-done | bytes 32800 | tf_op jit(solution)/shard_map/ppermute | solution.py:618
  140.9 3.0 %convolution_convert_fusion = bf16[32,2048]{1,0:T(8,128)(2,1)S(1)} fusion(bf16[1024,2048]{1,0:T(8,128)(2,1)} %param.13, bf16[32,512]{1,0:T(8,128)(2,1)S(1)} %get-tuple-element.34, bf16[32,512]{1,0:T(8,128)(2,1)S(1)} %get-tuple-element.33), kind=kOutput, calls=%fused_computation | convolution fusion | flops 134414336 | bytes 4390912 | tf_op jit(solution)/shard_map/dot_general | solution.py:622
  143.9 1.6 %collective-permute-start.28 = (bf16[32,2048]{1,0:T(8,128)(2,1)S(1)}, bf16[32,2048]{1,0:T(8,128)(2,1)S(1)}, u32[]{:S(2)}, u32[]{:S(2)}) collective-permute-start(bf16[32,2048]{1,0:T(8,128)(2,1)S(1)} %convolution_convert_fusion), channel_id=1, source_target_pairs={{0,16},{16,0},{1,17},{17,1},{2,18},{18,2},{3,19},{19,3},{4,20},{20... | collective-permute-start | bytes 393224 | tf_op jit(solution)/shard_map/ppermute | solution.py:623
  145.5 3.4 %collective-permute-done.28 = bf16[32,2048]{1,0:T(8,128)(2,1)S(1)} collective-permute-done((bf16[32,2048]{1,0:T(8,128)(2,1)S(1)}, bf16[32,2048]{1,0:T(8,128)(2,1)S(1)}, u32[]{:S(2)}, u32[]{:S(2)}) %collective-permute-start.28) | collective-permute-done | bytes 131104 | tf_op jit(solution)/shard_map/ppermute | solution.py:623
  148.9 0.7 fusion.2
  (96 shorter events, 4.4 us)
Async XLA Ops:
  0.0 8.5 %copy-start.21 = (bf16[2048]{0:T(1024)(128)(2,1)S(1)}, bf16[2048]{0:T(1024)(128)(2,1)}, u32[]{:S(2)}) copy-start(bf16[2048]{0:T(1024)(128)(2,1)} %param.9) | copy-start | bytes 12292
  0.0 8.5 %copy-start.20 = (bf16[1,32,2048]{2,1,0:T(8,128)(2,1)S(1)}, bf16[1,32,2048]{2,1,0:T(8,128)(2,1)}, u32[]{:S(2)}) copy-start(bf16[1,32,2048]{2,1,0:T(8,128)(2,1)} %param.8) | copy-start | bytes 393220
  0.0 64.9 %collective-permute-start = (bf16[4,256,4096]{2,1,0:T(8,128)(2,1)}, bf16[4,256,4096]{2,1,0:T(8,128)(2,1)}, u32[]{:S(2)}, u32[]{:S(2)}) collective-permute-start(bf16[4,256,4096]{2,1,0:T(8,128)(2,1)} %refs_1_.7), channel_id=1, source_target_pairs={{0,2},{2,0},{4,6},{6,4},{8,10},{10,8},{12,14},{14,12},{1,3},{3,1},... | collective-permute-start | bytes 25165832 | tf_op jit(solution)/shard_map/ppermute | solution.py:194
  1.4 23.7 %copy-start.22 = (s32[8,16]{1,0:T(8,128)S(1)}, s32[8,16]{1,0:T(8,128)}, u32[]{:S(2)}) copy-start(s32[8,16]{1,0:T(8,128)} %param.15) | copy-start | bytes 1540
  1.4 12.6 %collective-permute-start.1 = (bf16[256,1024]{1,0:T(8,128)(2,1)S(1)}, bf16[256,1024]{1,0:T(8,128)(2,1)}, u32[]{:S(2)}, u32[]{:S(2)}) collective-permute-start(bf16[256,1024]{1,0:T(8,128)(2,1)S(1)} %pad_maximum_fusion.2), channel_id=1, source_target_pairs={{0,2},{2,0},{4,6},{6,4},{8,10},{10,8},{12,14},{14,12},{1,3},{3,1},... | collective-permute-start | bytes 1572872 | tf_op jit(solution)/shard_map/ppermute | solution.py:194
  2.0 36.0 %copy-start.15 = (bf16[256,1024]{1,0:T(8,128)(2,1)}, bf16[256,1024]{1,0:T(8,128)(2,1)S(1)}, u32[]{:S(2)}) copy-start(bf16[256,1024]{1,0:T(8,128)(2,1)S(1)} %pad_maximum_fusion.1.refs_20_) | copy-start | bytes 1572868
  2.0 14.4 %collective-permute-start.2 = (bf16[256,1024]{1,0:T(8,128)(2,1)S(1)}, bf16[256,1024]{1,0:T(8,128)(2,1)S(1)}, u32[]{:S(2)}, u32[]{:S(2)}) collective-permute-start(bf16[256,1024]{1,0:T(8,128)(2,1)S(1)} %pad_maximum_fusion.1.refs_20_), channel_id=1, source_target_pairs={{0,1},{1,0},{2,3},{3,2},{4,5},{5,4},{6,7},{7,6},{8,9},{9,8},{10,11... | collective-permute-start | bytes 1572872 | tf_op jit(solution)/shard_map/ppermute | solution.py:208
  2.6 17.3 %collective-permute-start.5 = (bf16[256,1024]{1,0:T(8,128)(2,1)S(1)}, bf16[256,1024]{1,0:T(8,128)(2,1)S(1)}, u32[]{:S(2)}, u32[]{:S(2)}) collective-permute-start(bf16[256,1024]{1,0:T(8,128)(2,1)S(1)} %pad_maximum_fusion.1.refs_20_), channel_id=1, source_target_pairs={{4,0},{6,2},{8,4},{10,6},{12,8},{14,10},{5,1},{7,3},{9,5},{11,7},{... | collective-permute-start | bytes 1572872 | tf_op jit(solution)/shard_map/ppermute | solution.py:199
  4.5 15.5 %collective-permute-start.7 = (bf16[256,1024]{1,0:T(8,128)(2,1)S(1)}, bf16[256,1024]{1,0:T(8,128)(2,1)S(1)}, u32[]{:S(2)}, u32[]{:S(2)}) collective-permute-start(bf16[256,1024]{1,0:T(8,128)(2,1)S(1)} %pad_maximum_fusion.1.refs_20_), channel_id=1, source_target_pairs={{0,4},{2,6},{4,8},{6,10},{8,12},{10,14},{1,5},{3,7},{5,9},{7,11},{... | collective-permute-start | bytes 1572872 | tf_op jit(solution)/shard_map/ppermute | solution.py:202
  14.0 17.0 %collective-permute-start.4 = (bf16[256,1024]{1,0:T(8,128)(2,1)}, bf16[256,1024]{1,0:T(8,128)(2,1)}, u32[]{:S(2)}, u32[]{:S(2)}) collective-permute-start(bf16[256,1024]{1,0:T(8,128)(2,1)} %collective-permute-done.1.refs_21_), channel_id=1, source_target_pairs={{4,0},{6,2},{8,4},{10,6},{12,8},{14,10},{5,1},{7,3},{9,5},{11,7},{... | collective-permute-start | bytes 1572872 | tf_op jit(solution)/shard_map/ppermute | solution.py:199
  16.4 22.9 %copy-start.14 = (bf16[256,1024]{1,0:T(8,128)(2,1)}, bf16[256,1024]{1,0:T(8,128)(2,1)S(1)}, u32[]{:S(2)}) copy-start(bf16[256,1024]{1,0:T(8,128)(2,1)S(1)} %collective-permute-done.2.refs_22_) | copy-start | bytes 1572868
  16.4 16.4 %collective-permute-start.6 = (bf16[256,1024]{1,0:T(8,128)(2,1)}, bf16[256,1024]{1,0:T(8,128)(2,1)}, u32[]{:S(2)}, u32[]{:S(2)}) collective-permute-start(bf16[256,1024]{1,0:T(8,128)(2,1)} %collective-permute-done.1.refs_21_), channel_id=1, source_target_pairs={{0,4},{2,6},{4,8},{6,10},{8,12},{10,14},{1,5},{3,7},{5,9},{7,11},{... | collective-permute-start | bytes 1572872 | tf_op jit(solution)/shard_map/ppermute | solution.py:202
  19.9 19.4 %copy-start.9 = (bf16[256,1024]{1,0:T(8,128)(2,1)}, bf16[256,1024]{1,0:T(8,128)(2,1)S(1)}, u32[]{:S(2)}) copy-start(bf16[256,1024]{1,0:T(8,128)(2,1)S(1)} %collective-permute-done.5.refs_29_) | copy-start | bytes 1572868
  20.0 19.3 %copy-start.10 = (bf16[256,1024]{1,0:T(8,128)(2,1)}, bf16[256,1024]{1,0:T(8,128)(2,1)S(1)}, u32[]{:S(2)}) copy-start(bf16[256,1024]{1,0:T(8,128)(2,1)S(1)} %collective-permute-done.7.refs_28_) | copy-start | bytes 1572868
  21.3 23.1 %collective-permute-start.11 = (bf16[256,1024]{1,0:T(8,128)(2,1)}, bf16[256,1024]{1,0:T(8,128)(2,1)S(1)}, u32[]{:S(2)}, u32[]{:S(2)}) collective-permute-start(bf16[256,1024]{1,0:T(8,128)(2,1)} %get-tuple-element.26), channel_id=1, source_target_pairs={{4,0},{6,2},{8,4},{10,6},{12,8},{14,10},{5,1},{7,3},{9,5},{11,7},{... | collective-permute-start | bytes 1572872 | tf_op jit(solution)/shard_map/ppermute | solution.py:199
  24.2 15.1 %collective-permute-start.3 = (bf16[256,1024]{1,0:T(8,128)(2,1)}, bf16[256,1024]{1,0:T(8,128)(2,1)S(1)}, u32[]{:S(2)}, u32[]{:S(2)}) collective-permute-start(bf16[256,1024]{1,0:T(8,128)(2,1)} %collective-permute-done.1.refs_21_), channel_id=1, source_target_pairs={{0,1},{1,0},{2,3},{3,2},{4,5},{5,4},{6,7},{7,6},{8,9},{9,8},{10,11... | collective-permute-start | bytes 1572872 | tf_op jit(solution)/shard_map/ppermute | solution.py:208
  31.0 11.5 %collective-permute-start.17 = (f32[32,1152]{1,0:T(8,128)}, f32[32,1152]{1,0:T(8,128)S(1)}, u32[]{:S(2)}, u32[]{:S(2)}) collective-permute-start(f32[32,1152]{1,0:T(8,128)} %pad_maximum_fusion.3), channel_id=1, source_target_pairs={{0,1},{1,0},{2,3},{3,2},{4,5},{5,4},{6,7},{7,6},{8,9},{9,8},{10,11... | collective-permute-start | bytes 442376 | tf_op jit(solution)/shard_map/ppermute | solution.py:208
  32.9 15.7 %collective-permute-start.12 = (bf16[256,1024]{1,0:T(8,128)(2,1)}, bf16[256,1024]{1,0:T(8,128)(2,1)S(1)}, u32[]{:S(2)}, u32[]{:S(2)}) collective-permute-start(bf16[256,1024]{1,0:T(8,128)(2,1)} %get-tuple-element.25), channel_id=1, source_target_pairs={{0,4},{2,6},{4,8},{6,10},{8,12},{10,14},{1,5},{3,7},{5,9},{7,11},{... | collective-permute-start | bytes 1572872 | tf_op jit(solution)/shard_map/ppermute | solution.py:202
  39.3 24.4 %copy-start.3 = (bf16[256,1024]{1,0:T(8,128)(2,1)}, bf16[256,1024]{1,0:T(8,128)(2,1)S(1)}, u32[]{:S(2)}) copy-start(bf16[256,1024]{1,0:T(8,128)(2,1)S(1)} %collective-permute-done.3.refs_1_.refs_23_) | copy-start | bytes 1572868
  39.3 25.6 %copy-start.2 = (bf16[512,1024]{1,0:T(8,128)(2,1)}, bf16[512,1024]{1,0:T(8,128)(2,1)S(1)}, u32[]{:S(2)}) copy-start(bf16[512,1024]{1,0:T(8,128)(2,1)S(1)} %after.3.refs_24_) | copy-start | bytes 3145732
  39.3 24.4 %collective-permute-start.8 = (bf16[512,1024]{1,0:T(8,128)(2,1)S(1)}, bf16[512,1024]{1,0:T(8,128)(2,1)S(1)}, u32[]{:S(2)}, u32[]{:S(2)}) collective-permute-start(bf16[512,1024]{1,0:T(8,128)(2,1)S(1)} %after.3.refs_24_), channel_id=1, source_target_pairs={{0,1},{1,0},{2,3},{3,2},{4,5},{5,4},{6,7},{7,6},{8,9},{9,8},{10,11... | collective-permute-start | bytes 3145736 | tf_op jit(solution)/shard_map/ppermute | solution.py:208
  42.5 17.0 %collective-permute-start.10 = (bf16[256,1024]{1,0:T(8,128)(2,1)}, bf16[256,1024]{1,0:T(8,128)(2,1)S(1)}, u32[]{:S(2)}, u32[]{:S(2)}) collective-permute-start(bf16[256,1024]{1,0:T(8,128)(2,1)} %collective-permute-done.4), channel_id=1, source_target_pairs={{4,0},{6,2},{8,4},{10,6},{5,1},{7,3},{9,5},{11,7},{20,16},{22,18},... | collective-permute-start | bytes 1572872 | tf_op jit(solution)/shard_map/ppermute | solution.py:199
  44.4 20.5 %copy-start.7 = (bf16[256,1024]{1,0:T(8,128)(2,1)}, bf16[256,1024]{1,0:T(8,128)(2,1)S(1)}, u32[]{:S(2)}) copy-start(bf16[256,1024]{1,0:T(8,128)(2,1)S(1)} %collective-permute-done.11.refs_27_.refs_11_) | copy-start | bytes 1572868
  44.4 16.6 %collective-permute-start.9 = (bf16[256,1024]{1,0:T(8,128)(2,1)}, bf16[256,1024]{1,0:T(8,128)(2,1)S(1)}, u32[]{:S(2)}, u32[]{:S(2)}) collective-permute-start(bf16[256,1024]{1,0:T(8,128)(2,1)} %collective-permute-done.6), channel_id=1, source_target_pairs={{4,8},{6,10},{8,12},{10,14},{5,9},{7,11},{9,13},{11,15},{20,24},{2... | collective-permute-start | bytes 1572872 | tf_op jit(solution)/shard_map/ppermute | solution.py:202
  48.5 16.4 %copy-start.8 = (bf16[256,1024]{1,0:T(8,128)(2,1)}, bf16[256,1024]{1,0:T(8,128)(2,1)S(1)}, u32[]{:S(2)}) copy-start(bf16[256,1024]{1,0:T(8,128)(2,1)S(1)} %collective-permute-done.12.refs_30_.refs_12_) | copy-start | bytes 1572868
  48.6 35.6 %collective-permute-start.14 = (bf16[256,1024]{1,0:T(8,128)(2,1)S(1)}, bf16[256,1024]{1,0:T(8,128)(2,1)S(1)}, u32[]{:S(2)}, u32[]{:S(2)}) collective-permute-start(bf16[256,1024]{1,0:T(8,128)(2,1)S(1)} %collective-permute-done.11.refs_27_.refs_11_), channel_id=1, source_target_pairs={{4,0},{6,2},{8,4},{10,6},{5,1},{7,3},{9,5},{11,7},{20,16},{22,18},... | collective-permute-start | bytes 1572872 | tf_op jit(solution)/shard_map/ppermute | solution.py:199
  59.4 24.7 %collective-permute-start.15 = (bf16[256,1024]{1,0:T(8,128)(2,1)S(1)}, bf16[256,1024]{1,0:T(8,128)(2,1)S(1)}, u32[]{:S(2)}, u32[]{:S(2)}) collective-permute-start(bf16[256,1024]{1,0:T(8,128)(2,1)S(1)} %collective-permute-done.12.refs_30_.refs_12_), channel_id=1, source_target_pairs={{4,8},{6,10},{8,12},{10,14},{5,9},{7,11},{9,13},{11,15},{20,24},{2... | collective-permute-start | bytes 1572872 | tf_op jit(solution)/shard_map/ppermute | solution.py:202
  62.2 22.0 %collective-permute-start.13 = (bf16[256,1024]{1,0:T(8,128)(2,1)S(1)}, bf16[256,1024]{1,0:T(8,128)(2,1)S(1)}, u32[]{:S(2)}, u32[]{:S(2)}) collective-permute-start(bf16[256,1024]{1,0:T(8,128)(2,1)S(1)} %get-tuple-element.23), channel_id=1, source_target_pairs={{4,0},{6,2},{8,12},{10,14},{5,1},{7,3},{9,13},{11,15},{20,16},{22,... | collective-permute-start | bytes 1572872 | tf_op jit(solution)/shard_map/ppermute | solution.py:205
  63.8 1.3 copy-start.11
  63.8 1.0 copy-start.18
  64.8 30.3 %collective-permute-start.16 = (bf16[512,1024]{1,0:T(8,128)(2,1)S(1)}, bf16[512,1024]{1,0:T(8,128)(2,1)S(1)}, u32[]{:S(2)}, u32[]{:S(2)}) collective-permute-start(bf16[512,1024]{1,0:T(8,128)(2,1)S(1)} %pad_maximum_fusion.refs_26_), channel_id=1, source_target_pairs={{0,1},{1,0},{2,3},{3,2},{4,5},{5,4},{6,7},{7,6},{8,9},{9,8},{10,11... | collective-permute-start | bytes 3145736 | tf_op jit(solution)/shard_map/ppermute | solution.py:208
  64.9 23.4 %collective-permute-start.18 = (bf16[32,512]{1,0:T(8,128)(2,1)S(1)}, bf16[32,512]{1,0:T(8,128)(2,1)S(1)}, u32[]{:S(2)}, u32[]{:S(2)}) collective-permute-start(bf16[32,512]{1,0:T(8,128)(2,1)S(1)} %constant_dynamic-slice_fusion), channel_id=1, source_target_pairs={{0,2},{2,0},{4,6},{6,4},{8,10},{10,8},{12,14},{14,12},{1,3},{3,1},... | collective-permute-start | bytes 98312 | tf_op jit(solution)/shard_map/ppermute | solution.py:194
  84.9 3.5 %copy-start.6 = (f32[8,128]{1,0:T(8,128)S(1)}, f32[8,128]{1,0:T(8,128)}, u32[]{:S(2)}) copy-start(f32[8,128]{1,0:T(8,128)} %get-tuple-element.15.refs_3_.refs_1_) | copy-start | bytes 12292
  84.9 10.2 %copy-start = (bf16[256,1024]{1,0:T(8,128)(2,1)}, bf16[256,1024]{1,0:T(8,128)(2,1)S(1)}, u32[]{:S(2)}) copy-start(bf16[256,1024]{1,0:T(8,128)(2,1)S(1)} %get-tuple-element.17.refs_10_.refs_9_) | copy-start | bytes 1572868
  84.9 10.2 %copy-start.1 = (bf16[256,1024]{1,0:T(8,128)(2,1)}, bf16[256,1024]{1,0:T(8,128)(2,1)S(1)}, u32[]{:S(2)}) copy-start(bf16[256,1024]{1,0:T(8,128)(2,1)S(1)} %get-tuple-element.18.refs_13_.refs_10_) | copy-start | bytes 1572868
  85.0 10.2 %copy-start.16 = (bf16[256,1024]{1,0:T(8,128)(2,1)}, bf16[256,1024]{1,0:T(8,128)(2,1)S(1)}, u32[]{:S(2)}) copy-start(bf16[256,1024]{1,0:T(8,128)(2,1)S(1)} %select_select_fusion.refs_9_) | copy-start | bytes 1572868
  85.0 24.4 %collective-permute-start.21 = (bf16[256,1024]{1,0:T(8,128)(2,1)S(1)}, bf16[256,1024]{1,0:T(8,128)(2,1)S(1)}, u32[]{:S(2)}, u32[]{:S(2)}) collective-permute-start(bf16[256,1024]{1,0:T(8,128)(2,1)S(1)} %select_select_fusion.refs_9_), channel_id=1, source_target_pairs={{0,1},{1,0},{2,3},{3,2},{4,5},{5,4},{6,7},{7,6},{8,9},{9,8},{10,11... | collective-permute-start | bytes 1572872 | tf_op jit(solution)/shard_map/ppermute | solution.py:208
  87.0 22.4 %collective-permute-start.22 = (bf16[256,1024]{1,0:T(8,128)(2,1)S(1)}, bf16[256,1024]{1,0:T(8,128)(2,1)S(1)}, u32[]{:S(2)}, u32[]{:S(2)}) collective-permute-start(bf16[256,1024]{1,0:T(8,128)(2,1)S(1)} %broadcast_select_fusion.2), channel_id=1, source_target_pairs={{4,0},{6,2},{8,12},{10,14},{5,1},{7,3},{9,13},{11,15},{20,16},{22,... | collective-permute-start | bytes 1572872 | tf_op jit(solution)/shard_map/ppermute | solution.py:205
  88.4 20.9 %collective-permute-start.19 = (bf16[2,32,512]{2,1,0:T(8,128)(2,1)S(1)}, bf16[2,32,512]{2,1,0:T(8,128)(2,1)S(1)}, u32[]{:S(2)}, u32[]{:S(2)}) collective-permute-start(bf16[2,32,512]{2,1,0:T(8,128)(2,1)S(1)} %after.5), channel_id=1, source_target_pairs={{0,0},{2,2},{4,4},{6,6},{1,8},{3,10},{5,12},{7,14},{8,1},{10,3},{1... | collective-permute-start | bytes 196616 | tf_op jit(solution)/shard_map/ppermute | solution.py:543
  93.9 15.5 %collective-permute-start.20 = (bf16[2,32,512]{2,1,0:T(8,128)(2,1)S(1)}, bf16[2,32,512]{2,1,0:T(8,128)(2,1)S(1)}, u32[]{:S(2)}, u32[]{:S(2)}) collective-permute-start(bf16[2,32,512]{2,1,0:T(8,128)(2,1)S(1)} %after.5), channel_id=1, source_target_pairs={{4,0},{6,2},{0,4},{2,6},{5,8},{7,10},{1,12},{3,14},{12,1},{14,3},{... | collective-permute-start | bytes 196616 | tf_op jit(solution)/shard_map/ppermute | solution.py:543
  95.1 1.0 copy-start.17
  109.4 1.0 copy-start.13
  119.8 9.6 %collective-permute-start.23 = (f32[32,640]{1,0:T(8,128)}, f32[32,640]{1,0:T(8,128)S(1)}, u32[]{:S(2)}, u32[]{:S(2)}) collective-permute-start(f32[32,640]{1,0:T(8,128)} %get-tuple-element.20), channel_id=1, source_target_pairs={{0,4},{2,6},{4,8},{6,10},{8,12},{10,14},{12,0},{14,2},{1,5},{3,7},... | collective-permute-start | bytes 245768 | tf_op jit(solution)/shard_map/ppermute | solution.py:606
  119.9 9.6 %collective-permute-start.24 = (f32[32,640]{1,0:T(8,128)}, f32[32,640]{1,0:T(8,128)S(1)}, u32[]{:S(2)}, u32[]{:S(2)}) collective-permute-start(f32[32,640]{1,0:T(8,128)} %get-tuple-element.21), channel_id=1, source_target_pairs={{0,8},{2,10},{4,12},{6,14},{8,0},{10,2},{12,4},{14,6},{1,9},{3,11}... | collective-permute-start | bytes 245768 | tf_op jit(solution)/shard_map/ppermute | solution.py:606
  123.7 7.1 %collective-permute-start.25 = (f32[32,640]{1,0:T(8,128)}, f32[32,640]{1,0:T(8,128)S(1)}, u32[]{:S(2)}, u32[]{:S(2)}) collective-permute-start(f32[32,640]{1,0:T(8,128)} %get-tuple-element.22), channel_id=1, source_target_pairs={{0,12},{2,14},{4,0},{6,2},{8,4},{10,6},{12,8},{14,10},{1,13},{3,15... | collective-permute-start | bytes 245768 | tf_op jit(solution)/shard_map/ppermute | solution.py:606
  132.1 6.3 %collective-permute-start.26 = (bf16[32,512]{1,0:T(8,128)(2,1)S(1)}, bf16[32,512]{1,0:T(8,128)(2,1)S(1)}, u32[]{:S(2)}, u32[]{:S(2)}) collective-permute-start(bf16[32,512]{1,0:T(8,128)(2,1)S(1)} %merge.1), channel_id=1, source_target_pairs={{0,0},{1,8},{2,1},{3,9},{4,2},{5,10},{6,3},{7,11},{8,4},{9,12},{10... | collective-permute-start | bytes 98312 | tf_op jit(solution)/shard_map/ppermute | solution.py:618
  134.8 6.1 %collective-permute-start.27 = (bf16[32,512]{1,0:T(8,128)(2,1)S(1)}, bf16[32,512]{1,0:T(8,128)(2,1)S(1)}, u32[]{:S(2)}, u32[]{:S(2)}) collective-permute-start(bf16[32,512]{1,0:T(8,128)(2,1)S(1)} %merge.1), channel_id=1, source_target_pairs={{0,1},{1,9},{2,0},{3,8},{4,3},{5,11},{6,2},{7,10},{8,5},{9,13},{10... | collective-permute-start | bytes 98312 | tf_op jit(solution)/shard_map/ppermute | solution.py:618
  143.9 5.0 %collective-permute-start.28 = (bf16[32,2048]{1,0:T(8,128)(2,1)S(1)}, bf16[32,2048]{1,0:T(8,128)(2,1)S(1)}, u32[]{:S(2)}, u32[]{:S(2)}) collective-permute-start(bf16[32,2048]{1,0:T(8,128)(2,1)S(1)} %convolution_convert_fusion), channel_id=1, source_target_pairs={{0,16},{16,0},{1,17},{17,1},{2,18},{18,2},{3,19},{19,3},{4,20},{20... | collective-permute-start | bytes 393224 | tf_op jit(solution)/shard_map/ppermute | solution.py:623
  (4 other events, 3.3 us)

commit v4 on v3

--- a/solution.py
+++ b/solution.py
@@ -156,7 +156,7 @@
 
 
 CHIPS = 4
-VMEM_LIMIT = 56 * 2**20
+VMEM_LIMIT = 44 * 2**20
 PIECE = 256
 
 
@@ -194,7 +194,7 @@
     return lax.ppermute(value, "pb", [(p, p ^ 1) for p in range(2 * CHIPS)])
 
 
-def gather_pieces(own, partner, z, add_pieces, terms, pair_of, questions, other_rows):
+def gather_pieces(own, partner, z, add_pieces, terms, pair_of, questions, ready):
     def left(value, sources):
         return lax.ppermute(value, "pb", line(-1, sources))
 
@@ -252,7 +252,7 @@
         None,
     )
 
-    end_a3, l_b3, r_b3 = after((end_a3, l_b3, r_b3), (token,))
+    end_a3, l_b3, r_b3 = after((end_a3, l_b3, r_b3), (token, *ready))
     a3 = by_chip(z, (end_a3, l_a2, r_a2, end_a3))
     x_a3 = across(a3)
     end_b4 = outward(jnp.where(z < 2, l_b3, r_b3))
@@ -522,6 +522,51 @@
     )(*parts)
 
 
+def hold_kernel(weights, ready, out, sem):
+    copy = pltpu.make_async_copy(weights, out, sem)
+    copy.start()
+    copy.wait()
+
+
+def hold(weights, ready):
+    anywhere = pl.BlockSpec(memory_space=pl.ANY)
+    return pl.pallas_call(
+        hold_kernel,
+        in_specs=[anywhere, anywhere],
+        out_specs=pl.BlockSpec(memory_space=pltpu.VMEM),
+        out_shape=pltpu.VMEM(weights.shape, weights.dtype),
+        scratch_shapes=[pltpu.SemaphoreType.DMA],
+        compiler_params=pltpu.CompilerParams(vmem_limit_bytes=2**20),
+        cost_estimate=pl.CostEstimate(flops=0, bytes_accessed=2 * weights.size, transcendentals=0),
+        name="hold",
+    )(weights, ready)
+
+
+def output_kernel(place, weights, first, second, out):
+    width = first.shape[1]
+    total = jnp.zeros(out.shape, jnp.float32)
+    for part, core in ((first, place[0]), (second, 1 - place[0])):
+        rows = weights[pl.ds(pl.multiple_of(core * width, width), width), :]
+        total += jnp.dot(part[...], rows, preferred_element_type=jnp.float32)
+    out[...] = total.astype(out.dtype)
+
+
+def output_terms(place, weights, first, second):
+    inside = pl.BlockSpec(memory_space=pltpu.VMEM)
+    answers, columns = first.shape[0], weights.shape[1]
+    return pl.pallas_call(
+        output_kernel,
+        in_specs=[pl.BlockSpec(memory_space=pltpu.SMEM), inside, inside, inside],
+        out_specs=inside,
+        out_shape=jax.ShapeDtypeStruct((answers, columns), jnp.bfloat16),
+        compiler_params=pltpu.CompilerParams(vmem_limit_bytes=16 * 2**20),
+        cost_estimate=pl.CostEstimate(
+            flops=2 * answers * weights.size, bytes_accessed=4 * answers * columns, transcendentals=0
+        ),
+        name="output",
+    )(place, weights, first, second)
+
+
 def query_terms(states, norm_gain, query_weight):
     states_wide = states.astype(jnp.float32)
     square_part = jnp.sum(states_wide * states_wide, axis=1, keepdims=True)
@@ -584,9 +629,6 @@
         theirs = core_swap(lax.dynamic_slice_in_dim(query, (1 - c) * width, width, 1))
         return jnp.stack([jnp.where(c == 0, mine, theirs), jnp.where(c == 0, theirs, mine)])
 
-    sums, last, queries = gather_pieces(own, partner, z, add_pieces, terms, pair_of, questions, other_rows)
-    queries = jnp.concatenate(queries, axis=0)
-
     blocks_here = rows // BLOCK
     mine = lax.dynamic_slice_in_dim(block_mask, f * questions, questions, 0)
     live = jnp.concatenate(
@@ -594,6 +636,10 @@
         axis=1,
     )
     live = jnp.repeat(live, BLOCK, axis=1)[:, None, :]
+
+    sums, last, queries = gather_pieces(own, partner, z, add_pieces, terms, pair_of, questions, (live,))
+    queries = jnp.concatenate(queries, axis=0)
+
 
     def partials(first, amount):
         return attend_last(
@@ -616,10 +662,7 @@
             for x in range(2)
         ]
         received.append(lax.ppermute(attention, ("pb", "fsdp"), sends))
-    first = jnp.where(f == 0, received[0], received[1])
-    second = jnp.where(f == 0, received[1], received[0])
-    whole = jnp.concatenate([first, second], axis=1)
-    partial_out = jnp.dot(whole, out_weight, preferred_element_type=jnp.float32).astype(jnp.bfloat16)
+    partial_out = output_terms(f[None].astype(jnp.int32), hold(out_weight, attention), *received)
     other_out = lax.ppermute(partial_out, "section", [(0, 1), (1, 0)])
     summed = (partial_out.astype(jnp.float32) + other_out.astype(jnp.float32)).astype(jnp.bfloat16)
     return summed[None]

time: 151 us -> 138 us (0.914)
  Pallas kernels: 47.9 us -> 41.8 us
  local copies, waits for them, and re-layouts: 7.39 us -> 1.72 us
  matrix products: 6.02 us -> 3.01 us
  starting transfers between devices: 49.6 us -> 52.4 us
    pallas_call x2, Pallas kernels: 15.1 us -> 11 us  [attend_last(): pl.pallas_call(functools.partial(attend_kernel, wanted, len(arrays)), gri...]
    unnamed x47 -> x9, local copies, waits for them, and re-layouts: 3.88 us -> 0.02 us
    pallas_call x2, Pallas kernels: 32.3 us -> 29.3 us  [project_pieces(): pl.pallas_call(functools.partial(project_kernel, wanted, len(arrays), car...]
    dot_general x1 -> x0, matrix products: 3.01 us -> none  [gathered_shards(): jnp.dot(whole, out_weight, preferred_element_type=jnp.float32)]
    ppermute x3, starting transfers between devices: 3.86 us -> 6.26 us  [gathered_shards(): arrived.append(lax.ppermute(part, 'pb', turn))]
  transfers between devices with their start and end apart: 29 -> 29, of which waited for: 10 -> 11; matrix products, arithmetic and copies ran while one was open for 8% -> 7% of each run, Pallas kernels for 25% -> 24%
where the time goes in v4:
time: 138 us
  starting transfers between devices  52.4 us (38%)
  Pallas kernels  41.8 us (30%)
  waiting for transfers between devices  31.9 us (23%)
  other arithmetic  6.16 us (4%)
  matrix products  3.01 us (2%)
  local copies, waits for them, and re-layouts  1.72 us (1%)
    pallas_call x2, Pallas kernels, project_pieces(): pl.pallas_call(functools.partial(project_kernel, wanted, len(arrays), car...  29.3 us
    ppermute x5, starting transfers between devices, right(): return lax.ppermute(value, 'pb', line(1, sources))  16.4 us
    ppermute x5, waiting for transfers between devices, left(): return lax.ppermute(value, 'pb', line(-1, sources))  14.2 us
    ppermute x5, starting transfers between devices, left(): return lax.ppermute(value, 'pb', line(-1, sources))  11.1 us
    pallas_call x2, Pallas kernels, attend_last(): pl.pallas_call(functools.partial(attend_kernel, wanted, len(arrays)), gri...  11 us
    ppermute x3, starting transfers between devices, gathered_shards(): arrived.append(lax.ppermute(part, 'pb', turn))  6.26 us
    ppermute x2, starting transfers between devices, spread_queries(): spread.append(lax.ppermute(pair, ('pb', 'fsdp'), sends))  6.13 us
    ppermute x2, waiting for transfers between devices, gathered_shards(): received.append(lax.ppermute(attention, ('pb', 'fsdp'), sends))  4.84 us
  transfers between devices with their start and end apart: 29, of which 11 were waited for; matrix products, arithmetic and copies ran while one was open for 7% of the time, Pallas kernels for 24%

profile of v4, /device:TPU:10, one launch (start us, length us, event | category | flops | bytes accessed | tf_op | source)
XLA Modules:
  0.0 137.6 jit_solution(7024290109795012509)
XLA Ops:
  0.0 1.3 constant_dynamic-slice_fusion.1
  1.4 0.5 collective-permute-start.1
  2.0 0.6 collective-permute-start.2
  2.6 1.9 %collective-permute-start.5 = (bf16[256,1024]{1,0:T(8,128)(2,1)S(1)}, bf16[256,1024]{1,0:T(8,128)(2,1)S(1)}, u32[]{:S(2)}, u32[]{:S(2)}) collective-permute-start(bf16[256,1024]{1,0:T(8,128)(2,1)S(1)} %pad_maximum_fusion.1.refs_20_), channel_id=1, source_target_pairs={{4,0},{6,2},{8,4},{10,6},{12,8},{14,10},{5,1},{7,3},{9,5},{11,7},{... | collective-permute-start | bytes 1572872 | tf_op jit(solution)/shard_map/ppermute | solution.py:199
  4.5 3.9 %collective-permute-start.7 = (bf16[256,1024]{1,0:T(8,128)(2,1)S(1)}, bf16[256,1024]{1,0:T(8,128)(2,1)S(1)}, u32[]{:S(2)}, u32[]{:S(2)}) collective-permute-start(bf16[256,1024]{1,0:T(8,128)(2,1)S(1)} %pad_maximum_fusion.1.refs_20_), channel_id=1, source_target_pairs={{0,4},{2,6},{4,8},{6,10},{8,12},{10,14},{1,5},{3,7},{5,9},{7,11},{... | collective-permute-start | bytes 1572872 | tf_op jit(solution)/shard_map/ppermute | solution.py:202
  8.6 3.0 %fusion.3 = f32[32,1024]{1,0:T(8,128)S(1)} fusion(bf16[2048,1024]{1,0:T(8,128)(2,1)} %param.10, bf16[1,32,2048]{2,1,0:T(8,128)(2,1)S(1)} %copy-done.1, f32[2048]{0:T(1024)S(1)} %convert_element_type.26), kind=kOutput, calls=%fused_computation.18 | convolution fusion | flops 134414336 | bytes 4464640 | tf_op jit(solution)/shard_map/dot_general | solution.py:574
  11.6 2.4 %collective-permute-done.1.refs_21_ = bf16[256,1024]{1,0:T(8,128)(2,1)} collective-permute-done((bf16[256,1024]{1,0:T(8,128)(2,1)S(1)}, bf16[256,1024]{1,0:T(8,128)(2,1)}, u32[]{:S(2)}, u32[]{:S(2)}) %collective-permute-start.1) | collective-permute-done | bytes 524320 | tf_op jit(solution)/shard_map/ppermute | solution.py:194
  14.0 2.3 %collective-permute-start.4 = (bf16[256,1024]{1,0:T(8,128)(2,1)}, bf16[256,1024]{1,0:T(8,128)(2,1)}, u32[]{:S(2)}, u32[]{:S(2)}) collective-permute-start(bf16[256,1024]{1,0:T(8,128)(2,1)} %collective-permute-done.1.refs_21_), channel_id=1, source_target_pairs={{4,0},{6,2},{8,4},{10,6},{12,8},{14,10},{5,1},{7,3},{9,5},{11,7},{... | collective-permute-start | bytes 1572872 | tf_op jit(solution)/shard_map/ppermute | solution.py:199
  16.4 3.5 %collective-permute-start.6 = (bf16[256,1024]{1,0:T(8,128)(2,1)}, bf16[256,1024]{1,0:T(8,128)(2,1)}, u32[]{:S(2)}, u32[]{:S(2)}) collective-permute-start(bf16[256,1024]{1,0:T(8,128)(2,1)} %collective-permute-done.1.refs_21_), channel_id=1, source_target_pairs={{0,4},{2,6},{4,8},{6,10},{8,12},{10,14},{1,5},{3,7},{5,9},{7,11},{... | collective-permute-start | bytes 1572872 | tf_op jit(solution)/shard_map/ppermute | solution.py:202
  20.0 1.1 broadcast_select_fusion
  21.1 3.0 %collective-permute-start.11 = (bf16[256,1024]{1,0:T(8,128)(2,1)}, bf16[256,1024]{1,0:T(8,128)(2,1)S(1)}, u32[]{:S(2)}, u32[]{:S(2)}) collective-permute-start(bf16[256,1024]{1,0:T(8,128)(2,1)} %get-tuple-element.26), channel_id=1, source_target_pairs={{4,0},{6,2},{8,4},{10,6},{12,8},{14,10},{5,1},{7,3},{9,5},{11,7},{... | collective-permute-start | bytes 1572872 | tf_op jit(solution)/shard_map/ppermute | solution.py:199
  24.1 0.9 collective-permute-start.3
  25.1 0.7 pad_maximum_fusion.3
  25.8 5.2 %collective-permute-done.4 = bf16[256,1024]{1,0:T(8,128)(2,1)} collective-permute-done((bf16[256,1024]{1,0:T(8,128)(2,1)}, bf16[256,1024]{1,0:T(8,128)(2,1)}, u32[]{:S(2)}, u32[]{:S(2)}) %collective-permute-start.4) | collective-permute-done | bytes 524320 | tf_op jit(solution)/shard_map/ppermute | solution.py:199
  31.0 0.5 collective-permute-start.17
  31.8 0.5 collective-permute-done.6
  32.3 3.5 %collective-permute-start.12 = (bf16[256,1024]{1,0:T(8,128)(2,1)}, bf16[256,1024]{1,0:T(8,128)(2,1)S(1)}, u32[]{:S(2)}, u32[]{:S(2)}) collective-permute-start(bf16[256,1024]{1,0:T(8,128)(2,1)} %get-tuple-element.25), channel_id=1, source_target_pairs={{0,4},{2,6},{4,8},{6,10},{8,12},{10,14},{1,5},{3,7},{5,9},{7,11},{... | collective-permute-start | bytes 1572872 | tf_op jit(solution)/shard_map/ppermute | solution.py:202
  35.8 1.6 %maximum_select_fusion.refs_0_ = bf16[512,1024]{1,0:T(8,128)(2,1)S(1)} fusion(bf16[256,1024]{1,0:T(8,128)(2,1)S(1)} %collective-permute-done.5.refs_29_, bf16[256,1024]{1,0:T(8,128)(2,1)} %collective-permute-done.4, bf16[256,1024]{1,0:T(8,128)(2,1)S(1)} %collective-permute-done.7.refs_28_, bf16[256,1024]{1,0:T(8,128)(2,1)} %collective-permute-done.6, pred[]{:T(512)S(6)} %lt.34), kind=kLoop, calls=%fused_computation | loop fusion | flops 4718592 | bytes 3145729 | tf_op jit(solution)/shard_map/jit(_where)/select_n | solution.py:223
  37.4 1.8 %collective-permute-done.3.refs_1_.refs_23_ = bf16[256,1024]{1,0:T(8,128)(2,1)S(1)} collective-permute-done((bf16[256,1024]{1,0:T(8,128)(2,1)}, bf16[256,1024]{1,0:T(8,128)(2,1)S(1)}, u32[]{:S(2)}, u32[]{:S(2)}) %collective-permute-start.3) | collective-permute-done | bytes 524320 | tf_op jit(solution)/shard_map/ppermute | solution.py:208
  39.5 2.9 %collective-permute-done.17 = f32[32,1152]{1,0:T(8,128)S(1)} collective-permute-done((f32[32,1152]{1,0:T(8,128)}, f32[32,1152]{1,0:T(8,128)S(1)}, u32[]{:S(2)}, u32[]{:S(2)}) %collective-permute-start.17) | collective-permute-done | bytes 147488 | tf_op jit(solution)/shard_map/ppermute | solution.py:208
  42.4 1.9 %collective-permute-start.10 = (bf16[256,1024]{1,0:T(8,128)(2,1)}, bf16[256,1024]{1,0:T(8,128)(2,1)S(1)}, u32[]{:S(2)}, u32[]{:S(2)}) collective-permute-start(bf16[256,1024]{1,0:T(8,128)(2,1)} %collective-permute-done.4), channel_id=1, source_target_pairs={{4,0},{6,2},{8,4},{10,6},{5,1},{7,3},{9,5},{11,7},{20,16},{22,18},... | collective-permute-start | bytes 1572872 | tf_op jit(solution)/shard_map/ppermute | solution.py:199
  44.4 4.0 %collective-permute-start.9 = (bf16[256,1024]{1,0:T(8,128)(2,1)}, bf16[256,1024]{1,0:T(8,128)(2,1)S(1)}, u32[]{:S(2)}, u32[]{:S(2)}) collective-permute-start(bf16[256,1024]{1,0:T(8,128)(2,1)} %collective-permute-done.6), channel_id=1, source_target_pairs={{4,8},{6,10},{8,12},{10,14},{5,9},{7,11},{9,13},{11,15},{20,24},{2... | collective-permute-start | bytes 1572872 | tf_op jit(solution)/shard_map/ppermute | solution.py:202
  48.5 1.9 %collective-permute-start.14 = (bf16[256,1024]{1,0:T(8,128)(2,1)S(1)}, bf16[256,1024]{1,0:T(8,128)(2,1)S(1)}, u32[]{:S(2)}, u32[]{:S(2)}) collective-permute-start(bf16[256,1024]{1,0:T(8,128)(2,1)S(1)} %collective-permute-done.11.refs_27_.refs_11_), channel_id=1, source_target_pairs={{4,0},{6,2},{8,4},{10,6},{5,1},{7,3},{9,5},{11,7},{20,16},{22,18},... | collective-permute-start | bytes 1572872 | tf_op jit(solution)/shard_map/ppermute | solution.py:199
  50.4 9.0 %collective-permute-done.10 = bf16[256,1024]{1,0:T(8,128)(2,1)S(1)} collective-permute-done((bf16[256,1024]{1,0:T(8,128)(2,1)}, bf16[256,1024]{1,0:T(8,128)(2,1)S(1)}, u32[]{:S(2)}, u32[]{:S(2)}) %collective-permute-start.10) | collective-permute-done | bytes 524320 | tf_op jit(solution)/shard_map/ppermute | solution.py:199
  59.4 1.6 %collective-permute-start.15 = (bf16[256,1024]{1,0:T(8,128)(2,1)S(1)}, bf16[256,1024]{1,0:T(8,128)(2,1)S(1)}, u32[]{:S(2)}, u32[]{:S(2)}) collective-permute-start(bf16[256,1024]{1,0:T(8,128)(2,1)S(1)} %collective-permute-done.12.refs_30_.refs_12_), channel_id=1, source_target_pairs={{4,8},{6,10},{8,12},{10,14},{5,9},{7,11},{9,13},{11,15},{20,24},{2... | collective-permute-start | bytes 1572872 | tf_op jit(solution)/shard_map/ppermute | solution.py:202
  61.0 1.2 broadcast_select_fusion.3
  62.1 1.3 collective-permute-start.13
  63.9 17.7 %project.2 = (f32[4,512,1024]{2,1,0:T(8,128)}, f32[8,128]{1,0:T(8,128)S(1)}) custom-call(s32[11]{0:T(128)S(1)} %concatenate.36.info, bf16[4,256,4096]{2,1,0:T(8,128)(2,1)} %refs_1_.7, bf16[4,256,4096]{2,1,0:T(8,128)(2,1)} %refs_1_.7, bf16[4,256,4096]{2,1,0:T(8,128)(2,1)} %refs_1_.7, bf16[4,256,4096]{2,1,0:T(8,128)(2,1)} %refs_1_.7, ...), custom_call_target="tpu_custom_call" | custom-call | flops 1000 | bytes 1000 | tf_op jit(solution)/shard_map/project/pallas_call | solution.py:353
  81.8 2.0 %collective-permute-start.21 = (bf16[256,1024]{1,0:T(8,128)(2,1)S(1)}, bf16[256,1024]{1,0:T(8,128)(2,1)S(1)}, u32[]{:S(2)}, u32[]{:S(2)}) collective-permute-start(bf16[256,1024]{1,0:T(8,128)(2,1)S(1)} %select_select_fusion.refs_9_), channel_id=1, source_target_pairs={{0,1},{1,0},{2,3},{3,2},{4,5},{5,4},{6,7},{7,6},{8,9},{9,8},{10,11... | collective-permute-start | bytes 1572872 | tf_op jit(solution)/shard_map/ppermute | solution.py:208
  83.8 1.3 collective-permute-start.22
  85.2 4.9 %collective-permute-start.19 = (bf16[2,32,512]{2,1,0:T(8,128)(2,1)S(1)}, bf16[2,32,512]{2,1,0:T(8,128)(2,1)S(1)}, u32[]{:S(2)}, u32[]{:S(2)}) collective-permute-start(bf16[2,32,512]{2,1,0:T(8,128)(2,1)S(1)} %after.5), channel_id=1, source_target_pairs={{0,0},{2,2},{4,4},{6,6},{1,8},{3,10},{5,12},{7,14},{8,1},{10,3},{1... | collective-permute-start | bytes 196616 | tf_op jit(solution)/shard_map/ppermute | solution.py:588
  90.2 1.3 collective-permute-start.20
  91.4 11.6 %project.3 = (f32[4,512,1024]{2,1,0:T(8,128)}, f32[8,128]{1,0:T(8,128)}) custom-call(s32[5]{0:T(128)S(1)} %concatenate.35.info, bf16[4,256,4096]{2,1,0:T(8,128)(2,1)} %refs_1_.7, bf16[4,256,4096]{2,1,0:T(8,128)(2,1)} %refs_1_.7, bf16[4,256,4096]{2,1,0:T(8,128)(2,1)} %refs_1_.7, bf16[4,256,4096]{2,1,0:T(8,128)(2,1)} %refs_1_.7, ...), custom_call_target="tpu_custom_call", output_to_operand_aliasing={{0}: (9, {})} | custom-call | flops 1000 | bytes 1000 | tf_op jit(solution)/shard_map/project/pallas_call | solution.py:353
  103.1 7.2 %attend.2 = (f32[32,640]{1,0:T(8,128)S(1)}, f32[32,640]{1,0:T(8,128)S(1)}, f32[32,640]{1,0:T(8,128)S(1)}) custom-call(s32[3]{0:T(128)S(1)} %pad_add_fusion.1.info, bf16[4,256,4096]{2,1,0:T(8,128)(2,1)} %refs_1_.7, bf16[4,256,4096]{2,1,0:T(8,128)(2,1)} %refs_1_.7, ...), custom_call_target="tpu_custom_call" | custom-call | flops 2013265920 | bytes 7864320 | tf_op jit(solution)/shard_map/attend/pallas_call | solution.py:460
  110.3 2.3 %collective-permute-start.23 = (f32[32,640]{1,0:T(8,128)S(1)}, f32[32,640]{1,0:T(8,128)S(1)}, u32[]{:S(2)}, u32[]{:S(2)}) collective-permute-start(f32[32,640]{1,0:T(8,128)S(1)} %get-tuple-element.20), channel_id=1, source_target_pairs={{0,4},{2,6},{4,8},{6,10},{8,12},{10,14},{12,0},{14,2},{1,5},{3,7},... | collective-permute-start | bytes 245768 | tf_op jit(solution)/shard_map/ppermute | solution.py:652
  112.6 2.0 %collective-permute-start.24 = (f32[32,640]{1,0:T(8,128)S(1)}, f32[32,640]{1,0:T(8,128)S(1)}, u32[]{:S(2)}, u32[]{:S(2)}) collective-permute-start(f32[32,640]{1,0:T(8,128)S(1)} %get-tuple-element.21), channel_id=1, source_target_pairs={{0,8},{2,10},{4,12},{6,14},{8,0},{10,2},{12,4},{14,6},{1,9},{3,11}... | collective-permute-start | bytes 245768 | tf_op jit(solution)/shard_map/ppermute | solution.py:652
  114.6 1.9 %collective-permute-start.25 = (f32[32,640]{1,0:T(8,128)S(1)}, f32[32,640]{1,0:T(8,128)S(1)}, u32[]{:S(2)}, u32[]{:S(2)}) collective-permute-start(f32[32,640]{1,0:T(8,128)S(1)} %get-tuple-element.22), channel_id=1, source_target_pairs={{0,12},{2,14},{4,0},{6,2},{8,4},{10,6},{12,8},{14,10},{1,13},{3,15... | collective-permute-start | bytes 245768 | tf_op jit(solution)/shard_map/ppermute | solution.py:652
  116.5 3.8 %attend.3.refs_3_ = f32[32,640]{1,0:T(8,128)S(1)} custom-call(s32[3]{0:T(128)S(1)} %pad_add_fusion.1.info, bf16[4,256,4096]{2,1,0:T(8,128)(2,1)} %refs_1_.7, bf16[4,256,4096]{2,1,0:T(8,128)(2,1)} %refs_1_.7, ...), custom_call_target="tpu_custom_call" | custom-call | flops 671088640 | bytes 2621440 | tf_op jit(solution)/shard_map/attend/pallas_call | solution.py:460
  120.4 1.6 %collective-permute-done.25.refs_2_ = f32[32,640]{1,0:T(8,128)S(1)} collective-permute-done((f32[32,640]{1,0:T(8,128)S(1)}, f32[32,640]{1,0:T(8,128)S(1)}, u32[]{:S(2)}, u32[]{:S(2)}) %collective-permute-start.25) | collective-permute-done | bytes 81952 | tf_op jit(solution)/shard_map/ppermute | solution.py:652
  122.0 0.5 merge.1.ready
  122.5 1.9 %collective-permute-start.26 = (bf16[32,512]{1,0:T(8,128)(2,1)S(1)}, bf16[32,512]{1,0:T(8,128)(2,1)S(1)}, u32[]{:S(2)}, u32[]{:S(2)}) collective-permute-start(bf16[32,512]{1,0:T(8,128)(2,1)S(1)} %merge.1.ready), channel_id=1, source_target_pairs={{0,0},{1,8},{2,1},{3,9},{4,2},{5,10},{6,3},{7,11},{8,4},{9,12},{10... | collective-permute-start | bytes 98312 | tf_op jit(solution)/shard_map/ppermute | solution.py:664
  124.4 1.5 %collective-permute-start.27 = (bf16[32,512]{1,0:T(8,128)(2,1)S(1)}, bf16[32,512]{1,0:T(8,128)(2,1)S(1)}, u32[]{:S(2)}, u32[]{:S(2)}) collective-permute-start(bf16[32,512]{1,0:T(8,128)(2,1)S(1)} %merge.1.ready), channel_id=1, source_target_pairs={{0,1},{1,9},{2,0},{3,8},{4,3},{5,11},{6,2},{7,10},{8,5},{9,13},{10... | collective-permute-start | bytes 98312 | tf_op jit(solution)/shard_map/ppermute | solution.py:664
  126.3 2.6 %collective-permute-done.26.first = bf16[32,512]{1,0:T(8,128)(2,1)S(1)} collective-permute-done((bf16[32,512]{1,0:T(8,128)(2,1)S(1)}, bf16[32,512]{1,0:T(8,128)(2,1)S(1)}, u32[]{:S(2)}, u32[]{:S(2)}) %collective-permute-start.26) | collective-permute-done | bytes 32800 | tf_op jit(solution)/shard_map/ppermute | solution.py:664
  128.8 2.2 %collective-permute-done.27.second = bf16[32,512]{1,0:T(8,128)(2,1)S(1)} collective-permute-done((bf16[32,512]{1,0:T(8,128)(2,1)S(1)}, bf16[32,512]{1,0:T(8,128)(2,1)S(1)}, u32[]{:S(2)}, u32[]{:S(2)}) %collective-permute-start.27) | collective-permute-done | bytes 32800 | tf_op jit(solution)/shard_map/ppermute | solution.py:664
  131.1 0.8 output.1
  131.9 1.5 %collective-permute-start.28 = (bf16[32,2048]{1,0:T(8,128)(2,1)S(1)}, bf16[32,2048]{1,0:T(8,128)(2,1)S(1)}, u32[]{:S(2)}, u32[]{:S(2)}) collective-permute-start(bf16[32,2048]{1,0:T(8,128)(2,1)S(1)} %output.1), channel_id=1, source_target_pairs={{0,16},{16,0},{1,17},{17,1},{2,18},{18,2},{3,19},{19,3},{4,20},{20... | collective-permute-start | bytes 393224 | tf_op jit(solution)/shard_map/ppermute | solution.py:666
  133.4 3.4 %collective-permute-done.28 = bf16[32,2048]{1,0:T(8,128)(2,1)S(1)} collective-permute-done((bf16[32,2048]{1,0:T(8,128)(2,1)S(1)}, bf16[32,2048]{1,0:T(8,128)(2,1)S(1)}, u32[]{:S(2)}, u32[]{:S(2)}) %collective-permute-start.28) | collective-permute-done | bytes 131104 | tf_op jit(solution)/shard_map/ppermute | solution.py:666
  136.9 0.7 fusion.2
  (58 shorter events, 2.2 us)
Async XLA Ops:
  0.0 8.5 %copy-start.2 = (bf16[2048]{0:T(1024)(128)(2,1)S(1)}, bf16[2048]{0:T(1024)(128)(2,1)}, u32[]{:S(2)}) copy-start(bf16[2048]{0:T(1024)(128)(2,1)} %param.9) | copy-start | bytes 12292
  0.0 8.5 %copy-start.1 = (bf16[1,32,2048]{2,1,0:T(8,128)(2,1)S(1)}, bf16[1,32,2048]{2,1,0:T(8,128)(2,1)}, u32[]{:S(2)}) copy-start(bf16[1,32,2048]{2,1,0:T(8,128)(2,1)} %param.8) | copy-start | bytes 393220
  0.0 63.8 %collective-permute-start = (bf16[4,256,4096]{2,1,0:T(8,128)(2,1)}, bf16[4,256,4096]{2,1,0:T(8,128)(2,1)}, u32[]{:S(2)}, u32[]{:S(2)}) collective-permute-start(bf16[4,256,4096]{2,1,0:T(8,128)(2,1)} %refs_1_.7), channel_id=1, source_target_pairs={{0,2},{2,0},{4,6},{6,4},{8,10},{10,8},{12,14},{14,12},{1,3},{3,1},... | collective-permute-start | bytes 25165832 | tf_op jit(solution)/shard_map/ppermute | solution.py:194
  1.4 23.6 %copy-start.3 = (s32[8,16]{1,0:T(8,128)S(1)}, s32[8,16]{1,0:T(8,128)}, u32[]{:S(2)}) copy-start(s32[8,16]{1,0:T(8,128)} %param.15) | copy-start | bytes 1540
  1.4 12.6 %collective-permute-start.1 = (bf16[256,1024]{1,0:T(8,128)(2,1)S(1)}, bf16[256,1024]{1,0:T(8,128)(2,1)}, u32[]{:S(2)}, u32[]{:S(2)}) collective-permute-start(bf16[256,1024]{1,0:T(8,128)(2,1)S(1)} %pad_maximum_fusion.2), channel_id=1, source_target_pairs={{0,2},{2,0},{4,6},{6,4},{8,10},{10,8},{12,14},{14,12},{1,3},{3,1},... | collective-permute-start | bytes 1572872 | tf_op jit(solution)/shard_map/ppermute | solution.py:194
  2.0 14.4 %collective-permute-start.2 = (bf16[256,1024]{1,0:T(8,128)(2,1)S(1)}, bf16[256,1024]{1,0:T(8,128)(2,1)S(1)}, u32[]{:S(2)}, u32[]{:S(2)}) collective-permute-start(bf16[256,1024]{1,0:T(8,128)(2,1)S(1)} %pad_maximum_fusion.1.refs_20_), channel_id=1, source_target_pairs={{0,1},{1,0},{2,3},{3,2},{4,5},{5,4},{6,7},{7,6},{8,9},{9,8},{10,11... | collective-permute-start | bytes 1572872 | tf_op jit(solution)/shard_map/ppermute | solution.py:208
  2.6 17.3 %collective-permute-start.5 = (bf16[256,1024]{1,0:T(8,128)(2,1)S(1)}, bf16[256,1024]{1,0:T(8,128)(2,1)S(1)}, u32[]{:S(2)}, u32[]{:S(2)}) collective-permute-start(bf16[256,1024]{1,0:T(8,128)(2,1)S(1)} %pad_maximum_fusion.1.refs_20_), channel_id=1, source_target_pairs={{4,0},{6,2},{8,4},{10,6},{12,8},{14,10},{5,1},{7,3},{9,5},{11,7},{... | collective-permute-start | bytes 1572872 | tf_op jit(solution)/shard_map/ppermute | solution.py:199
  4.5 15.5 %collective-permute-start.7 = (bf16[256,1024]{1,0:T(8,128)(2,1)S(1)}, bf16[256,1024]{1,0:T(8,128)(2,1)S(1)}, u32[]{:S(2)}, u32[]{:S(2)}) collective-permute-start(bf16[256,1024]{1,0:T(8,128)(2,1)S(1)} %pad_maximum_fusion.1.refs_20_), channel_id=1, source_target_pairs={{0,4},{2,6},{4,8},{6,10},{8,12},{10,14},{1,5},{3,7},{5,9},{7,11},{... | collective-permute-start | bytes 1572872 | tf_op jit(solution)/shard_map/ppermute | solution.py:202
  14.0 17.0 %collective-permute-start.4 = (bf16[256,1024]{1,0:T(8,128)(2,1)}, bf16[256,1024]{1,0:T(8,128)(2,1)}, u32[]{:S(2)}, u32[]{:S(2)}) collective-permute-start(bf16[256,1024]{1,0:T(8,128)(2,1)} %collective-permute-done.1.refs_21_), channel_id=1, source_target_pairs={{4,0},{6,2},{8,4},{10,6},{12,8},{14,10},{5,1},{7,3},{9,5},{11,7},{... | collective-permute-start | bytes 1572872 | tf_op jit(solution)/shard_map/ppermute | solution.py:199
  16.4 15.9 %collective-permute-start.6 = (bf16[256,1024]{1,0:T(8,128)(2,1)}, bf16[256,1024]{1,0:T(8,128)(2,1)}, u32[]{:S(2)}, u32[]{:S(2)}) collective-permute-start(bf16[256,1024]{1,0:T(8,128)(2,1)} %collective-permute-done.1.refs_21_), channel_id=1, source_target_pairs={{0,4},{2,6},{4,8},{6,10},{8,12},{10,14},{1,5},{3,7},{5,9},{7,11},{... | collective-permute-start | bytes 1572872 | tf_op jit(solution)/shard_map/ppermute | solution.py:202
  21.1 23.2 %collective-permute-start.11 = (bf16[256,1024]{1,0:T(8,128)(2,1)}, bf16[256,1024]{1,0:T(8,128)(2,1)S(1)}, u32[]{:S(2)}, u32[]{:S(2)}) collective-permute-start(bf16[256,1024]{1,0:T(8,128)(2,1)} %get-tuple-element.26), channel_id=1, source_target_pairs={{4,0},{6,2},{8,4},{10,6},{12,8},{14,10},{5,1},{7,3},{9,5},{11,7},{... | collective-permute-start | bytes 1572872 | tf_op jit(solution)/shard_map/ppermute | solution.py:199
  24.1 15.1 %collective-permute-start.3 = (bf16[256,1024]{1,0:T(8,128)(2,1)}, bf16[256,1024]{1,0:T(8,128)(2,1)S(1)}, u32[]{:S(2)}, u32[]{:S(2)}) collective-permute-start(bf16[256,1024]{1,0:T(8,128)(2,1)} %collective-permute-done.1.refs_21_), channel_id=1, source_target_pairs={{0,1},{1,0},{2,3},{3,2},{4,5},{5,4},{6,7},{7,6},{8,9},{9,8},{10,11... | collective-permute-start | bytes 1572872 | tf_op jit(solution)/shard_map/ppermute | solution.py:208
  31.0 11.4 %collective-permute-start.17 = (f32[32,1152]{1,0:T(8,128)}, f32[32,1152]{1,0:T(8,128)S(1)}, u32[]{:S(2)}, u32[]{:S(2)}) collective-permute-start(f32[32,1152]{1,0:T(8,128)} %pad_maximum_fusion.3), channel_id=1, source_target_pairs={{0,1},{1,0},{2,3},{3,2},{4,5},{5,4},{6,7},{7,6},{8,9},{9,8},{10,11... | collective-permute-start | bytes 442376 | tf_op jit(solution)/shard_map/ppermute | solution.py:208
  32.3 16.2 %collective-permute-start.12 = (bf16[256,1024]{1,0:T(8,128)(2,1)}, bf16[256,1024]{1,0:T(8,128)(2,1)S(1)}, u32[]{:S(2)}, u32[]{:S(2)}) collective-permute-start(bf16[256,1024]{1,0:T(8,128)(2,1)} %get-tuple-element.25), channel_id=1, source_target_pairs={{0,4},{2,6},{4,8},{6,10},{8,12},{10,14},{1,5},{3,7},{5,9},{7,11},{... | collective-permute-start | bytes 1572872 | tf_op jit(solution)/shard_map/ppermute | solution.py:202
  39.3 24.4 %collective-permute-start.8 = (bf16[512,1024]{1,0:T(8,128)(2,1)S(1)}, bf16[512,1024]{1,0:T(8,128)(2,1)S(1)}, u32[]{:S(2)}, u32[]{:S(2)}) collective-permute-start(bf16[512,1024]{1,0:T(8,128)(2,1)S(1)} %after.3.refs_24_), channel_id=1, source_target_pairs={{0,1},{1,0},{2,3},{3,2},{4,5},{5,4},{6,7},{7,6},{8,9},{9,8},{10,11... | collective-permute-start | bytes 3145736 | tf_op jit(solution)/shard_map/ppermute | solution.py:208
  42.4 17.0 %collective-permute-start.10 = (bf16[256,1024]{1,0:T(8,128)(2,1)}, bf16[256,1024]{1,0:T(8,128)(2,1)S(1)}, u32[]{:S(2)}, u32[]{:S(2)}) collective-permute-start(bf16[256,1024]{1,0:T(8,128)(2,1)} %collective-permute-done.4), channel_id=1, source_target_pairs={{4,0},{6,2},{8,4},{10,6},{5,1},{7,3},{9,5},{11,7},{20,16},{22,18},... | collective-permute-start | bytes 1572872 | tf_op jit(solution)/shard_map/ppermute | solution.py:199
  44.4 16.6 %collective-permute-start.9 = (bf16[256,1024]{1,0:T(8,128)(2,1)}, bf16[256,1024]{1,0:T(8,128)(2,1)S(1)}, u32[]{:S(2)}, u32[]{:S(2)}) collective-permute-start(bf16[256,1024]{1,0:T(8,128)(2,1)} %collective-permute-done.6), channel_id=1, source_target_pairs={{4,8},{6,10},{8,12},{10,14},{5,9},{7,11},{9,13},{11,15},{20,24},{2... | collective-permute-start | bytes 1572872 | tf_op jit(solution)/shard_map/ppermute | solution.py:202
  48.5 33.1 %collective-permute-start.14 = (bf16[256,1024]{1,0:T(8,128)(2,1)S(1)}, bf16[256,1024]{1,0:T(8,128)(2,1)S(1)}, u32[]{:S(2)}, u32[]{:S(2)}) collective-permute-start(bf16[256,1024]{1,0:T(8,128)(2,1)S(1)} %collective-permute-done.11.refs_27_.refs_11_), channel_id=1, source_target_pairs={{4,0},{6,2},{8,4},{10,6},{5,1},{7,3},{9,5},{11,7},{20,16},{22,18},... | collective-permute-start | bytes 1572872 | tf_op jit(solution)/shard_map/ppermute | solution.py:199
  59.4 22.2 %collective-permute-start.15 = (bf16[256,1024]{1,0:T(8,128)(2,1)S(1)}, bf16[256,1024]{1,0:T(8,128)(2,1)S(1)}, u32[]{:S(2)}, u32[]{:S(2)}) collective-permute-start(bf16[256,1024]{1,0:T(8,128)(2,1)S(1)} %collective-permute-done.12.refs_30_.refs_12_), channel_id=1, source_target_pairs={{4,8},{6,10},{8,12},{10,14},{5,9},{7,11},{9,13},{11,15},{20,24},{2... | collective-permute-start | bytes 1572872 | tf_op jit(solution)/shard_map/ppermute | solution.py:202
  62.1 19.5 %collective-permute-start.13 = (bf16[256,1024]{1,0:T(8,128)(2,1)S(1)}, bf16[256,1024]{1,0:T(8,128)(2,1)S(1)}, u32[]{:S(2)}, u32[]{:S(2)}) collective-permute-start(bf16[256,1024]{1,0:T(8,128)(2,1)S(1)} %get-tuple-element.23), channel_id=1, source_target_pairs={{4,0},{6,2},{8,12},{10,14},{5,1},{7,3},{9,13},{11,15},{20,16},{22,... | collective-permute-start | bytes 1572872 | tf_op jit(solution)/shard_map/ppermute | solution.py:205
  63.7 27.7 %collective-permute-start.16 = (bf16[512,1024]{1,0:T(8,128)(2,1)S(1)}, bf16[512,1024]{1,0:T(8,128)(2,1)S(1)}, u32[]{:S(2)}, u32[]{:S(2)}) collective-permute-start(bf16[512,1024]{1,0:T(8,128)(2,1)S(1)} %pad_maximum_fusion.refs_26_), channel_id=1, source_target_pairs={{0,1},{1,0},{2,3},{3,2},{4,5},{5,4},{6,7},{7,6},{8,9},{9,8},{10,11... | collective-permute-start | bytes 3145736 | tf_op jit(solution)/shard_map/ppermute | solution.py:208
  63.8 21.3 %collective-permute-start.18 = (bf16[32,512]{1,0:T(8,128)(2,1)S(1)}, bf16[32,512]{1,0:T(8,128)(2,1)S(1)}, u32[]{:S(2)}, u32[]{:S(2)}) collective-permute-start(bf16[32,512]{1,0:T(8,128)(2,1)S(1)} %constant_dynamic-slice_fusion), channel_id=1, source_target_pairs={{0,2},{2,0},{4,6},{6,4},{8,10},{10,8},{12,14},{14,12},{1,3},{3,1},... | collective-permute-start | bytes 98312 | tf_op jit(solution)/shard_map/ppermute | solution.py:194
  81.8 21.3 %collective-permute-start.21 = (bf16[256,1024]{1,0:T(8,128)(2,1)S(1)}, bf16[256,1024]{1,0:T(8,128)(2,1)S(1)}, u32[]{:S(2)}, u32[]{:S(2)}) collective-permute-start(bf16[256,1024]{1,0:T(8,128)(2,1)S(1)} %select_select_fusion.refs_9_), channel_id=1, source_target_pairs={{0,1},{1,0},{2,3},{3,2},{4,5},{5,4},{6,7},{7,6},{8,9},{9,8},{10,11... | collective-permute-start | bytes 1572872 | tf_op jit(solution)/shard_map/ppermute | solution.py:208
  83.8 19.3 %collective-permute-start.22 = (bf16[256,1024]{1,0:T(8,128)(2,1)S(1)}, bf16[256,1024]{1,0:T(8,128)(2,1)S(1)}, u32[]{:S(2)}, u32[]{:S(2)}) collective-permute-start(bf16[256,1024]{1,0:T(8,128)(2,1)S(1)} %broadcast_select_fusion.2), channel_id=1, source_target_pairs={{4,0},{6,2},{8,12},{10,14},{5,1},{7,3},{9,13},{11,15},{20,16},{22,... | collective-permute-start | bytes 1572872 | tf_op jit(solution)/shard_map/ppermute | solution.py:205
  85.2 17.8 %collective-permute-start.19 = (bf16[2,32,512]{2,1,0:T(8,128)(2,1)S(1)}, bf16[2,32,512]{2,1,0:T(8,128)(2,1)S(1)}, u32[]{:S(2)}, u32[]{:S(2)}) collective-permute-start(bf16[2,32,512]{2,1,0:T(8,128)(2,1)S(1)} %after.5), channel_id=1, source_target_pairs={{0,0},{2,2},{4,4},{6,6},{1,8},{3,10},{5,12},{7,14},{8,1},{10,3},{1... | collective-permute-start | bytes 196616 | tf_op jit(solution)/shard_map/ppermute | solution.py:588
  90.2 12.9 %collective-permute-start.20 = (bf16[2,32,512]{2,1,0:T(8,128)(2,1)S(1)}, bf16[2,32,512]{2,1,0:T(8,128)(2,1)S(1)}, u32[]{:S(2)}, u32[]{:S(2)}) collective-permute-start(bf16[2,32,512]{2,1,0:T(8,128)(2,1)S(1)} %after.5), channel_id=1, source_target_pairs={{4,0},{6,2},{0,4},{2,6},{5,8},{7,10},{1,12},{3,14},{12,1},{14,3},{... | collective-permute-start | bytes 196616 | tf_op jit(solution)/shard_map/ppermute | solution.py:588
  110.3 10.1 %collective-permute-start.23 = (f32[32,640]{1,0:T(8,128)S(1)}, f32[32,640]{1,0:T(8,128)S(1)}, u32[]{:S(2)}, u32[]{:S(2)}) collective-permute-start(f32[32,640]{1,0:T(8,128)S(1)} %get-tuple-element.20), channel_id=1, source_target_pairs={{0,4},{2,6},{4,8},{6,10},{8,12},{10,14},{12,0},{14,2},{1,5},{3,7},... | collective-permute-start | bytes 245768 | tf_op jit(solution)/shard_map/ppermute | solution.py:652
  112.6 7.8 %collective-permute-start.24 = (f32[32,640]{1,0:T(8,128)S(1)}, f32[32,640]{1,0:T(8,128)S(1)}, u32[]{:S(2)}, u32[]{:S(2)}) collective-permute-start(f32[32,640]{1,0:T(8,128)S(1)} %get-tuple-element.21), channel_id=1, source_target_pairs={{0,8},{2,10},{4,12},{6,14},{8,0},{10,2},{12,4},{14,6},{1,9},{3,11}... | collective-permute-start | bytes 245768 | tf_op jit(solution)/shard_map/ppermute | solution.py:652
  114.6 11.4 %copy-start = (bf16[1024,2048]{1,0:T(8,128)(2,1)S(1)}, bf16[1024,2048]{1,0:T(8,128)(2,1)}, u32[]{:S(2)}) copy-start(bf16[1024,2048]{1,0:T(8,128)(2,1)} %weights.1) | copy-start | bytes 12582916
  114.6 7.5 %collective-permute-start.25 = (f32[32,640]{1,0:T(8,128)S(1)}, f32[32,640]{1,0:T(8,128)S(1)}, u32[]{:S(2)}, u32[]{:S(2)}) collective-permute-start(f32[32,640]{1,0:T(8,128)S(1)} %get-tuple-element.22), channel_id=1, source_target_pairs={{0,12},{2,14},{4,0},{6,2},{8,4},{10,6},{12,8},{14,10},{1,13},{3,15... | collective-permute-start | bytes 245768 | tf_op jit(solution)/shard_map/ppermute | solution.py:652
  122.5 6.3 %collective-permute-start.26 = (bf16[32,512]{1,0:T(8,128)(2,1)S(1)}, bf16[32,512]{1,0:T(8,128)(2,1)S(1)}, u32[]{:S(2)}, u32[]{:S(2)}) collective-permute-start(bf16[32,512]{1,0:T(8,128)(2,1)S(1)} %merge.1.ready), channel_id=1, source_target_pairs={{0,0},{1,8},{2,1},{3,9},{4,2},{5,10},{6,3},{7,11},{8,4},{9,12},{10... | collective-permute-start | bytes 98312 | tf_op jit(solution)/shard_map/ppermute | solution.py:664
  124.4 6.7 %collective-permute-start.27 = (bf16[32,512]{1,0:T(8,128)(2,1)S(1)}, bf16[32,512]{1,0:T(8,128)(2,1)S(1)}, u32[]{:S(2)}, u32[]{:S(2)}) collective-permute-start(bf16[32,512]{1,0:T(8,128)(2,1)S(1)} %merge.1.ready), channel_id=1, source_target_pairs={{0,1},{1,9},{2,0},{3,8},{4,3},{5,11},{6,2},{7,10},{8,5},{9,13},{10... | collective-permute-start | bytes 98312 | tf_op jit(solution)/shard_map/ppermute | solution.py:664
  131.9 5.0 %collective-permute-start.28 = (bf16[32,2048]{1,0:T(8,128)(2,1)S(1)}, bf16[32,2048]{1,0:T(8,128)(2,1)S(1)}, u32[]{:S(2)}, u32[]{:S(2)}) collective-permute-start(bf16[32,2048]{1,0:T(8,128)(2,1)S(1)} %output.1), channel_id=1, source_target_pairs={{0,16},{16,0},{1,17},{17,1},{2,18},{18,2},{3,19},{19,3},{4,20},{20... | collective-permute-start | bytes 393224 | tf_op jit(solution)/shard_map/ppermute | solution.py:666

commit v5 on v4

--- a/solution.py
+++ b/solution.py
@@ -320,7 +320,9 @@
 def project_kernel(wanted, amount, carried, info, *refs):
     refs = list(refs)
     count = len(wanted)
-    halves, refs = (refs[:count], refs[count : 2 * count]), refs[2 * count :]
+    wide = count > 8
+    held = 1 if wide else count
+    halves, refs = (refs[:held], refs[held : 2 * held]), refs[2 * held :]
     before = refs.pop(0) if carried else None
     sources, (total, token, weights, sems) = refs[:amount], refs[amount:]
 
@@ -334,7 +336,12 @@
     for half, blocks in enumerate(halves):
         rows = blocks[0].shape[1]
         here = pl.ds(half * rows, rows)
-        features = jnp.concatenate([block[0] for block in blocks], axis=1)
+        if wide:
+            places = [pl.multiple_of(info[1 + k] * PIECE, PIECE) for k in range(count)]
+            found = [blocks[0][0, :, pl.ds(place, PIECE)] for place in places]
+        else:
+            found = [block[0] for block in blocks]
+        features = jnp.concatenate(found, axis=1)
         part = jnp.dot(features, weights[...], preferred_element_type=jnp.float32)
         if carried:
             part = part + before[0, here, :]
@@ -348,6 +355,9 @@
     count = len(pieces)
     carried = before is not None
     blocks = [pl.BlockSpec((1, rows, PIECE), lambda i, info, k=k: (i, 0, info[1 + k])) for k in range(count)]
+    if count > 8:
+        blocks = [pl.BlockSpec((1, rows, width), lambda i, info: (i, 0, 0))]
+    held = len(blocks)
     sums = pl.BlockSpec((1, 2 * rows, columns), lambda i, info: (i, 0, 0))
     anywhere = pl.BlockSpec(memory_space=pl.ANY)
     return pl.pallas_call(
@@ -366,11 +376,11 @@
             jax.ShapeDtypeStruct((questions, 2 * rows, columns), jnp.float32),
             jax.ShapeDtypeStruct((8, 128), jnp.float32),
         ],
-        input_output_aliases={2 * count + 1: 0} if carried else {},
+        input_output_aliases={2 * held + 1: 0} if carried else {},
         compiler_params=pltpu.CompilerParams(vmem_limit_bytes=VMEM_LIMIT),
         cost_estimate=pl.CostEstimate(flops=1000, bytes_accessed=1000, transcendentals=0),
         name="project",
-    )(info, *([own_rows] * count), *([other_rows] * count), *([before] if carried else []), *arrays)
+    )(info, *([own_rows] * held), *([other_rows] * held), *([before] if carried else []), *arrays)
 
 
 def attend_kernel(wanted, amount, info, *refs):

time: 138 us -> 138 us (level)
  no operation moved by 1% of the time
where the time goes in v5:
time: 138 us; the launch traced here: 137 us
  starting transfers between devices  52.5 us (38%)
  Pallas kernels  41.5 us (30%)
  waiting for transfers between devices  32 us (23%)
  other arithmetic  6.16 us (4%)
  matrix products  3.01 us (2%)
  local copies, waits for them, and re-layouts  1.72 us (1%)
    pallas_call x2, Pallas kernels, project_pieces(): pl.pallas_call(functools.partial(project_kernel, wanted, len(arrays), car...  29 us
    ppermute x5, starting transfers between devices, right(): return lax.ppermute(value, 'pb', line(1, sources))  16.4 us
    ppermute x5, waiting for transfers between devices, left(): return lax.ppermute(value, 'pb', line(-1, sources))  14.2 us
    ppermute x5, starting transfers between devices, left(): return lax.ppermute(value, 'pb', line(-1, sources))  11.1 us
    pallas_call x2, Pallas kernels, attend_last(): pl.pallas_call(functools.partial(attend_kernel, wanted, len(arrays)), gri...  11 us
    ppermute x3, starting transfers between devices, gathered_shards(): arrived.append(lax.ppermute(part, 'pb', turn))  6.34 us
    ppermute x2, starting transfers between devices, spread_queries(): spread.append(lax.ppermute(pair, ('pb', 'fsdp'), sends))  6.12 us
    ppermute x2, waiting for transfers between devices, gathered_shards(): received.append(lax.ppermute(attention, ('pb', 'fsdp'), sends))  4.84 us
  transfers between devices with their start and end apart: 29, of which 11 were waited for; matrix products, arithmetic and copies ran while one was open for 7% of the time, Pallas kernels for 24%

profile of v5, /device:TPU:10, one launch (start us, length us, event | category | flops | bytes accessed | tf_op | source)
XLA Modules:
  0.0 137.4 jit_solution(5106406077770513765)
XLA Ops:
  0.0 1.3 constant_dynamic-slice_fusion.1
  1.4 0.5 collective-permute-start.1
  2.0 0.6 collective-permute-start.2
  2.6 1.9 %collective-permute-start.5 = (bf16[256,1024]{1,0:T(8,128)(2,1)S(1)}, bf16[256,1024]{1,0:T(8,128)(2,1)S(1)}, u32[]{:S(2)}, u32[]{:S(2)}) collective-permute-start(bf16[256,1024]{1,0:T(8,128)(2,1)S(1)} %pad_maximum_fusion.1.refs_2_), channel_id=1, source_target_pairs={{4,0},{6,2},{8,4},{10,6},{12,8},{14,10},{5,1},{7,3},{9,5},{11,7},{... | collective-permute-start | bytes 1572872 | tf_op jit(solution)/shard_map/ppermute | solution.py:199
  4.5 3.9 %collective-permute-start.7 = (bf16[256,1024]{1,0:T(8,128)(2,1)S(1)}, bf16[256,1024]{1,0:T(8,128)(2,1)S(1)}, u32[]{:S(2)}, u32[]{:S(2)}) collective-permute-start(bf16[256,1024]{1,0:T(8,128)(2,1)S(1)} %pad_maximum_fusion.1.refs_2_), channel_id=1, source_target_pairs={{0,4},{2,6},{4,8},{6,10},{8,12},{10,14},{1,5},{3,7},{5,9},{7,11},{... | collective-permute-start | bytes 1572872 | tf_op jit(solution)/shard_map/ppermute | solution.py:202
  8.6 3.0 %fusion.3 = f32[32,1024]{1,0:T(8,128)S(1)} fusion(bf16[2048,1024]{1,0:T(8,128)(2,1)} %param.10, bf16[1,32,2048]{2,1,0:T(8,128)(2,1)S(1)} %copy-done.1, f32[2048]{0:T(1024)S(1)} %convert_element_type.26), kind=kOutput, calls=%fused_computation.18 | convolution fusion | flops 134414336 | bytes 4464640 | tf_op jit(solution)/shard_map/dot_general | solution.py:584
  11.6 2.4 %collective-permute-done.1.refs_3_ = bf16[256,1024]{1,0:T(8,128)(2,1)} collective-permute-done((bf16[256,1024]{1,0:T(8,128)(2,1)S(1)}, bf16[256,1024]{1,0:T(8,128)(2,1)}, u32[]{:S(2)}, u32[]{:S(2)}) %collective-permute-start.1) | collective-permute-done | bytes 524320 | tf_op jit(solution)/shard_map/ppermute | solution.py:194
  14.0 2.3 %collective-permute-start.4 = (bf16[256,1024]{1,0:T(8,128)(2,1)}, bf16[256,1024]{1,0:T(8,128)(2,1)}, u32[]{:S(2)}, u32[]{:S(2)}) collective-permute-start(bf16[256,1024]{1,0:T(8,128)(2,1)} %collective-permute-done.1.refs_3_), channel_id=1, source_target_pairs={{4,0},{6,2},{8,4},{10,6},{12,8},{14,10},{5,1},{7,3},{9,5},{11,7},{... | collective-permute-start | bytes 1572872 | tf_op jit(solution)/shard_map/ppermute | solution.py:199
  16.4 3.5 %collective-permute-start.6 = (bf16[256,1024]{1,0:T(8,128)(2,1)}, bf16[256,1024]{1,0:T(8,128)(2,1)}, u32[]{:S(2)}, u32[]{:S(2)}) collective-permute-start(bf16[256,1024]{1,0:T(8,128)(2,1)} %collective-permute-done.1.refs_3_), channel_id=1, source_target_pairs={{0,4},{2,6},{4,8},{6,10},{8,12},{10,14},{1,5},{3,7},{5,9},{7,11},{... | collective-permute-start | bytes 1572872 | tf_op jit(solution)/shard_map/ppermute | solution.py:202
  20.0 1.1 broadcast_select_fusion
  21.1 3.0 %collective-permute-start.11 = (bf16[256,1024]{1,0:T(8,128)(2,1)}, bf16[256,1024]{1,0:T(8,128)(2,1)S(1)}, u32[]{:S(2)}, u32[]{:S(2)}) collective-permute-start(bf16[256,1024]{1,0:T(8,128)(2,1)} %get-tuple-element.26), channel_id=1, source_target_pairs={{4,0},{6,2},{8,4},{10,6},{12,8},{14,10},{5,1},{7,3},{9,5},{11,7},{... | collective-permute-start | bytes 1572872 | tf_op jit(solution)/shard_map/ppermute | solution.py:199
  24.1 0.9 collective-permute-start.3
  25.1 0.7 pad_maximum_fusion.3
  25.8 5.2 %collective-permute-done.4 = bf16[256,1024]{1,0:T(8,128)(2,1)} collective-permute-done((bf16[256,1024]{1,0:T(8,128)(2,1)}, bf16[256,1024]{1,0:T(8,128)(2,1)}, u32[]{:S(2)}, u32[]{:S(2)}) %collective-permute-start.4) | collective-permute-done | bytes 524320 | tf_op jit(solution)/shard_map/ppermute | solution.py:199
  31.0 0.5 collective-permute-start.17
  31.8 0.5 collective-permute-done.6
  32.3 3.5 %collective-permute-start.12 = (bf16[256,1024]{1,0:T(8,128)(2,1)}, bf16[256,1024]{1,0:T(8,128)(2,1)S(1)}, u32[]{:S(2)}, u32[]{:S(2)}) collective-permute-start(bf16[256,1024]{1,0:T(8,128)(2,1)} %get-tuple-element.25), channel_id=1, source_target_pairs={{0,4},{2,6},{4,8},{6,10},{8,12},{10,14},{1,5},{3,7},{5,9},{7,11},{... | collective-permute-start | bytes 1572872 | tf_op jit(solution)/shard_map/ppermute | solution.py:202
  35.8 1.6 %maximum_select_fusion.refs_0_ = bf16[512,1024]{1,0:T(8,128)(2,1)S(1)} fusion(bf16[256,1024]{1,0:T(8,128)(2,1)S(1)} %collective-permute-done.5.refs_11_, bf16[256,1024]{1,0:T(8,128)(2,1)} %collective-permute-done.4, bf16[256,1024]{1,0:T(8,128)(2,1)S(1)} %collective-permute-done.7.refs_10_, bf16[256,1024]{1,0:T(8,128)(2,1)} %collective-permute-done.6, pred[]{:T(512)S(6)} %lt.34), kind=kLoop, calls=%fused_computation | loop fusion | flops 4718592 | bytes 3145729 | tf_op jit(solution)/shard_map/jit(_where)/select_n | solution.py:223
  37.4 1.8 %collective-permute-done.3.refs_1_.refs_5_ = bf16[256,1024]{1,0:T(8,128)(2,1)S(1)} collective-permute-done((bf16[256,1024]{1,0:T(8,128)(2,1)}, bf16[256,1024]{1,0:T(8,128)(2,1)S(1)}, u32[]{:S(2)}, u32[]{:S(2)}) %collective-permute-start.3) | collective-permute-done | bytes 524320 | tf_op jit(solution)/shard_map/ppermute | solution.py:208
  39.5 2.9 %collective-permute-done.17 = f32[32,1152]{1,0:T(8,128)S(1)} collective-permute-done((f32[32,1152]{1,0:T(8,128)}, f32[32,1152]{1,0:T(8,128)S(1)}, u32[]{:S(2)}, u32[]{:S(2)}) %collective-permute-start.17) | collective-permute-done | bytes 147488 | tf_op jit(solution)/shard_map/ppermute | solution.py:208
  42.4 1.9 %collective-permute-start.10 = (bf16[256,1024]{1,0:T(8,128)(2,1)}, bf16[256,1024]{1,0:T(8,128)(2,1)S(1)}, u32[]{:S(2)}, u32[]{:S(2)}) collective-permute-start(bf16[256,1024]{1,0:T(8,128)(2,1)} %collective-permute-done.4), channel_id=1, source_target_pairs={{4,0},{6,2},{8,4},{10,6},{5,1},{7,3},{9,5},{11,7},{20,16},{22,18},... | collective-permute-start | bytes 1572872 | tf_op jit(solution)/shard_map/ppermute | solution.py:199
  44.4 4.0 %collective-permute-start.9 = (bf16[256,1024]{1,0:T(8,128)(2,1)}, bf16[256,1024]{1,0:T(8,128)(2,1)S(1)}, u32[]{:S(2)}, u32[]{:S(2)}) collective-permute-start(bf16[256,1024]{1,0:T(8,128)(2,1)} %collective-permute-done.6), channel_id=1, source_target_pairs={{4,8},{6,10},{8,12},{10,14},{5,9},{7,11},{9,13},{11,15},{20,24},{2... | collective-permute-start | bytes 1572872 | tf_op jit(solution)/shard_map/ppermute | solution.py:202
  48.5 1.9 %collective-permute-start.14 = (bf16[256,1024]{1,0:T(8,128)(2,1)S(1)}, bf16[256,1024]{1,0:T(8,128)(2,1)S(1)}, u32[]{:S(2)}, u32[]{:S(2)}) collective-permute-start(bf16[256,1024]{1,0:T(8,128)(2,1)S(1)} %collective-permute-done.11.refs_9_.refs_11_), channel_id=1, source_target_pairs={{4,0},{6,2},{8,4},{10,6},{5,1},{7,3},{9,5},{11,7},{20,16},{22,18},... | collective-permute-start | bytes 1572872 | tf_op jit(solution)/shard_map/ppermute | solution.py:199
  50.4 9.0 %collective-permute-done.10 = bf16[256,1024]{1,0:T(8,128)(2,1)S(1)} collective-permute-done((bf16[256,1024]{1,0:T(8,128)(2,1)}, bf16[256,1024]{1,0:T(8,128)(2,1)S(1)}, u32[]{:S(2)}, u32[]{:S(2)}) %collective-permute-start.10) | collective-permute-done | bytes 524320 | tf_op jit(solution)/shard_map/ppermute | solution.py:199
  59.4 1.6 %collective-permute-start.15 = (bf16[256,1024]{1,0:T(8,128)(2,1)S(1)}, bf16[256,1024]{1,0:T(8,128)(2,1)S(1)}, u32[]{:S(2)}, u32[]{:S(2)}) collective-permute-start(bf16[256,1024]{1,0:T(8,128)(2,1)S(1)} %collective-permute-done.12.refs_12_), channel_id=1, source_target_pairs={{4,8},{6,10},{8,12},{10,14},{5,9},{7,11},{9,13},{11,15},{20,24},{2... | collective-permute-start | bytes 1572872 | tf_op jit(solution)/shard_map/ppermute | solution.py:202
  61.0 1.2 broadcast_select_fusion.3
  62.1 1.3 collective-permute-start.13
  63.9 17.4 %project.2 = (f32[4,512,1024]{2,1,0:T(8,128)}, f32[8,128]{1,0:T(8,128)S(1)}) custom-call(s32[11]{0:T(128)S(1)} %concatenate.36.info, bf16[4,256,4096]{2,1,0:T(8,128)(2,1)} %refs_1_.5, bf16[4,256,4096]{2,1,0:T(8,128)(2,1)} %collective-permute-done.refs_1_.refs_4_.refs_5_.refs_6_.refs_7_.refs_2_.refs_3_, bf16[256,1024]{1,0:T(8,128)(2,1)S(1)} %pad_maximum_fusion.1.refs_2_, ...), custom_call_target="tpu_custom_call" | custom-call | flops 1000 | bytes 1000 | tf_op jit(solution)/shard_map/project/pallas_call | solution.py:363
  81.5 2.0 %collective-permute-start.21 = (bf16[256,1024]{1,0:T(8,128)(2,1)S(1)}, bf16[256,1024]{1,0:T(8,128)(2,1)S(1)}, u32[]{:S(2)}, u32[]{:S(2)}) collective-permute-start(bf16[256,1024]{1,0:T(8,128)(2,1)S(1)} %select_select_fusion.refs_9_), channel_id=1, source_target_pairs={{0,1},{1,0},{2,3},{3,2},{4,5},{5,4},{6,7},{7,6},{8,9},{9,8},{10,11... | collective-permute-start | bytes 1572872 | tf_op jit(solution)/shard_map/ppermute | solution.py:208
  83.5 1.3 collective-permute-start.22
  84.9 4.9 %collective-permute-start.19 = (bf16[2,32,512]{2,1,0:T(8,128)(2,1)S(1)}, bf16[2,32,512]{2,1,0:T(8,128)(2,1)S(1)}, u32[]{:S(2)}, u32[]{:S(2)}) collective-permute-start(bf16[2,32,512]{2,1,0:T(8,128)(2,1)S(1)} %after.5), channel_id=1, source_target_pairs={{0,0},{2,2},{4,4},{6,6},{1,8},{3,10},{5,12},{7,14},{8,1},{10,3},{1... | collective-permute-start | bytes 196616 | tf_op jit(solution)/shard_map/ppermute | solution.py:598
  89.9 1.2 collective-permute-start.20
  91.1 11.6 %project.3 = (f32[4,512,1024]{2,1,0:T(8,128)}, f32[8,128]{1,0:T(8,128)}) custom-call(s32[5]{0:T(128)S(1)} %concatenate.35.info, bf16[4,256,4096]{2,1,0:T(8,128)(2,1)} %refs_1_.5, bf16[4,256,4096]{2,1,0:T(8,128)(2,1)} %refs_1_.5, bf16[4,256,4096]{2,1,0:T(8,128)(2,1)} %refs_1_.5, bf16[4,256,4096]{2,1,0:T(8,128)(2,1)} %refs_1_.5, ...), custom_call_target="tpu_custom_call", output_to_operand_aliasing={{0}: (9, {})} | custom-call | flops 1000 | bytes 1000 | tf_op jit(solution)/shard_map/project/pallas_call | solution.py:363
  102.8 7.2 %attend.2 = (f32[32,640]{1,0:T(8,128)S(1)}, f32[32,640]{1,0:T(8,128)S(1)}, f32[32,640]{1,0:T(8,128)S(1)}) custom-call(s32[3]{0:T(128)S(1)} %pad_add_fusion.1.info, bf16[4,256,4096]{2,1,0:T(8,128)(2,1)} %refs_1_.5, bf16[4,256,4096]{2,1,0:T(8,128)(2,1)} %refs_1_.5, ...), custom_call_target="tpu_custom_call" | custom-call | flops 2013265920 | bytes 7864320 | tf_op jit(solution)/shard_map/attend/pallas_call | solution.py:470
  110.0 2.4 %collective-permute-start.23 = (f32[32,640]{1,0:T(8,128)S(1)}, f32[32,640]{1,0:T(8,128)S(1)}, u32[]{:S(2)}, u32[]{:S(2)}) collective-permute-start(f32[32,640]{1,0:T(8,128)S(1)} %get-tuple-element.20), channel_id=1, source_target_pairs={{0,4},{2,6},{4,8},{6,10},{8,12},{10,14},{12,0},{14,2},{1,5},{3,7},... | collective-permute-start | bytes 245768 | tf_op jit(solution)/shard_map/ppermute | solution.py:662
  112.4 2.0 %collective-permute-start.24 = (f32[32,640]{1,0:T(8,128)S(1)}, f32[32,640]{1,0:T(8,128)S(1)}, u32[]{:S(2)}, u32[]{:S(2)}) collective-permute-start(f32[32,640]{1,0:T(8,128)S(1)} %get-tuple-element.21), channel_id=1, source_target_pairs={{0,8},{2,10},{4,12},{6,14},{8,0},{10,2},{12,4},{14,6},{1,9},{3,11}... | collective-permute-start | bytes 245768 | tf_op jit(solution)/shard_map/ppermute | solution.py:662
  114.4 1.9 %collective-permute-start.25 = (f32[32,640]{1,0:T(8,128)S(1)}, f32[32,640]{1,0:T(8,128)S(1)}, u32[]{:S(2)}, u32[]{:S(2)}) collective-permute-start(f32[32,640]{1,0:T(8,128)S(1)} %get-tuple-element.22), channel_id=1, source_target_pairs={{0,12},{2,14},{4,0},{6,2},{8,4},{10,6},{12,8},{14,10},{1,13},{3,15... | collective-permute-start | bytes 245768 | tf_op jit(solution)/shard_map/ppermute | solution.py:662
  116.3 3.8 %attend.3.refs_3_ = f32[32,640]{1,0:T(8,128)S(1)} custom-call(s32[3]{0:T(128)S(1)} %pad_add_fusion.1.info, bf16[4,256,4096]{2,1,0:T(8,128)(2,1)} %refs_1_.5, bf16[4,256,4096]{2,1,0:T(8,128)(2,1)} %refs_1_.5, bf16[4,256,4096]{2,1,0:T(8,128)(2,1)} %collective-permute-done.refs_1_.refs_4_.refs_5_.refs_6_.refs_7_.refs_2_.refs_3_, ...), custom_call_target="tpu_custom_call" | custom-call | flops 671088640 | bytes 2621440 | tf_op jit(solution)/shard_map/attend/pallas_call | solution.py:470
  120.2 1.7 %collective-permute-done.25.refs_2_ = f32[32,640]{1,0:T(8,128)S(1)} collective-permute-done((f32[32,640]{1,0:T(8,128)S(1)}, f32[32,640]{1,0:T(8,128)S(1)}, u32[]{:S(2)}, u32[]{:S(2)}) %collective-permute-start.25) | collective-permute-done | bytes 81952 | tf_op jit(solution)/shard_map/ppermute | solution.py:662
  121.9 0.5 merge.1.ready
  122.3 1.9 %collective-permute-start.26 = (bf16[32,512]{1,0:T(8,128)(2,1)S(1)}, bf16[32,512]{1,0:T(8,128)(2,1)S(1)}, u32[]{:S(2)}, u32[]{:S(2)}) collective-permute-start(bf16[32,512]{1,0:T(8,128)(2,1)S(1)} %merge.1.ready), channel_id=1, source_target_pairs={{0,0},{1,8},{2,1},{3,9},{4,2},{5,10},{6,3},{7,11},{8,4},{9,12},{10... | collective-permute-start | bytes 98312 | tf_op jit(solution)/shard_map/ppermute | solution.py:674
  124.3 1.5 %collective-permute-start.27 = (bf16[32,512]{1,0:T(8,128)(2,1)S(1)}, bf16[32,512]{1,0:T(8,128)(2,1)S(1)}, u32[]{:S(2)}, u32[]{:S(2)}) collective-permute-start(bf16[32,512]{1,0:T(8,128)(2,1)S(1)} %merge.1.ready), channel_id=1, source_target_pairs={{0,1},{1,9},{2,0},{3,8},{4,3},{5,11},{6,2},{7,10},{8,5},{9,13},{10... | collective-permute-start | bytes 98312 | tf_op jit(solution)/shard_map/ppermute | solution.py:674
  126.1 2.6 %collective-permute-done.26.first = bf16[32,512]{1,0:T(8,128)(2,1)S(1)} collective-permute-done((bf16[32,512]{1,0:T(8,128)(2,1)S(1)}, bf16[32,512]{1,0:T(8,128)(2,1)S(1)}, u32[]{:S(2)}, u32[]{:S(2)}) %collective-permute-start.26) | collective-permute-done | bytes 32800 | tf_op jit(solution)/shard_map/ppermute | solution.py:674
  128.7 2.2 %collective-permute-done.27.second = bf16[32,512]{1,0:T(8,128)(2,1)S(1)} collective-permute-done((bf16[32,512]{1,0:T(8,128)(2,1)S(1)}, bf16[32,512]{1,0:T(8,128)(2,1)S(1)}, u32[]{:S(2)}, u32[]{:S(2)}) %collective-permute-start.27) | collective-permute-done | bytes 32800 | tf_op jit(solution)/shard_map/ppermute | solution.py:674
  130.9 0.8 output.1
  131.8 1.5 %collective-permute-start.28 = (bf16[32,2048]{1,0:T(8,128)(2,1)S(1)}, bf16[32,2048]{1,0:T(8,128)(2,1)S(1)}, u32[]{:S(2)}, u32[]{:S(2)}) collective-permute-start(bf16[32,2048]{1,0:T(8,128)(2,1)S(1)} %output.1), channel_id=1, source_target_pairs={{0,16},{16,0},{1,17},{17,1},{2,18},{18,2},{3,19},{19,3},{4,20},{20... | collective-permute-start | bytes 393224 | tf_op jit(solution)/shard_map/ppermute | solution.py:676
  133.3 3.4 %collective-permute-done.28 = bf16[32,2048]{1,0:T(8,128)(2,1)S(1)} collective-permute-done((bf16[32,2048]{1,0:T(8,128)(2,1)S(1)}, bf16[32,2048]{1,0:T(8,128)(2,1)S(1)}, u32[]{:S(2)}, u32[]{:S(2)}) %collective-permute-start.28) | collective-permute-done | bytes 131104 | tf_op jit(solution)/shard_map/ppermute | solution.py:676
  136.7 0.7 fusion.2
  (58 shorter events, 2.2 us)
Async XLA Ops:
  0.0 8.5 %copy-start.2 = (bf16[2048]{0:T(1024)(128)(2,1)S(1)}, bf16[2048]{0:T(1024)(128)(2,1)}, u32[]{:S(2)}) copy-start(bf16[2048]{0:T(1024)(128)(2,1)} %param.9) | copy-start | bytes 12292
  0.0 8.5 %copy-start.1 = (bf16[1,32,2048]{2,1,0:T(8,128)(2,1)S(1)}, bf16[1,32,2048]{2,1,0:T(8,128)(2,1)}, u32[]{:S(2)}) copy-start(bf16[1,32,2048]{2,1,0:T(8,128)(2,1)} %param.8) | copy-start | bytes 393220
  0.0 63.8 %collective-permute-start = (bf16[4,256,4096]{2,1,0:T(8,128)(2,1)}, bf16[4,256,4096]{2,1,0:T(8,128)(2,1)}, u32[]{:S(2)}, u32[]{:S(2)}) collective-permute-start(bf16[4,256,4096]{2,1,0:T(8,128)(2,1)} %refs_1_.5), channel_id=1, source_target_pairs={{0,2},{2,0},{4,6},{6,4},{8,10},{10,8},{12,14},{14,12},{1,3},{3,1},... | collective-permute-start | bytes 25165832 | tf_op jit(solution)/shard_map/ppermute | solution.py:194
  1.4 23.6 %copy-start.3 = (s32[8,16]{1,0:T(8,128)S(1)}, s32[8,16]{1,0:T(8,128)}, u32[]{:S(2)}) copy-start(s32[8,16]{1,0:T(8,128)} %param.15) | copy-start | bytes 1540
  1.4 12.6 %collective-permute-start.1 = (bf16[256,1024]{1,0:T(8,128)(2,1)S(1)}, bf16[256,1024]{1,0:T(8,128)(2,1)}, u32[]{:S(2)}, u32[]{:S(2)}) collective-permute-start(bf16[256,1024]{1,0:T(8,128)(2,1)S(1)} %pad_maximum_fusion.2), channel_id=1, source_target_pairs={{0,2},{2,0},{4,6},{6,4},{8,10},{10,8},{12,14},{14,12},{1,3},{3,1},... | collective-permute-start | bytes 1572872 | tf_op jit(solution)/shard_map/ppermute | solution.py:194
  2.0 14.4 %collective-permute-start.2 = (bf16[256,1024]{1,0:T(8,128)(2,1)S(1)}, bf16[256,1024]{1,0:T(8,128)(2,1)S(1)}, u32[]{:S(2)}, u32[]{:S(2)}) collective-permute-start(bf16[256,1024]{1,0:T(8,128)(2,1)S(1)} %pad_maximum_fusion.1.refs_2_), channel_id=1, source_target_pairs={{0,1},{1,0},{2,3},{3,2},{4,5},{5,4},{6,7},{7,6},{8,9},{9,8},{10,11... | collective-permute-start | bytes 1572872 | tf_op jit(solution)/shard_map/ppermute | solution.py:208
  2.6 17.3 %collective-permute-start.5 = (bf16[256,1024]{1,0:T(8,128)(2,1)S(1)}, bf16[256,1024]{1,0:T(8,128)(2,1)S(1)}, u32[]{:S(2)}, u32[]{:S(2)}) collective-permute-start(bf16[256,1024]{1,0:T(8,128)(2,1)S(1)} %pad_maximum_fusion.1.refs_2_), channel_id=1, source_target_pairs={{4,0},{6,2},{8,4},{10,6},{12,8},{14,10},{5,1},{7,3},{9,5},{11,7},{... | collective-permute-start | bytes 1572872 | tf_op jit(solution)/shard_map/ppermute | solution.py:199
  4.5 15.5 %collective-permute-start.7 = (bf16[256,1024]{1,0:T(8,128)(2,1)S(1)}, bf16[256,1024]{1,0:T(8,128)(2,1)S(1)}, u32[]{:S(2)}, u32[]{:S(2)}) collective-permute-start(bf16[256,1024]{1,0:T(8,128)(2,1)S(1)} %pad_maximum_fusion.1.refs_2_), channel_id=1, source_target_pairs={{0,4},{2,6},{4,8},{6,10},{8,12},{10,14},{1,5},{3,7},{5,9},{7,11},{... | collective-permute-start | bytes 1572872 | tf_op jit(solution)/shard_map/ppermute | solution.py:202
  14.0 17.0 %collective-permute-start.4 = (bf16[256,1024]{1,0:T(8,128)(2,1)}, bf16[256,1024]{1,0:T(8,128)(2,1)}, u32[]{:S(2)}, u32[]{:S(2)}) collective-permute-start(bf16[256,1024]{1,0:T(8,128)(2,1)} %collective-permute-done.1.refs_3_), channel_id=1, source_target_pairs={{4,0},{6,2},{8,4},{10,6},{12,8},{14,10},{5,1},{7,3},{9,5},{11,7},{... | collective-permute-start | bytes 1572872 | tf_op jit(solution)/shard_map/ppermute | solution.py:199
  16.4 15.9 %collective-permute-start.6 = (bf16[256,1024]{1,0:T(8,128)(2,1)}, bf16[256,1024]{1,0:T(8,128)(2,1)}, u32[]{:S(2)}, u32[]{:S(2)}) collective-permute-start(bf16[256,1024]{1,0:T(8,128)(2,1)} %collective-permute-done.1.refs_3_), channel_id=1, source_target_pairs={{0,4},{2,6},{4,8},{6,10},{8,12},{10,14},{1,5},{3,7},{5,9},{7,11},{... | collective-permute-start | bytes 1572872 | tf_op jit(solution)/shard_map/ppermute | solution.py:202
  21.1 23.2 %collective-permute-start.11 = (bf16[256,1024]{1,0:T(8,128)(2,1)}, bf16[256,1024]{1,0:T(8,128)(2,1)S(1)}, u32[]{:S(2)}, u32[]{:S(2)}) collective-permute-start(bf16[256,1024]{1,0:T(8,128)(2,1)} %get-tuple-element.26), channel_id=1, source_target_pairs={{4,0},{6,2},{8,4},{10,6},{12,8},{14,10},{5,1},{7,3},{9,5},{11,7},{... | collective-permute-start | bytes 1572872 | tf_op jit(solution)/shard_map/ppermute | solution.py:199
  24.1 15.1 %collective-permute-start.3 = (bf16[256,1024]{1,0:T(8,128)(2,1)}, bf16[256,1024]{1,0:T(8,128)(2,1)S(1)}, u32[]{:S(2)}, u32[]{:S(2)}) collective-permute-start(bf16[256,1024]{1,0:T(8,128)(2,1)} %collective-permute-done.1.refs_3_), channel_id=1, source_target_pairs={{0,1},{1,0},{2,3},{3,2},{4,5},{5,4},{6,7},{7,6},{8,9},{9,8},{10,11... | collective-permute-start | bytes 1572872 | tf_op jit(solution)/shard_map/ppermute | solution.py:208
  31.0 11.4 %collective-permute-start.17 = (f32[32,1152]{1,0:T(8,128)}, f32[32,1152]{1,0:T(8,128)S(1)}, u32[]{:S(2)}, u32[]{:S(2)}) collective-permute-start(f32[32,1152]{1,0:T(8,128)} %pad_maximum_fusion.3), channel_id=1, source_target_pairs={{0,1},{1,0},{2,3},{3,2},{4,5},{5,4},{6,7},{7,6},{8,9},{9,8},{10,11... | collective-permute-start | bytes 442376 | tf_op jit(solution)/shard_map/ppermute | solution.py:208
  32.3 16.2 %collective-permute-start.12 = (bf16[256,1024]{1,0:T(8,128)(2,1)}, bf16[256,1024]{1,0:T(8,128)(2,1)S(1)}, u32[]{:S(2)}, u32[]{:S(2)}) collective-permute-start(bf16[256,1024]{1,0:T(8,128)(2,1)} %get-tuple-element.25), channel_id=1, source_target_pairs={{0,4},{2,6},{4,8},{6,10},{8,12},{10,14},{1,5},{3,7},{5,9},{7,11},{... | collective-permute-start | bytes 1572872 | tf_op jit(solution)/shard_map/ppermute | solution.py:202
  39.3 24.4 %collective-permute-start.8 = (bf16[512,1024]{1,0:T(8,128)(2,1)S(1)}, bf16[512,1024]{1,0:T(8,128)(2,1)S(1)}, u32[]{:S(2)}, u32[]{:S(2)}) collective-permute-start(bf16[512,1024]{1,0:T(8,128)(2,1)S(1)} %after.3.refs_6_), channel_id=1, source_target_pairs={{0,1},{1,0},{2,3},{3,2},{4,5},{5,4},{6,7},{7,6},{8,9},{9,8},{10,11... | collective-permute-start | bytes 3145736 | tf_op jit(solution)/shard_map/ppermute | solution.py:208
  42.4 17.0 %collective-permute-start.10 = (bf16[256,1024]{1,0:T(8,128)(2,1)}, bf16[256,1024]{1,0:T(8,128)(2,1)S(1)}, u32[]{:S(2)}, u32[]{:S(2)}) collective-permute-start(bf16[256,1024]{1,0:T(8,128)(2,1)} %collective-permute-done.4), channel_id=1, source_target_pairs={{4,0},{6,2},{8,4},{10,6},{5,1},{7,3},{9,5},{11,7},{20,16},{22,18},... | collective-permute-start | bytes 1572872 | tf_op jit(solution)/shard_map/ppermute | solution.py:199
  44.4 16.6 %collective-permute-start.9 = (bf16[256,1024]{1,0:T(8,128)(2,1)}, bf16[256,1024]{1,0:T(8,128)(2,1)S(1)}, u32[]{:S(2)}, u32[]{:S(2)}) collective-permute-start(bf16[256,1024]{1,0:T(8,128)(2,1)} %collective-permute-done.6), channel_id=1, source_target_pairs={{4,8},{6,10},{8,12},{10,14},{5,9},{7,11},{9,13},{11,15},{20,24},{2... | collective-permute-start | bytes 1572872 | tf_op jit(solution)/shard_map/ppermute | solution.py:202
  48.5 32.8 %collective-permute-start.14 = (bf16[256,1024]{1,0:T(8,128)(2,1)S(1)}, bf16[256,1024]{1,0:T(8,128)(2,1)S(1)}, u32[]{:S(2)}, u32[]{:S(2)}) collective-permute-start(bf16[256,1024]{1,0:T(8,128)(2,1)S(1)} %collective-permute-done.11.refs_9_.refs_11_), channel_id=1, source_target_pairs={{4,0},{6,2},{8,4},{10,6},{5,1},{7,3},{9,5},{11,7},{20,16},{22,18},... | collective-permute-start | bytes 1572872 | tf_op jit(solution)/shard_map/ppermute | solution.py:199
  59.4 21.9 %collective-permute-start.15 = (bf16[256,1024]{1,0:T(8,128)(2,1)S(1)}, bf16[256,1024]{1,0:T(8,128)(2,1)S(1)}, u32[]{:S(2)}, u32[]{:S(2)}) collective-permute-start(bf16[256,1024]{1,0:T(8,128)(2,1)S(1)} %collective-permute-done.12.refs_12_), channel_id=1, source_target_pairs={{4,8},{6,10},{8,12},{10,14},{5,9},{7,11},{9,13},{11,15},{20,24},{2... | collective-permute-start | bytes 1572872 | tf_op jit(solution)/shard_map/ppermute | solution.py:202
  62.1 19.2 %collective-permute-start.13 = (bf16[256,1024]{1,0:T(8,128)(2,1)S(1)}, bf16[256,1024]{1,0:T(8,128)(2,1)S(1)}, u32[]{:S(2)}, u32[]{:S(2)}) collective-permute-start(bf16[256,1024]{1,0:T(8,128)(2,1)S(1)} %get-tuple-element.23), channel_id=1, source_target_pairs={{4,0},{6,2},{8,12},{10,14},{5,1},{7,3},{9,13},{11,15},{20,16},{22,... | collective-permute-start | bytes 1572872 | tf_op jit(solution)/shard_map/ppermute | solution.py:205
  63.7 27.4 %collective-permute-start.16 = (bf16[512,1024]{1,0:T(8,128)(2,1)S(1)}, bf16[512,1024]{1,0:T(8,128)(2,1)S(1)}, u32[]{:S(2)}, u32[]{:S(2)}) collective-permute-start(bf16[512,1024]{1,0:T(8,128)(2,1)S(1)} %pad_maximum_fusion.refs_8_), channel_id=1, source_target_pairs={{0,1},{1,0},{2,3},{3,2},{4,5},{5,4},{6,7},{7,6},{8,9},{9,8},{10,11... | collective-permute-start | bytes 3145736 | tf_op jit(solution)/shard_map/ppermute | solution.py:208
  63.8 21.0 %collective-permute-start.18 = (bf16[32,512]{1,0:T(8,128)(2,1)S(1)}, bf16[32,512]{1,0:T(8,128)(2,1)S(1)}, u32[]{:S(2)}, u32[]{:S(2)}) collective-permute-start(bf16[32,512]{1,0:T(8,128)(2,1)S(1)} %constant_dynamic-slice_fusion), channel_id=1, source_target_pairs={{0,2},{2,0},{4,6},{6,4},{8,10},{10,8},{12,14},{14,12},{1,3},{3,1},... | collective-permute-start | bytes 98312 | tf_op jit(solution)/shard_map/ppermute | solution.py:194
  81.5 21.3 %collective-permute-start.21 = (bf16[256,1024]{1,0:T(8,128)(2,1)S(1)}, bf16[256,1024]{1,0:T(8,128)(2,1)S(1)}, u32[]{:S(2)}, u32[]{:S(2)}) collective-permute-start(bf16[256,1024]{1,0:T(8,128)(2,1)S(1)} %select_select_fusion.refs_9_), channel_id=1, source_target_pairs={{0,1},{1,0},{2,3},{3,2},{4,5},{5,4},{6,7},{7,6},{8,9},{9,8},{10,11... | collective-permute-start | bytes 1572872 | tf_op jit(solution)/shard_map/ppermute | solution.py:208
  83.5 19.3 %collective-permute-start.22 = (bf16[256,1024]{1,0:T(8,128)(2,1)S(1)}, bf16[256,1024]{1,0:T(8,128)(2,1)S(1)}, u32[]{:S(2)}, u32[]{:S(2)}) collective-permute-start(bf16[256,1024]{1,0:T(8,128)(2,1)S(1)} %broadcast_select_fusion.2), channel_id=1, source_target_pairs={{4,0},{6,2},{8,12},{10,14},{5,1},{7,3},{9,13},{11,15},{20,16},{22,... | collective-permute-start | bytes 1572872 | tf_op jit(solution)/shard_map/ppermute | solution.py:205
  84.9 17.8 %collective-permute-start.19 = (bf16[2,32,512]{2,1,0:T(8,128)(2,1)S(1)}, bf16[2,32,512]{2,1,0:T(8,128)(2,1)S(1)}, u32[]{:S(2)}, u32[]{:S(2)}) collective-permute-start(bf16[2,32,512]{2,1,0:T(8,128)(2,1)S(1)} %after.5), channel_id=1, source_target_pairs={{0,0},{2,2},{4,4},{6,6},{1,8},{3,10},{5,12},{7,14},{8,1},{10,3},{1... | collective-permute-start | bytes 196616 | tf_op jit(solution)/shard_map/ppermute | solution.py:598
  89.9 12.9 %collective-permute-start.20 = (bf16[2,32,512]{2,1,0:T(8,128)(2,1)S(1)}, bf16[2,32,512]{2,1,0:T(8,128)(2,1)S(1)}, u32[]{:S(2)}, u32[]{:S(2)}) collective-permute-start(bf16[2,32,512]{2,1,0:T(8,128)(2,1)S(1)} %after.5), channel_id=1, source_target_pairs={{4,0},{6,2},{0,4},{2,6},{5,8},{7,10},{1,12},{3,14},{12,1},{14,3},{... | collective-permute-start | bytes 196616 | tf_op jit(solution)/shard_map/ppermute | solution.py:598
  110.0 10.2 %collective-permute-start.23 = (f32[32,640]{1,0:T(8,128)S(1)}, f32[32,640]{1,0:T(8,128)S(1)}, u32[]{:S(2)}, u32[]{:S(2)}) collective-permute-start(f32[32,640]{1,0:T(8,128)S(1)} %get-tuple-element.20), channel_id=1, source_target_pairs={{0,4},{2,6},{4,8},{6,10},{8,12},{10,14},{12,0},{14,2},{1,5},{3,7},... | collective-permute-start | bytes 245768 | tf_op jit(solution)/shard_map/ppermute | solution.py:662
  112.4 7.8 %collective-permute-start.24 = (f32[32,640]{1,0:T(8,128)S(1)}, f32[32,640]{1,0:T(8,128)S(1)}, u32[]{:S(2)}, u32[]{:S(2)}) collective-permute-start(f32[32,640]{1,0:T(8,128)S(1)} %get-tuple-element.21), channel_id=1, source_target_pairs={{0,8},{2,10},{4,12},{6,14},{8,0},{10,2},{12,4},{14,6},{1,9},{3,11}... | collective-permute-start | bytes 245768 | tf_op jit(solution)/shard_map/ppermute | solution.py:662
  114.4 11.4 %copy-start = (bf16[1024,2048]{1,0:T(8,128)(2,1)S(1)}, bf16[1024,2048]{1,0:T(8,128)(2,1)}, u32[]{:S(2)}) copy-start(bf16[1024,2048]{1,0:T(8,128)(2,1)} %weights.1) | copy-start | bytes 12582916
  114.4 7.5 %collective-permute-start.25 = (f32[32,640]{1,0:T(8,128)S(1)}, f32[32,640]{1,0:T(8,128)S(1)}, u32[]{:S(2)}, u32[]{:S(2)}) collective-permute-start(f32[32,640]{1,0:T(8,128)S(1)} %get-tuple-element.22), channel_id=1, source_target_pairs={{0,12},{2,14},{4,0},{6,2},{8,4},{10,6},{12,8},{14,10},{1,13},{3,15... | collective-permute-start | bytes 245768 | tf_op jit(solution)/shard_map/ppermute | solution.py:662
  122.3 6.4 %collective-permute-start.26 = (bf16[32,512]{1,0:T(8,128)(2,1)S(1)}, bf16[32,512]{1,0:T(8,128)(2,1)S(1)}, u32[]{:S(2)}, u32[]{:S(2)}) collective-permute-start(bf16[32,512]{1,0:T(8,128)(2,1)S(1)} %merge.1.ready), channel_id=1, source_target_pairs={{0,0},{1,8},{2,1},{3,9},{4,2},{5,10},{6,3},{7,11},{8,4},{9,12},{10... | collective-permute-start | bytes 98312 | tf_op jit(solution)/shard_map/ppermute | solution.py:674
  124.3 6.7 %collective-permute-start.27 = (bf16[32,512]{1,0:T(8,128)(2,1)S(1)}, bf16[32,512]{1,0:T(8,128)(2,1)S(1)}, u32[]{:S(2)}, u32[]{:S(2)}) collective-permute-start(bf16[32,512]{1,0:T(8,128)(2,1)S(1)} %merge.1.ready), channel_id=1, source_target_pairs={{0,1},{1,9},{2,0},{3,8},{4,3},{5,11},{6,2},{7,10},{8,5},{9,13},{10... | collective-permute-start | bytes 98312 | tf_op jit(solution)/shard_map/ppermute | solution.py:674
  131.8 5.0 %collective-permute-start.28 = (bf16[32,2048]{1,0:T(8,128)(2,1)S(1)}, bf16[32,2048]{1,0:T(8,128)(2,1)S(1)}, u32[]{:S(2)}, u32[]{:S(2)}) collective-permute-start(bf16[32,2048]{1,0:T(8,128)(2,1)S(1)} %output.1), channel_id=1, source_target_pairs={{0,16},{16,0},{1,17},{17,1},{2,18},{18,2},{3,19},{19,3},{4,20},{20... | collective-permute-start | bytes 393224 | tf_op jit(solution)/shard_map/ppermute | solution.py:676
